TPU v7x, 32 devices: a whole 2x2x4 slice. The times are simulated.
32 devices in a mesh: groups: 2 (over y), dp: 16 (over z, x, core).
Axes of the slice: x: 2, y: 2, z: 4, core: 2. Of those that a mesh axis runs over, the one named last changes fastest.
Arguments:
- teacher_post: bfloat16 [32, 3, 2048], P(('groups', 'dp')), parts along dimension 0, may hold values from 0 to 1, as said below
- assignment: int32 [32], P('groups'), parts along dimension 0, may hold values from 0 to 15, each once
- encoder_out: bfloat16 [32, 64, 640], P(('groups', 'dp')), parts along dimension 0, may hold values from -5 to 5
- predictor_out: bfloat16 [32, 32, 640], P(('groups', 'dp')), parts along dimension 0, may hold values from -5 to 5
- frame_lengths: int32 [32], P(('groups', 'dp')), parts along dimension 0, may hold values from 16 to 64, as said below
- token_lengths: int32 [32], P(('groups', 'dp')), parts along dimension 0, may hold values from 1 to 31, as said below
- labels: int32 [32, 31], P(('groups', 'dp')), parts along dimension 0, may hold values from 1 to 1023
- out_weight: bfloat16 [640, 1024], replicated, may hold values from -1 to 1
- out_bias: float32 [1024], replicated, may hold values from -5 to 5
Outputs:
- utt_loss: float32 [32], P(('groups', 'dp')), parts along dimension 0
- grad_weight: float32 [1280, 1024], P('groups'), parts along dimension 0
- grad_bias: float32 [2048], P('groups'), parts along dimension 0
- grad_encoder: bfloat16 [32, 64, 640], P(('groups', 'dp')), parts along dimension 0
- grad_predictor: bfloat16 [32, 32, 640], P(('groups', 'dp')), parts along dimension 0
There are 2 independent parts, one for each index of `groups`. A program takes and returns all parts, laid end to end along the dimension named above; an argument that names none is the same for every part. Nothing has to cross between parts.
Inputs may be any that keep to these rules, and one draw needn't show every extreme that they name: `frame_lengths`: one utterance of each group has exactly 64 frames. `token_lengths`: one utterance of each group has exactly 31 labels. `teacher_post`: each cell's three posteriors are positive and sum to about one.
All inputs are finite; a program needn't handle non-finite values.
Results may differ from a plain program's by a relative error of at most 0.0042.
Values may be sent and summed in bfloat16 or wider, within the bound.
No kernel may reach another device: no remote copies, remote signals or barrier semaphores. Data moves between devices by JAX's collectives and lax.ppermute only.
A program may use at most 64 MiB of HBM per device.

v0:
```python
import jax
import jax.numpy as jnp
from jax import lax
from jax.sharding import PartitionSpec as P

FB = 16


def collapse(logits, q_blank, q_label, q_rest, label_hot, weight_cell):
    vocab_ids = lax.broadcasted_iota(jnp.int32, logits.shape, 1)
    blank_hot = (vocab_ids == 0).astype(logits.dtype)
    rest_mask = (1.0 - blank_hot) * (1.0 - label_hot)
    row_max = jnp.max(logits, axis=1, keepdims=True)
    shifted = jnp.exp(logits - row_max)
    exp_total = jnp.sum(shifted, axis=1)
    rest_sum = jnp.sum(shifted * rest_mask, axis=1)
    log_norm = row_max[:, 0] + jnp.log(exp_total)
    label_logit = jnp.sum(logits * label_hot, axis=1)
    cell_loss = -(
        q_blank * (logits[:, 0] - log_norm)
        + q_label * (label_logit - log_norm)
        + q_rest * (jnp.log(rest_sum) - jnp.log(exp_total))
    )
    soft_probs = shifted / exp_total[:, None]
    q_total = q_blank + q_label + q_rest
    d_logits = weight_cell[:, None] * (
        q_total[:, None] * soft_probs
        - q_blank[:, None] * blank_hot
        - q_label[:, None] * label_hot
        - q_rest[:, None] * rest_mask * shifted / rest_sum[:, None]
    )
    return (jnp.sum(cell_loss * weight_cell), d_logits)


def on_device(
    teacher_post,
    assignment,
    encoder_out,
    predictor_out,
    frame_lengths,
    token_lengths,
    labels,
    out_weight,
    out_bias,
):
    per_dev = encoder_out.shape[0]
    frames = encoder_out.shape[1]
    tok_slots = predictor_out.shape[1]
    joint_width = out_weight.shape[0]
    vocab_size = out_weight.shape[1]
    own_index = lax.axis_index("dp")
    targets = lax.dynamic_slice_in_dim(assignment, own_index * per_dev, per_dev)
    block_piece = lax.all_gather(teacher_post, "dp", axis=0, tiled=True)
    row_ids = jnp.arange(block_piece.shape[0], dtype=jnp.int32)
    select = (targets[:, None] == row_ids[None, :]).astype(jnp.bfloat16)
    routed = jnp.einsum(
        "ur,rkc->ukc", select, block_piece, preferred_element_type=jnp.float32
    ).astype(jnp.bfloat16)
    block_rows = FB * tok_slots
    blocks = frames // FB
    row_ids = jnp.arange(block_rows, dtype=jnp.int32)
    frame_in = row_ids // tok_slots
    token_of = row_ids % tok_slots
    vocab_ids = lax.broadcasted_iota(jnp.int32, (block_rows, vocab_size), 1)

    def joint_block(slot_data, block_index):
        first_frame = block_index * FB
        enc_blk = lax.dynamic_slice_in_dim(slot_data[0], first_frame, FB, 0).astype(jnp.float32)
        return jnp.tanh(enc_blk[:, None, :] + slot_data[1][None, :, :]).reshape(
            block_rows, joint_width
        )

    def forward_block(slot_data, block_index, joint_act):
        frame_len, token_len, label_hot, label_keep, cell_count, post_slot = slot_data[2:]
        first_frame = block_index * FB
        joint_in = joint_act.astype(jnp.bfloat16)
        logits = jnp.dot(joint_in, out_weight, preferred_element_type=jnp.float32) + out_bias
        post_blk = lax.dynamic_slice_in_dim(
            post_slot, first_frame * tok_slots, block_rows, 1
        ).astype(jnp.float32)
        frame_of = first_frame + frame_in
        valid_cell = (frame_of < frame_len) & (token_of <= token_len)
        weight_cell = valid_cell.astype(jnp.float32) / cell_count
        block_loss, d_logits = collapse(
            logits, post_blk[0], post_blk[1] * label_keep, post_blk[2], label_hot, weight_cell
        )
        return (joint_in, block_loss, d_logits, d_logits.astype(jnp.bfloat16))

    def input_grads(joint_act, d_low):
        d_hidden = lax.dot_general(
            d_low, out_weight, (((1,), (1,)), ((), ())), preferred_element_type=jnp.float32
        )
        d_pre = (d_hidden * (1.0 - joint_act * joint_act)).reshape(FB, tok_slots, joint_width)
        return (jnp.sum(d_pre, axis=1), jnp.sum(d_pre, axis=0))

    frame_len = frame_lengths[0]
    token_len = token_lengths[0]
    padded_lab = jnp.concatenate([labels[0], jnp.zeros((1,), jnp.int32)])
    target = padded_lab[token_of]
    label_ok = token_of < token_len
    label_hot = ((vocab_ids == target[:, None]) & label_ok[:, None]).astype(jnp.float32)
    label_keep = label_ok.astype(jnp.float32)
    cell_count = (frame_len * (token_len + 1)).astype(jnp.float32)
    slot_list = (
        encoder_out[0],
        predictor_out[0].astype(jnp.float32),
        frame_len,
        token_len,
        label_hot,
        label_keep,
        cell_count,
        routed[0],
    )
    grad_w = jnp.zeros((joint_width, vocab_size), jnp.float32)
    grad_b = jnp.zeros((vocab_size,), jnp.float32)
    slot_data = slot_list

    def block_step(block_index, state_carry):
        grad_w, grad_b, loss_sum, enc_acc, pred_acc = state_carry
        joint_act = joint_block(slot_data, block_index)
        joint_in, block_loss, d_logits, d_low = forward_block(slot_data, block_index, joint_act)
        grad_w = grad_w + lax.dot_general(
            joint_in, d_low, (((0,), (0,)), ((), ())), preferred_element_type=jnp.float32
        )
        grad_b = grad_b + jnp.sum(d_logits, axis=0)
        enc_part, pred_part = input_grads(joint_act, d_low)
        enc_acc = lax.dynamic_update_slice_in_dim(enc_acc, enc_part, block_index * FB, 0)
        return (grad_w, grad_b, loss_sum + block_loss, enc_acc, pred_acc + pred_part)

    start_state = (
        grad_w,
        grad_b,
        jnp.zeros((), jnp.float32),
        jnp.zeros((frames, joint_width), jnp.float32),
        jnp.zeros((tok_slots, joint_width), jnp.float32),
    )
    grad_w, grad_b, loss_sum, enc_acc, pred_acc = lax.fori_loop(0, blocks, block_step, start_state)
    losses = [loss_sum]
    enc_grads = [enc_acc.astype(jnp.bfloat16)]
    pred_grads = [pred_acc.astype(jnp.bfloat16)]
    grad_weight, grad_bias = lax.psum((grad_w, grad_b), "dp")
    return (jnp.stack(losses), grad_weight, grad_bias, jnp.stack(enc_grads), jnp.stack(pred_grads))


def solution(mesh):
    in_specs = (
        P(("groups", "dp"), None, None),
        P("groups"),
        P(("groups", "dp"), None, None),
        P(("groups", "dp"), None, None),
        P(("groups", "dp")),
        P(("groups", "dp")),
        P(("groups", "dp"), None),
        P(),
        P(),
    )
    out_specs = (
        P(("groups", "dp")),
        P("groups", None),
        P("groups"),
        P(("groups", "dp"), None, None),
        P(("groups", "dp"), None, None),
    )
    return jax.shard_map(
        on_device, mesh=mesh, in_specs=in_specs, out_specs=out_specs, check_vma=False
    )
```

profile of v0, /device:TPU:0, one launch (start us, length us, event | category | flops | bytes accessed | tf_op | source)
XLA Modules:
  0.0 237.6 jit_solution(6132414459662129424)
XLA Ops:
  8.0 1.8 fusion.47
  9.8 2.1 fusion.46
  14.0 24.0 %all_gather.3 = bf16[16,3,2048]{2,1,0:T(4,128)(2,1)S(1)} all-gather(bf16[1,3,2048]{2,1,0:T(4,128)(2,1)} %param.11), channel_id=1, replica_groups=mesh['groups'=2,'dp'=16] {'dp'}, dimensions={0}, use_global_device_ids=true | all-gather | bytes 208896 | tf_op jit(solution)/shard_map/all_gather | solution.py:53
  40.3 4.5 %compare_select_fusion.2 = s32[512,1]{0,1:T(1,128)S(1)} fusion(s32[]{:T(128)} %bitcast.31, s32[]{:T(128)} %bitcast.32, s32[]{:T(128)} %bitcast.33, s32[]{:T(128)} %bitcast.34, s32[]{:T(128)} %bitcast.35, s32[]{:T(128)} %bitcast.37, s32[]{:T(128)} %bitcast.36), kind=kLoop, calls=%fused_computation.86 | loop fusion | flops 10752 | bytes 2076 | tf_op jit(solution)/shard_map/gather | solution.py:99
  44.8 14.9 %select_select_fusion = s32[512]{0:T(512)S(1)} fusion(pred[512]{0:T(512)(128)(4,1)S(1)} %compare_reduce_fusion, pred[512]{0:T(512)(128)(4,1)S(1)} %compare_reduce_fusion.1, pred[512]{0:T(512)(128)(4,1)S(1)} %compare_reduce_fusion.2, pred[512]{0:T(512)(128)(4,1)S(1)} %compare_reduce_fusion.3, pred[512]{0:T(512)(128)(4,1)S(1)} %compare_reduce_fusion.4, ...), kind=kLoop, calls=%fused_computation.95 | loop fusion | flops 12800 | bytes 16992 | tf_op jit(solution)/shard_map/gather | solution.py:99
  60.4 67.6 %while.26 = (s32[]{:T(128)}, f32[640,1024]{1,0:T(8,128)}, f32[1024]{0:T(1024)S(1)}, f32[]{:T(128)}, bf16[64,640]{1,0:T(8,128)(2,1)}, /*index=5*/f32[32,640]{1,0:...) while((s32[]{:T(128)}, f32[640,1024]{1,0:T(8,128)}, ...), condition=%wide.region_9.10_spmd.clone.clone.clone, body=%wide.region_0.9_spmd.clone.clone.clone.sunk | while | flops 2033689600 | bytes 36362768 | solution.py:137
  61.3 1.3 multiply_subtract_fusion.2
  63.8 1.6 select_reduce_fusion.2
  65.4 1.9 multiply_reduce_fusion.2
  68.0 2.0 fusion.71
  70.0 2.8 %bitcast_reduce_fusion.2 = (bf16[16,640]{1,0:T(8,128)(2,1)S(1)}, f32[512,640]{1,0:T(8,128)S(1)}) fusion(f32[512,640]{1,0:T(8,128)} %bitcast.93, bf16[640,1024]{1,0:T(8,128)(2,1)} %get-tuple-element.847, bf16[512,1024]{1,0:T(8,128)(2,1)S(1)} %get-tuple-element.783), kind=kOutput, calls=%fused_computation.53.clone.1 | convolution fusion | flops 671733760 | bytes 5001216 | tf_op jit(solution)/shard_map/while/body/eval_jaxpr/dot_general | solution.py:90
  73.6 2.4 select_add_fusion.6
  76.9 1.3 multiply_subtract_fusion.2
  79.4 1.6 select_reduce_fusion.2
  81.0 1.9 multiply_reduce_fusion.2
  83.6 2.0 fusion.71
  85.6 2.8 %bitcast_reduce_fusion.2 = (bf16[16,640]{1,0:T(8,128)(2,1)S(1)}, f32[512,640]{1,0:T(8,128)S(1)}) fusion(f32[512,640]{1,0:T(8,128)} %bitcast.93, bf16[640,1024]{1,0:T(8,128)(2,1)} %get-tuple-element.847, bf16[512,1024]{1,0:T(8,128)(2,1)S(1)} %get-tuple-element.783), kind=kOutput, calls=%fused_computation.53.clone.1 | convolution fusion | flops 671733760 | bytes 5001216 | tf_op jit(solution)/shard_map/while/body/eval_jaxpr/dot_general | solution.py:90
  89.2 4.1 %select_add_fusion.6 = f32[640,1024]{1,0:T(8,128)} fusion(f32[640,1024]{1,0:T(8,128)} %get-tuple-element.813, bf16[512,640]{1,0:T(8,128)(2,1)S(1)} %bitcast.96, pred[]{:T(512)S(6)} %compare.134, bf16[512,1024]{1,0:T(8,128)(2,1)S(1)} %get-tuple-element.783), kind=kOutput, calls=%fused_computation.4.clone.1 | convolution fusion | flops 672399360 | bytes 6946817 | tf_op jit(solution)/shard_map/while/body/eval_jaxpr/dot_general | solution.py:122
  94.2 1.3 multiply_subtract_fusion.2
  96.7 1.6 select_reduce_fusion.2
  98.3 1.9 multiply_reduce_fusion.2
  100.9 2.0 fusion.71
  102.9 2.8 %bitcast_reduce_fusion.2 = (bf16[16,640]{1,0:T(8,128)(2,1)S(1)}, f32[512,640]{1,0:T(8,128)S(1)}) fusion(f32[512,640]{1,0:T(8,128)} %bitcast.93, bf16[640,1024]{1,0:T(8,128)(2,1)} %get-tuple-element.847, bf16[512,1024]{1,0:T(8,128)(2,1)S(1)} %get-tuple-element.783), kind=kOutput, calls=%fused_computation.53.clone.1 | convolution fusion | flops 671733760 | bytes 5001216 | tf_op jit(solution)/shard_map/while/body/eval_jaxpr/dot_general | solution.py:90
  106.5 4.1 %select_add_fusion.6 = f32[640,1024]{1,0:T(8,128)} fusion(f32[640,1024]{1,0:T(8,128)} %get-tuple-element.813, bf16[512,640]{1,0:T(8,128)(2,1)S(1)} %bitcast.96, pred[]{:T(512)S(6)} %compare.134, bf16[512,1024]{1,0:T(8,128)(2,1)S(1)} %get-tuple-element.783), kind=kOutput, calls=%fused_computation.4.clone.1 | convolution fusion | flops 672399360 | bytes 6946817 | tf_op jit(solution)/shard_map/while/body/eval_jaxpr/dot_general | solution.py:122
  114.1 1.6 select_reduce_fusion.2
  115.6 1.9 multiply_reduce_fusion.2
  118.2 2.0 fusion.71
  120.3 2.8 %bitcast_reduce_fusion.2 = (bf16[16,640]{1,0:T(8,128)(2,1)S(1)}, f32[512,640]{1,0:T(8,128)S(1)}) fusion(f32[512,640]{1,0:T(8,128)} %bitcast.93, bf16[640,1024]{1,0:T(8,128)(2,1)} %get-tuple-element.847, bf16[512,1024]{1,0:T(8,128)(2,1)S(1)} %get-tuple-element.783), kind=kOutput, calls=%fused_computation.53.clone.1 | convolution fusion | flops 671733760 | bytes 5001216 | tf_op jit(solution)/shard_map/while/body/eval_jaxpr/dot_general | solution.py:90
  123.8 4.1 %select_add_fusion.6 = f32[640,1024]{1,0:T(8,128)} fusion(f32[640,1024]{1,0:T(8,128)} %get-tuple-element.813, bf16[512,640]{1,0:T(8,128)(2,1)S(1)} %bitcast.96, pred[]{:T(512)S(6)} %compare.134, bf16[512,1024]{1,0:T(8,128)(2,1)S(1)} %get-tuple-element.783), kind=kOutput, calls=%fused_computation.4.clone.1 | convolution fusion | flops 672399360 | bytes 6946817 | tf_op jit(solution)/shard_map/while/body/eval_jaxpr/dot_general | solution.py:122
  128.0 31.1 %psum.15 = f32[1024]{0:T(1024)} all-reduce(f32[1024]{0:T(1024)S(1)} %get-tuple-element.431), channel_id=1, replica_groups=mesh['groups'=2,'dp'=16] {'dp'}, use_global_device_ids=true, to_apply=%region_11.12 | all-reduce | flops 1024 | bytes 8192 | tf_op jit(solution)/shard_map/psum | solution.py:141
  159.7 66.4 %all-reduce.2.cloned.1.call-done = f32[640,1024]{1,0:T(8,128)} async-done(((f32[640,1024]{1,0:T(8,128)}), f32[640,1024]{1,0:T(8,128)}) %all-reduce.2.cloned.1.call-update) | async-done | bytes 2621456 | tf_op jit(solution)/shard_map/psum | solution.py:141
  226.1 3.6 %copy.42 = f32[640,1024]{1,0:T(8,128)} copy(f32[640,1024]{1,0:T(8,128)} %all-reduce.2.cloned.1.call-done) | data formatting | bytes 5242880
  (136 shorter events, 17.8 us)
Async XLA Ops:
  7.2 218.9 %all-reduce.2.cloned.1.call-start = ((), (), s32[]{:S(2)}) async-start(), calls=%async_computation | async-start | bytes 5242880 | tf_op jit(solution)/shard_map/psum | solution.py:141
  60.4 2.2 copy-start.2
  60.4 2.2 copy-start.6
  62.6 1.1 copy-start
  70.0 2.9 %copy-start.3 = (f32[32,640]{1,0:T(8,128)S(1)}, f32[32,640]{1,0:T(8,128)}, u32[]{:S(2)}) copy-start(f32[32,640]{1,0:T(8,128)} %get-tuple-element.817) | copy-start | bytes 245764 | tf_op jit(solution)/shard_map/while
  70.0 3.6 %copy-start.1 = (bf16[16,32,640]{2,1,0:T(8,128)(2,1)S(1)}, bf16[16,32,640]{2,1,0:T(8,128)(2,1)}, u32[]{:S(2)}) copy-start(bf16[16,32,640]{2,1,0:T(8,128)(2,1)} %copy-done) | copy-start | bytes 1966084 | tf_op jit(solution)/shard_map/while
  73.0 3.0 %copy-start.4 = (f32[32,640]{1,0:T(8,128)}, f32[32,640]{1,0:T(8,128)S(1)}, u32[]{:S(2)}) copy-start(f32[32,640]{1,0:T(8,128)S(1)} %select_add_fusion.8) | copy-start | bytes 245764 | tf_op jit(solution)/shard_map/while
  76.0 2.2 copy-start.2
  76.0 2.2 copy-start.6
  78.2 1.1 copy-start
  85.6 2.9 %copy-start.3 = (f32[32,640]{1,0:T(8,128)S(1)}, f32[32,640]{1,0:T(8,128)}, u32[]{:S(2)}) copy-start(f32[32,640]{1,0:T(8,128)} %get-tuple-element.817) | copy-start | bytes 245764 | tf_op jit(solution)/shard_map/while
  85.6 3.6 %copy-start.1 = (bf16[16,32,640]{2,1,0:T(8,128)(2,1)S(1)}, bf16[16,32,640]{2,1,0:T(8,128)(2,1)}, u32[]{:S(2)}) copy-start(bf16[16,32,640]{2,1,0:T(8,128)(2,1)} %copy-done) | copy-start | bytes 1966084 | tf_op jit(solution)/shard_map/while
  88.6 4.7 %copy-start.4 = (f32[32,640]{1,0:T(8,128)}, f32[32,640]{1,0:T(8,128)S(1)}, u32[]{:S(2)}) copy-start(f32[32,640]{1,0:T(8,128)S(1)} %select_add_fusion.8) | copy-start | bytes 245764 | tf_op jit(solution)/shard_map/while
  93.3 2.2 copy-start.2
  93.3 2.2 copy-start.6
  95.5 1.1 copy-start
  102.9 2.9 %copy-start.3 = (f32[32,640]{1,0:T(8,128)S(1)}, f32[32,640]{1,0:T(8,128)}, u32[]{:S(2)}) copy-start(f32[32,640]{1,0:T(8,128)} %get-tuple-element.817) | copy-start | bytes 245764 | tf_op jit(solution)/shard_map/while
  102.9 3.6 %copy-start.1 = (bf16[16,32,640]{2,1,0:T(8,128)(2,1)S(1)}, bf16[16,32,640]{2,1,0:T(8,128)(2,1)}, u32[]{:S(2)}) copy-start(bf16[16,32,640]{2,1,0:T(8,128)(2,1)} %copy-done) | copy-start | bytes 1966084 | tf_op jit(solution)/shard_map/while
  105.9 4.7 %copy-start.4 = (f32[32,640]{1,0:T(8,128)}, f32[32,640]{1,0:T(8,128)S(1)}, u32[]{:S(2)}) copy-start(f32[32,640]{1,0:T(8,128)S(1)} %select_add_fusion.8) | copy-start | bytes 245764 | tf_op jit(solution)/shard_map/while
  110.6 2.2 copy-start.2
  110.6 2.2 copy-start.6
  112.8 1.1 copy-start
  120.2 2.9 %copy-start.3 = (f32[32,640]{1,0:T(8,128)S(1)}, f32[32,640]{1,0:T(8,128)}, u32[]{:S(2)}) copy-start(f32[32,640]{1,0:T(8,128)} %get-tuple-element.817) | copy-start | bytes 245764 | tf_op jit(solution)/shard_map/while
  120.3 3.6 %copy-start.1 = (bf16[16,32,640]{2,1,0:T(8,128)(2,1)S(1)}, bf16[16,32,640]{2,1,0:T(8,128)(2,1)}, u32[]{:S(2)}) copy-start(bf16[16,32,640]{2,1,0:T(8,128)(2,1)} %copy-done) | copy-start | bytes 1966084 | tf_op jit(solution)/shard_map/while
  123.2 4.7 %copy-start.4 = (f32[32,640]{1,0:T(8,128)}, f32[32,640]{1,0:T(8,128)S(1)}, u32[]{:S(2)}) copy-start(f32[32,640]{1,0:T(8,128)S(1)} %select_add_fusion.8) | copy-start | bytes 245764 | tf_op jit(solution)/shard_map/while
  127.9 31.1 %copy-start.5 = (f32[32,640]{1,0:T(8,128)S(1)}, f32[32,640]{1,0:T(8,128)}, u32[]{:S(2)}) copy-start(f32[32,640]{1,0:T(8,128)} %get-tuple-element.433) | copy-start | bytes 245764
Sparse Core Ops, SparseCore 0:
  128.1 97.9 all-reduce.1
where the time goes:
time: 239 us; the launch traced here: 238 us
  waiting for transfers between devices  66.4 us (28%)
  blocking collectives  55.1 us (23%)
  other arithmetic  52.7 us (22%)
  matrix products  31.2 us (13%)
  between operations  16.6 us (7%)
  local copies, waits for them, and re-layouts  12.6 us (5%)
  loops' own time  3.03 us (1%)
    psum x1, waiting for transfers between devices, on_device(): grad_weight, grad_bias = lax.psum((grad_w, grad_b), 'dp')  66.4 us
    psum x1, blocking collectives, on_device(): grad_weight, grad_bias = lax.psum((grad_w, grad_b), 'dp')  31.1 us
    all_gather x1, blocking collectives, on_device(): block_piece = lax.all_gather(teacher_post, 'dp', axis=0, tiled=True)  24 us
    gather x27, other arithmetic, on_device(): target = padded_lab[token_of]  20.2 us
    dot_general x4, matrix products, block_step(): lax.dot_general(joint_in, d_low, (((0,), (0,)), ((), ())), preferred_elem...  14.7 us
    dot_general x4, matrix products, input_grads(): lax.dot_general(d_low, out_weight, (((1,), (1,)), ((), ())), preferred_el...  11.3 us
    reduce_sum x4, other arithmetic, block_step(): grad_b = grad_b + jnp.sum(d_logits, axis=0)  7.99 us
    reduce_sum x4, other arithmetic, collapse(): return (jnp.sum(cell_loss * weight_cell), d_logits)  7.73 us
  transfers between devices with their start and end apart: 1, of which 1 were waited for; matrix products, arithmetic and copies ran while one was open for 0% of the time, Pallas kernels for 0%

commit v1 on v0

v1 whole, which is shorter than its diff:
```python
import functools

import jax
import jax.numpy as jnp
from jax import lax
from jax.experimental import pallas as pl
from jax.experimental.pallas import tpu as pltpu
from jax.sharding import PartitionSpec as P

F32 = jnp.float32
BF16 = jnp.bfloat16
LANES = 128
EXTRA = 16
VMEM_LIMIT = 56 * 1024 * 1024


def params():
    return pltpu.CompilerParams(
        dimension_semantics=("arbitrary",), vmem_limit_bytes=VMEM_LIMIT
    )


def target_column(labels_ref, token_len, tok_slots, reps):
    tok = labels_ref.shape[1]
    row = lax.broadcasted_iota(jnp.int32, (tok_slots, tok), 0)
    lane = lax.broadcasted_iota(jnp.int32, (tok_slots, tok), 1)
    picked = jnp.where(row == lane, labels_ref[...].astype(F32), 0.0)
    column = jnp.sum(picked, axis=1, keepdims=True)
    token = lax.broadcasted_iota(jnp.int32, (tok_slots, 1), 0)
    column = jnp.where(token < token_len, column, -1.0).astype(jnp.int32)
    whole = jnp.broadcast_to(column[None], (reps, tok_slots, 1))
    return whole.reshape(reps * tok_slots, 1)


def forward_kernel(tlen_ref, labels_ref, enc_ref, pred_ref, w_ref, b_ref, e_ref, st_ref, jt_ref, enc_scr):
    step = pl.program_id(0)
    rows, vocab = e_ref.shape
    tok_slots, width = pred_ref.shape
    block_frames = rows // tok_slots

    @pl.when(step == 0)
    def _():
        enc_scr[...] = enc_ref[...].astype(F32)

    first = pl.multiple_of(step * block_frames, block_frames)
    enc = enc_scr[pl.ds(first, block_frames), :]
    pred = pred_ref[...].astype(F32)
    act = jnp.tanh(enc[:, None, :] + pred[None, :, :]).reshape(rows, width)
    joint_in = act.astype(BF16)
    jt_ref[...] = joint_in.T
    logits = jnp.dot(joint_in, w_ref[...], preferred_element_type=F32) + b_ref[...]
    row_max = jnp.max(logits, axis=1, keepdims=True)
    target = target_column(labels_ref, tlen_ref[0], tok_slots, block_frames)
    lane = lax.broadcasted_iota(jnp.int32, (rows, LANES), 1)
    rest_acc = jnp.zeros((rows, LANES), F32)
    label_acc = jnp.zeros((rows, LANES), F32)
    for j in range(vocab // LANES):
        shifted = logits[:, j * LANES : (j + 1) * LANES] - row_max
        e = jnp.exp(shifted)
        e_ref[:, j * LANES : (j + 1) * LANES] = e
        hot = lane == target - j * LANES
        rest = jnp.where(hot, 0.0, e)
        if j == 0:
            z_blank = shifted[:, 0:1]
            rest = jnp.where(lane == 0, 0.0, rest)
        rest_acc = rest_acc + rest
        label_acc = label_acc + jnp.where(hot, shifted, 0.0)
    rest_sum = jnp.sum(rest_acc, axis=1, keepdims=True)
    z_label = jnp.sum(label_acc, axis=1, keepdims=True)
    e_label = jnp.where(target >= 0, jnp.exp(z_label), 0.0)
    total = rest_sum + jnp.exp(z_blank) + e_label
    st_ref[...] = jnp.concatenate([total, rest_sum, z_blank, z_label], axis=1)


def grad_kernel(
    pick_ref, flen_ref, tlen_ref, labels_ref, qa_ref, qb_ref, e_ref, st_ref, jt_ref,
    d_ref, loss_ref, send_ref, keep_ref, keepb_ref, d_scr, gb_scr, loss_scr,
):
    step = pl.program_id(0)
    steps = pl.num_programs(0)
    rows, vocab = e_ref.shape
    tok_slots = labels_ref.shape[1] + 1
    block_frames = rows // tok_slots
    width = jt_ref.shape[0]

    @pl.when(step == 0)
    def _():
        gb_scr[...] = jnp.zeros_like(gb_scr)
        loss_scr[...] = jnp.zeros_like(loss_scr)

    half_count = pick_ref[1]
    chosen = jnp.where(pick_ref[0] < half_count, qa_ref[0].astype(F32), qb_ref[0].astype(F32))
    padded = jnp.concatenate([chosen, jnp.zeros((5, rows), F32)], axis=0)
    q = padded.T
    frame_len, token_len = flen_ref[0], tlen_ref[0]
    row = lax.broadcasted_iota(jnp.int32, (block_frames, tok_slots, 1), 0).reshape(rows, 1)
    frame = row + step * block_frames
    token = lax.broadcasted_iota(jnp.int32, (block_frames, tok_slots, 1), 1).reshape(rows, 1)
    count = (frame_len * (token_len + 1)).astype(F32)
    weight = jnp.where((frame < frame_len) & (token <= token_len), 1.0 / count, 0.0)
    q_blank = q[:, 0:1]
    q_label = jnp.where(token < token_len, q[:, 1:2], 0.0)
    q_rest = q[:, 2:3]
    total = st_ref[:, 0:1]
    rest_sum = st_ref[:, 1:2]
    z_blank = st_ref[:, 2:3]
    z_label = st_ref[:, 3:4]
    log_total = jnp.log(total)
    cell_loss = -(
        q_blank * (z_blank - log_total)
        + q_label * (z_label - log_total)
        + q_rest * (jnp.log(rest_sum) - log_total)
    )
    loss_scr[...] += jnp.sum((cell_loss * weight).reshape(rows // 8, 8, 1), axis=0)
    soft = weight * (q_blank + q_label + q_rest) / total
    scale = soft - weight * q_rest / rest_sum
    d_blank = soft * jnp.exp(z_blank) - weight * q_blank
    d_label = soft * jnp.exp(z_label) - weight * q_label
    target = target_column(labels_ref, token_len, tok_slots, block_frames)
    lane = lax.broadcasted_iota(jnp.int32, (rows, LANES), 1)
    base = pl.multiple_of(step * rows, rows)
    for j in range(vocab // LANES):
        cols = slice(j * LANES, (j + 1) * LANES)
        d = jnp.where(lane == target - j * LANES, d_label, e_ref[:, cols] * scale)
        if j == 0:
            d = jnp.where(lane == 0, d_blank, d)
        low = d.astype(BF16)
        d_ref[:, cols] = low
        d_scr[pl.ds(base, rows), cols] = low
        gb_scr[:, cols] += jnp.sum(d.reshape(rows // 8, 8, LANES), axis=0)

    @pl.when(step == steps - 1)
    def _():
        loss_ref[...] = jnp.broadcast_to(jnp.sum(loss_scr[...], axis=0, keepdims=True), loss_ref.shape)
        part = vocab // 2
        tile = part // 2
        core = pick_ref[2]
        for j in range(2):
            col = pl.multiple_of((1 - core) * part + j * tile, tile)
            dw = jnp.dot(jt_ref[...], d_scr[:, pl.ds(col, tile)], preferred_element_type=F32)
            send_ref[:width, j * tile : (j + 1) * tile] = dw.astype(BF16)
        for j in range(2):
            col = pl.multiple_of(core * part + j * tile, tile)
            dw = jnp.dot(jt_ref[...], d_scr[:, pl.ds(col, tile)], preferred_element_type=F32)
            keep_ref[:, j * tile : (j + 1) * tile] = dw
        bias = jnp.sum(gb_scr[...], axis=0, keepdims=True)
        first, second = bias[:, :part], bias[:, part:]
        mine = jnp.where(core == 0, first, second)
        other = jnp.where(core == 0, second, first)
        keepb_ref[...] = mine
        high = other.astype(BF16)
        low = (other - high.astype(F32)).astype(BF16)
        place = lax.broadcasted_iota(jnp.int32, (EXTRA, part), 0)
        packed = jnp.where(place == 0, high.astype(F32), jnp.where(place == 1, low.astype(F32), 0.0))
        send_ref[width:, :] = packed.astype(BF16)


def input_kernel(enc_ref, pred_ref, d_ref, w_ref, ge_ref, gp_ref, enc_scr, ge_scr, gp_scr):
    step = pl.program_id(0)
    steps = pl.num_programs(0)
    rows = d_ref.shape[0]
    tok_slots, width = pred_ref.shape
    block_frames = rows // tok_slots

    @pl.when(step == 0)
    def _():
        enc_scr[...] = enc_ref[...].astype(F32)
        gp_scr[...] = jnp.zeros_like(gp_scr)

    first = pl.multiple_of(step * block_frames, block_frames)
    d_hidden = lax.dot_general(
        d_ref[...], w_ref[...], (((1,), (1,)), ((), ())), preferred_element_type=F32
    )
    enc = enc_scr[pl.ds(first, block_frames), :]
    act = jnp.tanh(enc[:, None, :] + pred_ref[...].astype(F32)[None, :, :])
    d_pre = d_hidden.reshape(block_frames, tok_slots, width) * (1.0 - act * act)
    ge_scr[pl.ds(first, block_frames), :] = jnp.sum(d_pre, axis=1)
    gp_scr[...] += jnp.sum(d_pre, axis=0)

    @pl.when(step == steps - 1)
    def _():
        ge_ref[...] = ge_scr[...].astype(BF16)
        gp_ref[...] = gp_scr[...].astype(BF16)


def whole(shape):
    return pl.BlockSpec(shape, lambda *_: (0,) * len(shape))


SMEM_SPEC = pl.BlockSpec(memory_space=pltpu.SMEM)


def forward(tlen, labels, enc, pred, w, bias, rows):
    frames, width = enc.shape
    tok_slots = pred.shape[0]
    vocab = w.shape[1]
    cells = frames * tok_slots
    return pl.pallas_call(
        forward_kernel,
        grid=(cells // rows,),
        in_specs=[
            SMEM_SPEC, whole(labels.shape), whole(enc.shape), whole(pred.shape),
            whole(w.shape), whole(bias.shape),
        ],
        out_specs=[
            pl.BlockSpec((rows, vocab), lambda i: (i, 0)),
            pl.BlockSpec((rows, 4), lambda i: (i, 0)),
            pl.BlockSpec((width, rows), lambda i: (0, i)),
        ],
        out_shape=[
            jax.ShapeDtypeStruct((cells, vocab), F32),
            jax.ShapeDtypeStruct((cells, 4), F32),
            jax.ShapeDtypeStruct((width, cells), BF16),
        ],
        scratch_shapes=[pltpu.VMEM((frames, width), F32)],
        compiler_params=params(),
        cost_estimate=pl.CostEstimate(
            flops=2 * cells * width * vocab, bytes_accessed=16 * 1024 * 1024,
            transcendentals=cells * (width + vocab),
        ),
    )(tlen, labels, enc, pred, w, bias)


def gradients(pick, flen, tlen, labels, qa, qb, e, st, jt, rows):
    cells, vocab = e.shape
    width = jt.shape[0]
    part = vocab // 2
    smem = pl.BlockSpec(memory_space=pltpu.SMEM)
    grid_spec = pltpu.PrefetchScalarGridSpec(
        num_scalar_prefetch=1,
        grid=(cells // rows,),
        in_specs=[
            smem, smem, whole(labels.shape),
            pl.BlockSpec((1, 3, rows), lambda i, pick: (lax.rem(pick[0], pick[1]), 0, i)),
            pl.BlockSpec((1, 3, rows), lambda i, pick: (lax.rem(pick[0], pick[1]), 0, i)),
            pl.BlockSpec((rows, vocab), lambda i, pick: (i, 0)),
            pl.BlockSpec((rows, 4), lambda i, pick: (i, 0)),
            whole(jt.shape),
        ],
        out_specs=[
            pl.BlockSpec((rows, vocab), lambda i, pick: (i, 0)),
            whole((8, LANES)),
            whole((width + EXTRA, part)),
            whole((width, part)),
            whole((1, part)),
        ],
        scratch_shapes=[
            pltpu.VMEM((cells, vocab), BF16),
            pltpu.VMEM((8, vocab), F32),
            pltpu.VMEM((8, 1), F32),
        ],
    )
    return pl.pallas_call(
        grad_kernel,
        grid_spec=grid_spec,
        out_shape=[
            jax.ShapeDtypeStruct((cells, vocab), BF16),
            jax.ShapeDtypeStruct((8, LANES), F32),
            jax.ShapeDtypeStruct((width + EXTRA, part), BF16),
            jax.ShapeDtypeStruct((width, part), F32),
            jax.ShapeDtypeStruct((1, part), F32),
        ],
        compiler_params=params(),
        cost_estimate=pl.CostEstimate(
            flops=2 * cells * width * vocab, bytes_accessed=16 * 1024 * 1024, transcendentals=cells * 8
        ),
    )(pick, flen, tlen, labels, qa, qb, e, st, jt)


def input_gradients(enc, pred, d_low, w, rows):
    cells, vocab = d_low.shape
    return pl.pallas_call(
        input_kernel,
        grid=(cells // rows,),
        in_specs=[
            whole(enc.shape), whole(pred.shape),
            pl.BlockSpec((rows, vocab), lambda i: (i, 0)), whole(w.shape),
        ],
        out_specs=[whole(enc.shape), whole(pred.shape)],
        out_shape=[
            jax.ShapeDtypeStruct(enc.shape, BF16),
            jax.ShapeDtypeStruct(pred.shape, BF16),
        ],
        scratch_shapes=[
            pltpu.VMEM(enc.shape, F32), pltpu.VMEM(enc.shape, F32), pltpu.VMEM(pred.shape, F32)
        ],
        compiler_params=params(),
        cost_estimate=pl.CostEstimate(
            flops=2 * cells * w.shape[0] * vocab, bytes_accessed=6 * 1024 * 1024,
            transcendentals=cells * w.shape[0],
        ),
    )(enc, pred, d_low, w)


def split_two(value):
    high = lax.reduce_precision(value, 8, 7)
    return high, lax.reduce_precision(value - high, 8, 7)


def on_device(
    dp, teacher_post, assignment, encoder_out, predictor_out, frame_lengths, token_lengths,
    labels, out_weight, out_bias,
):
    own = lax.axis_index("dp")
    core = own & 1
    masks = [1 << k for k in range(dp.bit_length() - 1)]
    enc, pred = encoder_out[0], predictor_out[0]
    rows = 8 * pred.shape[0]
    width, vocab = out_weight.shape
    part = vocab // 2

    def exchange(value, even, odd):
        pairs = [(k, k ^ (odd if k & 1 else even)) for k in range(dp)]
        return lax.ppermute(value, "dp", pairs)

    held = teacher_post
    for mask in masks[:-1]:
        held = jnp.concatenate([held, exchange(held, mask, mask)], axis=0)
    far = exchange(held, masks[-1], masks[-1])
    place = lax.dynamic_index_in_dim(assignment, own, keepdims=False) ^ own
    pick = jnp.stack([place, jnp.int32(dp // 2), core]).astype(jnp.int32)

    e, st, jt = forward(
        token_lengths, labels, enc, pred, out_weight, out_bias.reshape(1, vocab), rows
    )
    d_low, loss, send, keep, bias = gradients(
        pick, frame_lengths, token_lengths, labels, held, far, e, st, jt, rows
    )
    got = exchange(send, 1, 1)
    grad_enc, grad_pred = input_gradients(enc, pred, d_low, out_weight, rows)

    def got_bias(rows_of):
        return rows_of[0:1].astype(F32) + rows_of[1:2].astype(F32)

    def bias_rows(high, low):
        filler = jnp.zeros((EXTRA - 2, part), BF16)
        return jnp.concatenate([high.astype(BF16), low.astype(BF16), filler], axis=0)

    acc = keep + got[:width].astype(F32)
    bias = bias + got_bias(got[width:])
    rest = masks[1:]
    even_order = rest[:1] + rest[1:][::-1]
    odd_order = rest[1:2] + rest[:1] + rest[2:]
    sides = []
    count = width
    for even, odd in zip(even_order, odd_order):
        side = (own & jnp.where(core == 0, even, odd)) != 0
        sides.append(side)
        count //= 2
        top, bottom = acc[:count], acc[count:]
        high, low = split_two(bias)
        send = jnp.where(side, top, bottom).astype(BF16)
        got = exchange(jnp.concatenate([send, bias_rows(high, low)], axis=0), even, odd)
        acc = jnp.where(side, bottom, top) + got[:count].astype(F32)
        bias = (high + low) + got_bias(got[count:])
    have = acc.astype(BF16)
    for even, odd, side in list(zip(even_order, odd_order, sides))[::-1]:
        got = exchange(have, even, odd)
        have = jnp.where(
            side, jnp.concatenate([got, have], axis=0), jnp.concatenate([have, got], axis=0)
        )
    high, low = split_two(bias)
    got = exchange(jnp.concatenate([have, bias_rows(high, low)], axis=0), 1, 1)
    other = got[:width]
    grad_weight = jnp.where(
        core == 0, jnp.concatenate([have, other], axis=1), jnp.concatenate([other, have], axis=1)
    ).astype(F32)
    bias, other_bias = high + low, got_bias(got[width:])
    grad_bias = jnp.where(
        core == 0,
        jnp.concatenate([bias, other_bias], axis=1),
        jnp.concatenate([other_bias, bias], axis=1),
    ).reshape(vocab)
    return (loss[0, 0:1], grad_weight, grad_bias, grad_enc[None], grad_pred[None])


def solution(mesh):
    in_specs = (
        P(("groups", "dp"), None, None),
        P("groups"),
        P(("groups", "dp"), None, None),
        P(("groups", "dp"), None, None),
        P(("groups", "dp")),
        P(("groups", "dp")),
        P(("groups", "dp"), None),
        P(),
        P(),
    )
    out_specs = (
        P(("groups", "dp")),
        P("groups", None),
        P("groups"),
        P(("groups", "dp"), None, None),
        P(("groups", "dp"), None, None),
    )
    return jax.shard_map(
        functools.partial(on_device, mesh.shape["dp"]),
        mesh=mesh, in_specs=in_specs, out_specs=out_specs, check_vma=False,
    )
```

time: 239 us -> 112 us (0.47)
  blocking collectives: 55.1 us -> 0 us
  other arithmetic: 52.7 us -> 6.26 us
  Pallas kernels: 0 us -> 37.6 us
  matrix products: 31.2 us -> 0 us
  waiting for transfers between devices: 66.4 us -> 49.4 us
  between operations: 16.6 us -> 2.84 us
  starting transfers between devices: 0.04 us -> 12.4 us
  local copies, waits for them, and re-layouts: 12.6 us -> 2.57 us
  loops' own time: 3.03 us -> 0 us
    psum x1 -> x0, waiting for transfers between devices: 66.4 us -> none  [on_device(): grad_weight, grad_bias = lax.psum((grad_w, grad_b), 'dp')]
    ppermute x0 -> x12, waiting for transfers between devices: none -> 49.4 us  [exchange(): return lax.ppermute(value, 'dp', pairs)]
    pallas_call x0 -> x3, Pallas kernels: none -> 37.6 us  [the longest x1 17.3 us: gradients(): pl.pallas_call(grad_kernel, grid_spec=grid_spec, out_shape=[jax.ShapeDtyp...]
    dot_general x13 -> x0, matrix products: 31.2 us -> none  [the longest x4 14.7 us: block_step(): lax.dot_general(joint_in, d_low, (((0,), (0,)), ((), ())), preferred_elem...]
    psum x1 -> x0, blocking collectives: 31.1 us -> none  [on_device(): grad_weight, grad_bias = lax.psum((grad_w, grad_b), 'dp')]
    all_gather x1 -> x0, blocking collectives: 24 us -> none  [on_device(): block_piece = lax.all_gather(teacher_post, 'dp', axis=0, tiled=True)]
    reduce_sum x16 -> x0, other arithmetic: 22.3 us -> none  [the longest x4 7.99 us: block_step(): grad_b = grad_b + jnp.sum(d_logits, axis=0)]
    gather x27 -> x0, other arithmetic: 20.2 us -> none  [on_device(): target = padded_lab[token_of]]
  transfers between devices with their start and end apart: 1 -> 12, of which waited for: 1 -> 10; matrix products, arithmetic and copies ran while one was open for 0% -> 2% of each run, Pallas kernels for 0% -> 18%
where the time goes in v1:
time: 112 us; the launch traced here: 111 us
  waiting for transfers between devices  49.4 us (44%)
  Pallas kernels  37.6 us (34%)
  starting transfers between devices  12.4 us (11%)
  other arithmetic  6.26 us (6%)
  between operations  2.84 us (3%)
  local copies, waits for them, and re-layouts  2.57 us (2%)
    ppermute x12, waiting for transfers between devices, exchange(): return lax.ppermute(value, 'dp', pairs)  49.4 us
    pallas_call x1, Pallas kernels, gradients(): pl.pallas_call(grad_kernel, grid_spec=grid_spec, out_shape=[jax.ShapeDtyp...  17.3 us
    ppermute x12, starting transfers between devices, exchange(): return lax.ppermute(value, 'dp', pairs)  12.4 us
    pallas_call x1, Pallas kernels, forward(): pl.pallas_call(forward_kernel, grid=(cells // rows,), in_specs=[SMEM_SPEC...  11.6 us
    pallas_call x1, Pallas kernels, input_gradients(): pl.pallas_call(input_kernel, grid=(cells // rows,), in_specs=[whole(enc.s...  8.68 us
  transfers between devices with their start and end apart: 12, of which 10 were waited for; matrix products, arithmetic and copies ran while one was open for 2% of the time, Pallas kernels for 18%

profile of v1, /device:TPU:0, one launch (start us, length us, event | category | flops | bytes accessed | tf_op | source)
XLA Modules:
  0.0 111.1 jit_solution(6461268668664699404)
XLA Ops:
  0.6 0.5 collective-permute-start
  1.8 11.6 %shard_map.128 = (f32[2048,1024]{1,0:T(8,128)}, f32[2048,4]{1,0:T(8,128)}, bf16[640,2048]{1,0:T(8,128)(2,1)}) custom-call(s32[1]{0:T(128)S(6)} %copy.18.tlen_ref, s32[1,31]{1,0:T(1,128)} %labels_ref.3, bf16[64,640]{1,0:T(8,128)(2,1)} %bitcast.13, bf16[32,640]{1,0:T(8,128)(2,1)} %bitcast.15, bf16[640,1024]{1,0:T(8,128)(2,1)} %w_ref.3, f32[1,1024]{1,0:T(1,128)} %bitcast.17), custom_call_target="tpu_custom_call" | custom-call | flops 2684354560 | bytes 16777216 | tf_op jit(solution)/shard_map/pallas_call | solution.py:198
  13.4 0.6 dynamic_slice.4
  15.4 2.6 %collective-permute-start.1 = (bf16[2,3,2048]{2,1,0:T(4,128)(2,1)S(1)}, bf16[2,3,2048]{2,1,0:T(4,128)(2,1)S(1)}, u32[]{:S(2)}, u32[]{:S(2)}) collective-permute-start(bf16[2,3,2048]{2,1,0:T(4,128)(2,1)S(1)} %pad_maximum_fusion.5), channel_id=1, source_target_pairs={{0,2},{1,3},{2,0},{3,1},{4,6},{5,7},{6,4},{7,5},{8,10},{9,11},{10,... | collective-permute-start | bytes 73736 | tf_op jit(solution)/shard_map/ppermute | solution.py:314
  18.0 2.0 %collective-permute-done.1 = bf16[2,3,2048]{2,1,0:T(4,128)(2,1)S(1)} collective-permute-done((bf16[2,3,2048]{2,1,0:T(4,128)(2,1)S(1)}, bf16[2,3,2048]{2,1,0:T(4,128)(2,1)S(1)}, u32[]{:S(2)}, u32[]{:S(2)}) %collective-permute-start.1) | collective-permute-done | bytes 24608 | tf_op jit(solution)/shard_map/ppermute | solution.py:314
  20.0 2.0 %collective-permute-start.2 = (bf16[4,3,2048]{2,1,0:T(4,128)(2,1)S(1)}, bf16[4,3,2048]{2,1,0:T(4,128)(2,1)S(1)}, u32[]{:S(2)}, u32[]{:S(2)}) collective-permute-start(bf16[4,3,2048]{2,1,0:T(4,128)(2,1)S(1)} %pad_maximum_fusion.4), channel_id=1, source_target_pairs={{0,4},{1,5},{2,6},{3,7},{4,0},{5,1},{6,2},{7,3},{8,12},{9,13},{10,... | collective-permute-start | bytes 147464 | tf_op jit(solution)/shard_map/ppermute | solution.py:314
  22.1 2.3 %collective-permute-done.2 = bf16[4,3,2048]{2,1,0:T(4,128)(2,1)S(1)} collective-permute-done((bf16[4,3,2048]{2,1,0:T(4,128)(2,1)S(1)}, bf16[4,3,2048]{2,1,0:T(4,128)(2,1)S(1)}, u32[]{:S(2)}, u32[]{:S(2)}) %collective-permute-start.2) | collective-permute-done | bytes 49184 | tf_op jit(solution)/shard_map/ppermute | solution.py:314
  24.4 3.0 %collective-permute-start.3 = (bf16[8,3,2048]{2,1,0:T(4,128)(2,1)S(1)}, bf16[8,3,2048]{2,1,0:T(4,128)(2,1)S(1)}, u32[]{:S(2)}, u32[]{:S(2)}) collective-permute-start(bf16[8,3,2048]{2,1,0:T(4,128)(2,1)S(1)} %constant_dynamic-update-slice_fusion.qa_ref), channel_id=1, source_target_pairs={{0,8},{1,9},{2,10},{3,11},{4,12},{5,13},{6,14},{7,15},{8,0},{9,1},... | collective-permute-start | bytes 294920 | tf_op jit(solution)/shard_map/ppermute | solution.py:314
  27.4 0.6 pad_add_fusion.pick_ref
  28.0 4.3 %collective-permute-done.3.qb_ref = bf16[8,3,2048]{2,1,0:T(4,128)(2,1)S(1)} collective-permute-done((bf16[8,3,2048]{2,1,0:T(4,128)(2,1)S(1)}, bf16[8,3,2048]{2,1,0:T(4,128)(2,1)S(1)}, u32[]{:S(2)}, u32[]{:S(2)}) %collective-permute-start.3) | collective-permute-done | bytes 98336 | tf_op jit(solution)/shard_map/ppermute | solution.py:314
  32.3 0.6 copy-done.2
  33.0 17.3 %shard_map.129 = (bf16[2048,1024]{1,0:T(8,128)(2,1)}, f32[8,128]{1,0:T(8,128)}, bf16[656,512]{1,0:T(8,128)(2,1)}, f32[640,512]{1,0:T(8,128)}, f32[1,512]{1,0:T(1,128)}) custom-call(s32[3]{0:T(128)} %pad_add_fusion.pick_ref, s32[1]{0:T(128)S(6)} %copy.17.flen_ref, s32[1]{0:T(128)S(6)} %copy.18.tlen_ref, s32[1,31]{1,0:T(1,128)} %labels_ref.3, ...), custom_call_target="tpu_custom_call" | custom-call | flops 2684354560 | bytes 16777216 | tf_op jit(solution)/shard_map/pallas_call | solution.py:253
  50.4 2.3 %collective-permute-done.4 = bf16[656,512]{1,0:T(8,128)(2,1)S(1)} collective-permute-done((bf16[656,512]{1,0:T(8,128)(2,1)}, bf16[656,512]{1,0:T(8,128)(2,1)S(1)}, u32[]{:S(2)}, u32[]{:S(2)}) %collective-permute-start.4) | collective-permute-done | bytes 671776 | tf_op jit(solution)/shard_map/ppermute | solution.py:314
  52.7 0.7 reduce-precision_convert_fusion.3
  53.4 1.5 %convert_add_fusion = f32[640,512]{1,0:T(8,128)S(1)} fusion(f32[640,512]{1,0:T(8,128)} %get-tuple-element.19, bf16[656,512]{1,0:T(8,128)(2,1)S(1)} %collective-permute-done.4), kind=kLoop, calls=%fused_computation.2 | loop fusion | flops 655360 | bytes 3276800 | tf_op jit(solution)/shard_map/add | solution.py:339
  55.1 1.4 %collective-permute-start.5 = (bf16[336,512]{1,0:T(8,128)(2,1)S(1)}, bf16[336,512]{1,0:T(8,128)(2,1)S(1)}, u32[]{:S(2)}, u32[]{:S(2)}) collective-permute-start(bf16[336,512]{1,0:T(8,128)(2,1)S(1)} %pad_maximum_fusion.1), channel_id=1, source_target_pairs={{0,2},{1,5},{2,0},{3,7},{4,6},{5,1},{6,4},{7,3},{8,10},{9,13},{10,... | collective-permute-start | bytes 1032200 | tf_op jit(solution)/shard_map/ppermute | solution.py:314
  56.4 5.9 %collective-permute-done.5 = bf16[336,512]{1,0:T(8,128)(2,1)S(1)} collective-permute-done((bf16[336,512]{1,0:T(8,128)(2,1)S(1)}, bf16[336,512]{1,0:T(8,128)(2,1)S(1)}, u32[]{:S(2)}, u32[]{:S(2)}) %collective-permute-start.5) | collective-permute-done | bytes 344096 | tf_op jit(solution)/shard_map/ppermute | solution.py:314
  62.4 0.2 convert_add_fusion.1
  62.6 1.1 %collective-permute-start.6 = (bf16[176,512]{1,0:T(8,128)(2,1)S(1)}, bf16[176,512]{1,0:T(8,128)(2,1)S(1)}, u32[]{:S(2)}, u32[]{:S(2)}) collective-permute-start(bf16[176,512]{1,0:T(8,128)(2,1)S(1)} %pad_maximum_fusion.2), channel_id=1, source_target_pairs={{0,8},{1,3},{2,10},{3,1},{4,12},{5,7},{6,14},{7,5},{8,0},{9,11},{1... | collective-permute-start | bytes 540680 | tf_op jit(solution)/shard_map/ppermute | solution.py:314
  63.8 9.2 %collective-permute-done.6 = bf16[176,512]{1,0:T(8,128)(2,1)S(1)} collective-permute-done((bf16[176,512]{1,0:T(8,128)(2,1)S(1)}, bf16[176,512]{1,0:T(8,128)(2,1)S(1)}, u32[]{:S(2)}, u32[]{:S(2)}) %collective-permute-start.6) | collective-permute-done | bytes 180256 | tf_op jit(solution)/shard_map/ppermute | solution.py:314
  73.1 0.1 collective-permute-start.7
  73.2 5.4 %collective-permute-done.7 = bf16[96,512]{1,0:T(8,128)(2,1)S(1)} collective-permute-done((bf16[96,512]{1,0:T(8,128)(2,1)S(1)}, bf16[96,512]{1,0:T(8,128)(2,1)S(1)}, u32[]{:S(2)}, u32[]{:S(2)}) %collective-permute-start.7) | collective-permute-done | bytes 98336 | tf_op jit(solution)/shard_map/ppermute | solution.py:314
  78.8 4.4 %collective-permute-done.8 = bf16[80,512]{1,0:T(8,128)(2,1)S(1)} collective-permute-done((bf16[80,512]{1,0:T(8,128)(2,1)S(1)}, bf16[80,512]{1,0:T(8,128)(2,1)S(1)}, u32[]{:S(2)}, u32[]{:S(2)}) %collective-permute-start.8) | collective-permute-done | bytes 81952 | tf_op jit(solution)/shard_map/ppermute | solution.py:314
  83.3 7.7 %collective-permute-done.9 = bf16[160,512]{1,0:T(8,128)(2,1)S(1)} collective-permute-done((bf16[160,512]{1,0:T(8,128)(2,1)S(1)}, bf16[160,512]{1,0:T(8,128)(2,1)S(1)}, u32[]{:S(2)}, u32[]{:S(2)}) %collective-permute-start.9) | collective-permute-done | bytes 163872 | tf_op jit(solution)/shard_map/ppermute | solution.py:314
  91.0 0.1 maximum_select_fusion.2
  91.1 1.4 %collective-permute-start.10 = (bf16[320,512]{1,0:T(8,128)(2,1)S(1)}, bf16[320,512]{1,0:T(8,128)(2,1)S(1)}, u32[]{:S(2)}, u32[]{:S(2)}) collective-permute-start(bf16[320,512]{1,0:T(8,128)(2,1)S(1)} %maximum_select_fusion.2), channel_id=1, source_target_pairs={{0,2},{1,5},{2,0},{3,7},{4,6},{5,1},{6,4},{7,3},{8,10},{9,13},{10,... | collective-permute-start | bytes 983048 | tf_op jit(solution)/shard_map/ppermute | solution.py:314
  92.5 5.7 %collective-permute-done.10 = bf16[320,512]{1,0:T(8,128)(2,1)S(1)} collective-permute-done((bf16[320,512]{1,0:T(8,128)(2,1)S(1)}, bf16[320,512]{1,0:T(8,128)(2,1)S(1)}, u32[]{:S(2)}, u32[]{:S(2)}) %collective-permute-start.10) | collective-permute-done | bytes 327712 | tf_op jit(solution)/shard_map/ppermute | solution.py:314
  98.3 0.3 maximum_select_fusion.1
  98.7 1.2 %slice.81 = f32[1,1]{1,0:T(1,128)} slice(f32[8,128]{1,0:T(8,128)} %get-tuple-element.18), slice={[0:1], [0:1]} | slice | bytes 8 | tf_op jit(solution)/shard_map/slice | solution.py:374
  99.9 8.7 %shard_map.130 = (bf16[64,640]{1,0:T(8,128)(2,1)}, bf16[32,640]{1,0:T(8,128)(2,1)}) custom-call(bf16[64,640]{1,0:T(8,128)(2,1)} %bitcast.14, bf16[32,640]{1,0:T(8,128)(2,1)} %bitcast.16, bf16[2048,1024]{1,0:T(8,128)(2,1)} %get-tuple-element.22.d_ref, bf16[640,1024]{1,0:T(8,128)(2,1)} %w_ref.3), custom_call_target="tpu_custom_call" | custom-call | flops 2684354560 | bytes 6291456 | tf_op jit(solution)/shard_map/pallas_call | solution.py:272
  108.6 1.9 %fusion = f32[640,1024]{1,0:T(8,128)} fusion(bf16[640,512]{1,0:T(8,128)(2,1)S(1)} %slice.121, bf16[640,512]{1,0:T(8,128)(2,1)S(1)} %maximum_select_fusion.1, pred[]{:T(512)S(6)} %eq.2), kind=kLoop, calls=%fused_computation.1 | loop fusion | flops 6553600 | bytes 3932161 | tf_op jit(solution)/shard_map/convert_element_type | solution.py:367
  110.5 0.6 maximum_select_fusion.4
  (39 shorter events, 0.9 us)
Async XLA Ops:
  0.6 14.7 %collective-permute-start = (bf16[1,3,2048]{2,1,0:T(4,128)(2,1)}, bf16[1,3,2048]{2,1,0:T(4,128)(2,1)S(1)}, u32[]{:S(2)}, u32[]{:S(2)}) collective-permute-start(bf16[1,3,2048]{2,1,0:T(4,128)(2,1)} %param.9), channel_id=1, source_target_pairs={{0,1},{1,0},{2,3},{3,2},{4,5},{5,4},{6,7},{7,6},{8,9},{9,8},{10,11... | collective-permute-start | bytes 36872 | tf_op jit(solution)/shard_map/ppermute | solution.py:314
  1.8 11.6 %copy-start.1 = (bf16[1,3,2048]{2,1,0:T(4,128)(2,1)S(1)}, bf16[1,3,2048]{2,1,0:T(4,128)(2,1)}, u32[]{:S(2)}) copy-start(bf16[1,3,2048]{2,1,0:T(4,128)(2,1)} %param.9) | copy-start | bytes 36868
  1.8 11.6 %copy-start.3 = (s32[16]{0:T(128)S(1)}, s32[16]{0:T(128)}, u32[]{:S(2)}) copy-start(s32[16]{0:T(128)} %param.10) | copy-start | bytes 196
  15.4 4.6 %collective-permute-start.1 = (bf16[2,3,2048]{2,1,0:T(4,128)(2,1)S(1)}, bf16[2,3,2048]{2,1,0:T(4,128)(2,1)S(1)}, u32[]{:S(2)}, u32[]{:S(2)}) collective-permute-start(bf16[2,3,2048]{2,1,0:T(4,128)(2,1)S(1)} %pad_maximum_fusion.5), channel_id=1, source_target_pairs={{0,2},{1,3},{2,0},{3,1},{4,6},{5,7},{6,4},{7,5},{8,10},{9,11},{10,... | collective-permute-start | bytes 73736 | tf_op jit(solution)/shard_map/ppermute | solution.py:314
  20.0 4.3 %collective-permute-start.2 = (bf16[4,3,2048]{2,1,0:T(4,128)(2,1)S(1)}, bf16[4,3,2048]{2,1,0:T(4,128)(2,1)S(1)}, u32[]{:S(2)}, u32[]{:S(2)}) collective-permute-start(bf16[4,3,2048]{2,1,0:T(4,128)(2,1)S(1)} %pad_maximum_fusion.4), channel_id=1, source_target_pairs={{0,4},{1,5},{2,6},{3,7},{4,0},{5,1},{6,2},{7,3},{8,12},{9,13},{10,... | collective-permute-start | bytes 147464 | tf_op jit(solution)/shard_map/ppermute | solution.py:314
  24.4 7.9 %copy-start = (bf16[8,3,2048]{2,1,0:T(4,128)(2,1)}, bf16[8,3,2048]{2,1,0:T(4,128)(2,1)S(1)}, u32[]{:S(2)}) copy-start(bf16[8,3,2048]{2,1,0:T(4,128)(2,1)S(1)} %constant_dynamic-update-slice_fusion.qa_ref) | copy-start | bytes 294916
  24.4 7.9 %collective-permute-start.3 = (bf16[8,3,2048]{2,1,0:T(4,128)(2,1)S(1)}, bf16[8,3,2048]{2,1,0:T(4,128)(2,1)S(1)}, u32[]{:S(2)}, u32[]{:S(2)}) collective-permute-start(bf16[8,3,2048]{2,1,0:T(4,128)(2,1)S(1)} %constant_dynamic-update-slice_fusion.qa_ref), channel_id=1, source_target_pairs={{0,8},{1,9},{2,10},{3,11},{4,12},{5,13},{6,14},{7,15},{8,0},{9,1},... | collective-permute-start | bytes 294920 | tf_op jit(solution)/shard_map/ppermute | solution.py:314
  32.3 0.6 copy-start.2
  50.3 2.4 %collective-permute-start.4 = (bf16[656,512]{1,0:T(8,128)(2,1)}, bf16[656,512]{1,0:T(8,128)(2,1)S(1)}, u32[]{:S(2)}, u32[]{:S(2)}) collective-permute-start(bf16[656,512]{1,0:T(8,128)(2,1)} %get-tuple-element.20), channel_id=1, source_target_pairs={{0,1},{1,0},{2,3},{3,2},{4,5},{5,4},{6,7},{7,6},{8,9},{9,8},{10,11... | collective-permute-start | bytes 2015240 | tf_op jit(solution)/shard_map/ppermute | solution.py:314
  55.1 7.3 %collective-permute-start.5 = (bf16[336,512]{1,0:T(8,128)(2,1)S(1)}, bf16[336,512]{1,0:T(8,128)(2,1)S(1)}, u32[]{:S(2)}, u32[]{:S(2)}) collective-permute-start(bf16[336,512]{1,0:T(8,128)(2,1)S(1)} %pad_maximum_fusion.1), channel_id=1, source_target_pairs={{0,2},{1,5},{2,0},{3,7},{4,6},{5,1},{6,4},{7,3},{8,10},{9,13},{10,... | collective-permute-start | bytes 1032200 | tf_op jit(solution)/shard_map/ppermute | solution.py:314
  62.6 10.4 %collective-permute-start.6 = (bf16[176,512]{1,0:T(8,128)(2,1)S(1)}, bf16[176,512]{1,0:T(8,128)(2,1)S(1)}, u32[]{:S(2)}, u32[]{:S(2)}) collective-permute-start(bf16[176,512]{1,0:T(8,128)(2,1)S(1)} %pad_maximum_fusion.2), channel_id=1, source_target_pairs={{0,8},{1,3},{2,10},{3,1},{4,12},{5,7},{6,14},{7,5},{8,0},{9,11},{1... | collective-permute-start | bytes 540680 | tf_op jit(solution)/shard_map/ppermute | solution.py:314
  73.1 5.5 %collective-permute-start.7 = (bf16[96,512]{1,0:T(8,128)(2,1)S(1)}, bf16[96,512]{1,0:T(8,128)(2,1)S(1)}, u32[]{:S(2)}, u32[]{:S(2)}) collective-permute-start(bf16[96,512]{1,0:T(8,128)(2,1)S(1)} %pad_maximum_fusion.3), channel_id=1, source_target_pairs={{0,4},{1,9},{2,6},{3,11},{4,0},{5,13},{6,2},{7,15},{8,12},{9,1},{1... | collective-permute-start | bytes 294920 | tf_op jit(solution)/shard_map/ppermute | solution.py:314
  78.7 4.5 %collective-permute-start.8 = (bf16[80,512]{1,0:T(8,128)(2,1)S(1)}, bf16[80,512]{1,0:T(8,128)(2,1)S(1)}, u32[]{:S(2)}, u32[]{:S(2)}) collective-permute-start(bf16[80,512]{1,0:T(8,128)(2,1)S(1)} %add_convert_fusion), channel_id=1, source_target_pairs={{0,4},{1,9},{2,6},{3,11},{4,0},{5,13},{6,2},{7,15},{8,12},{9,1},{1... | collective-permute-start | bytes 245768 | tf_op jit(solution)/shard_map/ppermute | solution.py:314
  83.2 7.8 %collective-permute-start.9 = (bf16[160,512]{1,0:T(8,128)(2,1)S(1)}, bf16[160,512]{1,0:T(8,128)(2,1)S(1)}, u32[]{:S(2)}, u32[]{:S(2)}) collective-permute-start(bf16[160,512]{1,0:T(8,128)(2,1)S(1)} %maximum_select_fusion.3), channel_id=1, source_target_pairs={{0,8},{1,3},{2,10},{3,1},{4,12},{5,7},{6,14},{7,5},{8,0},{9,11},{1... | collective-permute-start | bytes 491528 | tf_op jit(solution)/shard_map/ppermute | solution.py:314
  91.1 7.1 %collective-permute-start.10 = (bf16[320,512]{1,0:T(8,128)(2,1)S(1)}, bf16[320,512]{1,0:T(8,128)(2,1)S(1)}, u32[]{:S(2)}, u32[]{:S(2)}) collective-permute-start(bf16[320,512]{1,0:T(8,128)(2,1)S(1)} %maximum_select_fusion.2), channel_id=1, source_target_pairs={{0,2},{1,5},{2,0},{3,7},{4,6},{5,1},{6,4},{7,3},{8,10},{9,13},{10,... | collective-permute-start | bytes 983048 | tf_op jit(solution)/shard_map/ppermute | solution.py:314
  98.6 10.0 %collective-permute-start.11 = (bf16[656,512]{1,0:T(8,128)(2,1)S(1)}, bf16[656,512]{1,0:T(8,128)(2,1)S(1)}, u32[]{:S(2)}, u32[]{:S(2)}) collective-permute-start(bf16[656,512]{1,0:T(8,128)(2,1)S(1)} %pad_maximum_fusion), channel_id=1, source_target_pairs={{0,1},{1,0},{2,3},{3,2},{4,5},{5,4},{6,7},{7,6},{8,9},{9,8},{10,11... | collective-permute-start | bytes 2015240 | tf_op jit(solution)/shard_map/ppermute | solution.py:314

commit v2 on v1

--- a/solution.py
+++ b/solution.py
@@ -32,7 +32,8 @@
     return whole.reshape(reps * tok_slots, 1)
 
 
-def forward_kernel(tlen_ref, labels_ref, enc_ref, pred_ref, w_ref, b_ref, e_ref, st_ref, jt_ref, enc_scr):
+def forward_kernel(begin, tlen_ref, labels_ref, enc_ref, pred_ref, w_ref, b_ref, *refs):
+    e_ref, st_ref, jt_ref, enc_scr = refs[-4:]
     step = pl.program_id(0)
     rows, vocab = e_ref.shape
     tok_slots, width = pred_ref.shape
@@ -42,7 +43,7 @@
     def _():
         enc_scr[...] = enc_ref[...].astype(F32)
 
-    first = pl.multiple_of(step * block_frames, block_frames)
+    first = pl.multiple_of((begin + step) * block_frames, block_frames)
     enc = enc_scr[pl.ds(first, block_frames), :]
     pred = pred_ref[...].astype(F32)
     act = jnp.tanh(enc[:, None, :] + pred[None, :, :]).reshape(rows, width)
@@ -155,7 +156,7 @@
         send_ref[width:, :] = packed.astype(BF16)
 
 
-def input_kernel(enc_ref, pred_ref, d_ref, w_ref, ge_ref, gp_ref, enc_scr, ge_scr, gp_scr):
+def input_kernel(enc_ref, pred_ref, d_ref, w_ref, base_ref, ge_ref, gp_ref, enc_scr, ge_scr):
     step = pl.program_id(0)
     steps = pl.num_programs(0)
     rows = d_ref.shape[0]
@@ -165,7 +166,7 @@
     @pl.when(step == 0)
     def _():
         enc_scr[...] = enc_ref[...].astype(F32)
-        gp_scr[...] = jnp.zeros_like(gp_scr)
+        gp_ref[...] = base_ref[...]
 
     first = pl.multiple_of(step * block_frames, block_frames)
     d_hidden = lax.dot_general(
@@ -175,12 +176,11 @@
     act = jnp.tanh(enc[:, None, :] + pred_ref[...].astype(F32)[None, :, :])
     d_pre = d_hidden.reshape(block_frames, tok_slots, width) * (1.0 - act * act)
     ge_scr[pl.ds(first, block_frames), :] = jnp.sum(d_pre, axis=1)
-    gp_scr[...] += jnp.sum(d_pre, axis=0)
+    gp_ref[...] += jnp.sum(d_pre, axis=0)
 
     @pl.when(step == steps - 1)
     def _():
         ge_ref[...] = ge_scr[...].astype(BF16)
-        gp_ref[...] = gp_scr[...].astype(BF16)
 
 
 def whole(shape):
@@ -190,22 +190,22 @@
 SMEM_SPEC = pl.BlockSpec(memory_space=pltpu.SMEM)
 
 
-def forward(tlen, labels, enc, pred, w, bias, rows):
+def forward(tlen, labels, enc, pred, w, bias, rows, begin, blocks, before):
     frames, width = enc.shape
     tok_slots = pred.shape[0]
     vocab = w.shape[1]
     cells = frames * tok_slots
     return pl.pallas_call(
-        forward_kernel,
-        grid=(cells // rows,),
+        functools.partial(forward_kernel, begin),
+        grid=(blocks,),
         in_specs=[
             SMEM_SPEC, whole(labels.shape), whole(enc.shape), whole(pred.shape),
             whole(w.shape), whole(bias.shape),
-        ],
+        ] + [pl.BlockSpec(memory_space=pl.ANY)] * len(before),
         out_specs=[
-            pl.BlockSpec((rows, vocab), lambda i: (i, 0)),
-            pl.BlockSpec((rows, 4), lambda i: (i, 0)),
-            pl.BlockSpec((width, rows), lambda i: (0, i)),
+            pl.BlockSpec((rows, vocab), lambda i: (i + begin, 0)),
+            pl.BlockSpec((rows, 4), lambda i: (i + begin, 0)),
+            pl.BlockSpec((width, rows), lambda i: (0, i + begin)),
         ],
         out_shape=[
             jax.ShapeDtypeStruct((cells, vocab), F32),
@@ -213,12 +213,13 @@
             jax.ShapeDtypeStruct((width, cells), BF16),
         ],
         scratch_shapes=[pltpu.VMEM((frames, width), F32)],
+        input_output_aliases={6 + k: k for k in range(len(before))},
         compiler_params=params(),
         cost_estimate=pl.CostEstimate(
-            flops=2 * cells * width * vocab, bytes_accessed=16 * 1024 * 1024,
-            transcendentals=cells * (width + vocab),
+            flops=2 * blocks * rows * width * vocab, bytes_accessed=blocks * rows * vocab * 8,
+            transcendentals=blocks * rows * (width + vocab),
         ),
-    )(tlen, labels, enc, pred, w, bias)
+    )(tlen, labels, enc, pred, w, bias, *before)
 
 
 def gradients(pick, flen, tlen, labels, qa, qb, e, st, jt, rows):
@@ -267,29 +268,28 @@
     )(pick, flen, tlen, labels, qa, qb, e, st, jt)
 
 
-def input_gradients(enc, pred, d_low, w, rows):
-    cells, vocab = d_low.shape
+def input_gradients(enc, pred, d_low, w, base, rows, begin):
+    vocab = d_low.shape[1]
+    cells = enc.shape[0] * pred.shape[0]
     return pl.pallas_call(
         input_kernel,
         grid=(cells // rows,),
         in_specs=[
             whole(enc.shape), whole(pred.shape),
-            pl.BlockSpec((rows, vocab), lambda i: (i, 0)), whole(w.shape),
+            pl.BlockSpec((rows, vocab), lambda i: (i + begin, 0)), whole(w.shape), whole(base.shape),
         ],
         out_specs=[whole(enc.shape), whole(pred.shape)],
         out_shape=[
             jax.ShapeDtypeStruct(enc.shape, BF16),
-            jax.ShapeDtypeStruct(pred.shape, BF16),
-        ],
-        scratch_shapes=[
-            pltpu.VMEM(enc.shape, F32), pltpu.VMEM(enc.shape, F32), pltpu.VMEM(pred.shape, F32)
-        ],
+            jax.ShapeDtypeStruct(pred.shape, F32),
+        ],
+        scratch_shapes=[pltpu.VMEM(enc.shape, F32), pltpu.VMEM(enc.shape, F32)],
         compiler_params=params(),
         cost_estimate=pl.CostEstimate(
-            flops=2 * cells * w.shape[0] * vocab, bytes_accessed=6 * 1024 * 1024,
+            flops=2 * cells * w.shape[0] * vocab, bytes_accessed=cells * vocab * 4,
             transcendentals=cells * w.shape[0],
         ),
-    )(enc, pred, d_low, w)
+    )(enc, pred, d_low, w, base)
 
 
 def split_two(value):
@@ -313,21 +313,30 @@
         pairs = [(k, k ^ (odd if k & 1 else even)) for k in range(dp)]
         return lax.ppermute(value, "dp", pairs)
 
-    held = teacher_post
-    for mask in masks[:-1]:
-        held = jnp.concatenate([held, exchange(held, mask, mask)], axis=0)
-    far = exchange(held, masks[-1], masks[-1])
+    blocks = enc.shape[0] * pred.shape[0] // rows
+    quarter = blocks // 4
+    shares = [(0, quarter), (quarter, quarter), (2 * quarter, blocks - 2 * quarter)]
+    bias_row = out_bias.reshape(1, vocab)
+    held, made = teacher_post, ()
+    for k, mask in enumerate(masks):
+        got = exchange(held, mask, mask)
+        part_no = k - (len(masks) - len(shares))
+        if part_no >= 0:
+            begin, number = shares[part_no]
+            made = tuple(forward(
+                token_lengths, labels, enc, pred, out_weight, bias_row, rows, begin, number, made
+            ))
+        if k < len(masks) - 1:
+            held = jnp.concatenate([held, got], axis=0)
+            held, made = lax.optimization_barrier((held, made))
+    far = got
+    e, st, jt = made
     place = lax.dynamic_index_in_dim(assignment, own, keepdims=False) ^ own
     pick = jnp.stack([place, jnp.int32(dp // 2), core]).astype(jnp.int32)
-
-    e, st, jt = forward(
-        token_lengths, labels, enc, pred, out_weight, out_bias.reshape(1, vocab), rows
-    )
     d_low, loss, send, keep, bias = gradients(
         pick, frame_lengths, token_lengths, labels, held, far, e, st, jt, rows
     )
     got = exchange(send, 1, 1)
-    grad_enc, grad_pred = input_gradients(enc, pred, d_low, out_weight, rows)
 
     def got_bias(rows_of):
         return rows_of[0:1].astype(F32) + rows_of[1:2].astype(F32)
@@ -339,22 +348,40 @@
     acc = keep + got[:width].astype(F32)
     bias = bias + got_bias(got[width:])
     rest = masks[1:]
-    even_order = rest[:1] + rest[1:][::-1]
+    even_order = rest
     odd_order = rest[1:2] + rest[:1] + rest[2:]
+    orders = list(zip(even_order, odd_order))
     sides = []
     count = width
-    for even, odd in zip(even_order, odd_order):
-        side = (own & jnp.where(core == 0, even, odd)) != 0
-        sides.append(side)
-        count //= 2
-        top, bottom = acc[:count], acc[count:]
+    frames = enc.shape[0]
+    grad_enc, grad_pred = [], jnp.zeros(pred.shape, F32)
+    for k, (even, odd) in enumerate(orders):
         high, low = split_two(bias)
-        send = jnp.where(side, top, bottom).astype(BF16)
-        got = exchange(jnp.concatenate([send, bias_rows(high, low)], axis=0), even, odd)
-        acc = jnp.where(side, bottom, top) + got[:count].astype(F32)
+        if k < len(orders) - 1:
+            side = (own & jnp.where(core == 0, even, odd)) != 0
+            sides.append(side)
+            count //= 2
+            top, bottom = acc[:count], acc[count:]
+            send = jnp.where(side, top, bottom).astype(BF16)
+            acc = jnp.where(side, bottom, top)
+        else:
+            send = acc.astype(BF16)
+            acc = lax.reduce_precision(acc, 8, 7)
+        send = jnp.concatenate([send, bias_rows(high, low)], axis=0)
+        if k < 2:
+            send, d_low = lax.optimization_barrier((send, d_low))
+        got = exchange(send, even, odd)
+        if k < 2:
+            piece = enc[k * (frames // 2) : (k + 1) * (frames // 2)]
+            grad_rows, grad_pred = input_gradients(
+                piece, pred, d_low, out_weight, grad_pred, rows, k * (blocks // 2)
+            )
+            got, grad_rows, grad_pred = lax.optimization_barrier((got, grad_rows, grad_pred))
+            grad_enc.append(grad_rows)
+        acc = acc + got[:count].astype(F32)
         bias = (high + low) + got_bias(got[count:])
     have = acc.astype(BF16)
-    for even, odd, side in list(zip(even_order, odd_order, sides))[::-1]:
+    for (even, odd), side in list(zip(orders, sides))[::-1]:
         got = exchange(have, even, odd)
         have = jnp.where(
             side, jnp.concatenate([got, have], axis=0), jnp.concatenate([have, got], axis=0)
@@ -371,7 +398,10 @@
         jnp.concatenate([bias, other_bias], axis=1),
         jnp.concatenate([other_bias, bias], axis=1),
     ).reshape(vocab)
-    return (loss[0, 0:1], grad_weight, grad_bias, grad_enc[None], grad_pred[None])
+    return (
+        loss[0, 0:1], grad_weight, grad_bias, jnp.concatenate(grad_enc, axis=0)[None],
+        grad_pred.astype(BF16)[None],
+    )
 
 
 def solution(mesh):

time: 112 us -> 94.9 us (0.85)
  waiting for transfers between devices: 49.4 us -> 22.2 us
  Pallas kernels: 37.6 us -> 43.6 us
  other arithmetic: 6.26 us -> 8.38 us
  local copies, waits for them, and re-layouts: 2.57 us -> 4.55 us
    ppermute x12 -> x11, waiting for transfers between devices: 49.4 us -> 22.2 us  [exchange(): return lax.ppermute(value, 'dp', pairs)]
    pallas_call x1 -> x3, Pallas kernels: 11.6 us -> 15.9 us  [forward(): pl.pallas_call(functools.partial(forward_kernel, begin), grid=(blocks,),...]
    pallas_call x1 -> x2, Pallas kernels: 8.68 us -> 10.5 us  [input_gradients(): pl.pallas_call(input_kernel, grid=(cells // rows,), in_specs=[whole(enc.s...]
    broadcast_in_dim x0 -> x2, other arithmetic: none -> 1.27 us  [the longest x1 0.64 us: on_device(): jnp.concatenate(grad_enc, axis=0)[None]]
    ppermute x12 -> x11, starting transfers between devices: 12.4 us -> 12.5 us  [exchange(): return lax.ppermute(value, 'dp', pairs)]
  transfers between devices with their start and end apart: 12 -> 11, of which waited for: 10 -> 5; matrix products, arithmetic and copies ran while one was open for 2% -> 6% of each run, Pallas kernels for 18% -> 28%
where the time goes in v2:
time: 94.9 us; the launch traced here: 94.1 us
  Pallas kernels  43.6 us (46%)
  waiting for transfers between devices  22.2 us (23%)
  starting transfers between devices  12.5 us (13%)
  other arithmetic  8.38 us (9%)
  local copies, waits for them, and re-layouts  4.55 us (5%)
  between operations  2.85 us (3%)
    ppermute x11, waiting for transfers between devices, exchange(): return lax.ppermute(value, 'dp', pairs)  22.2 us
    pallas_call x1, Pallas kernels, gradients(): pl.pallas_call(grad_kernel, grid_spec=grid_spec, out_shape=[jax.ShapeDtyp...  17.3 us
    pallas_call x3, Pallas kernels, forward(): pl.pallas_call(functools.partial(forward_kernel, begin), grid=(blocks,),...  15.9 us
    ppermute x11, starting transfers between devices, exchange(): return lax.ppermute(value, 'dp', pairs)  12.5 us
    pallas_call x2, Pallas kernels, input_gradients(): pl.pallas_call(input_kernel, grid=(cells // rows,), in_specs=[whole(enc.s...  10.5 us
  transfers between devices with their start and end apart: 11, of which 5 were waited for; matrix products, arithmetic and copies ran while one was open for 6% of the time, Pallas kernels for 28%

profile of v2, /device:TPU:0, one launch (start us, length us, event | category | flops | bytes accessed | tf_op | source)
XLA Modules:
  0.0 94.1 jit_solution(2935385856755350870)
XLA Ops:
  0.6 0.5 collective-permute-start
  1.1 1.2 %dynamic_slice.4 = s32[1]{0:T(128)} dynamic-slice(s32[16]{0:T(128)} %param.10, s32[]{:T(128)S(6)} %select_n.70), dynamic_slice_sizes={1} | dynamic-slice | bytes 12 | tf_op jit(solution)/shard_map/jit(dynamic_index_in_dim)/dynamic_slice | solution.py:334
  3.0 0.6 pad_add_fusion.pick_ref
  4.3 0.7 pad_maximum_fusion.6
  5.0 2.6 %collective-permute-start.1 = (bf16[2,3,2048]{2,1,0:T(4,128)(2,1)S(1)}, bf16[2,3,2048]{2,1,0:T(4,128)(2,1)S(1)}, u32[]{:S(2)}, u32[]{:S(2)}) collective-permute-start(bf16[2,3,2048]{2,1,0:T(4,128)(2,1)S(1)} %pad_maximum_fusion.6), channel_id=1, source_target_pairs={{0,2},{1,3},{2,0},{3,1},{4,6},{5,7},{6,4},{7,5},{8,10},{9,11},{10,... | collective-permute-start | bytes 73736 | tf_op jit(solution)/shard_map/ppermute | solution.py:314
  7.6 4.5 %shard_map.128 = (f32[2048,1024]{1,0:T(8,128)}, f32[2048,4]{1,0:T(8,128)}, bf16[640,2048]{1,0:T(8,128)(2,1)}) custom-call(s32[1]{0:T(128)S(6)} %copy.27.tlen_ref, s32[1,31]{1,0:T(1,128)} %labels_ref.7, bf16[64,640]{1,0:T(8,128)(2,1)} %bitcast.17, bf16[32,640]{1,0:T(8,128)(2,1)} %bitcast.20, bf16[640,1024]{1,0:T(8,128)(2,1)} %w_ref.9, f32[1,1024]{1,0:T(1,128)} %bitcast.25), custom_call_target="tpu_custom_call" | custom-call | flops 671088640 | bytes 4194304 | tf_op jit(solution)/shard_map/pallas_call | solution.py:198
  12.8 1.6 %collective-permute-start.2 = (bf16[4,3,2048]{2,1,0:T(4,128)(2,1)S(1)}, bf16[4,3,2048]{2,1,0:T(4,128)(2,1)S(1)}, u32[]{:S(2)}, u32[]{:S(2)}) collective-permute-start(bf16[4,3,2048]{2,1,0:T(4,128)(2,1)S(1)} %pad_maximum_fusion.5), channel_id=1, source_target_pairs={{0,4},{1,5},{2,6},{3,7},{4,0},{5,1},{6,2},{7,3},{8,12},{9,13},{10,... | collective-permute-start | bytes 147464 | tf_op jit(solution)/shard_map/ppermute | solution.py:314
  14.5 4.5 %shard_map.129 = (f32[2048,1024]{1,0:T(8,128)}, f32[2048,4]{1,0:T(8,128)}, bf16[640,2048]{1,0:T(8,128)(2,1)}) custom-call(s32[1]{0:T(128)S(6)} %copy.27.tlen_ref, s32[1,31]{1,0:T(1,128)} %labels_ref.7, bf16[64,640]{1,0:T(8,128)(2,1)} %bitcast.18, bf16[32,640]{1,0:T(8,128)(2,1)} %bitcast.21, ...), custom_call_target="tpu_custom_call", output_to_operand_aliasing={{0}: (6, {}), {1}: (7, {}), {2}: (8, {})} | custom-call | flops 671088640 | bytes 4194304 | tf_op jit(solution)/shard_map/pallas_call | solution.py:198
  19.1 2.7 %collective-permute-start.3 = (bf16[8,3,2048]{2,1,0:T(4,128)(2,1)S(1)}, bf16[8,3,2048]{2,1,0:T(4,128)(2,1)S(1)}, u32[]{:S(2)}, u32[]{:S(2)}) collective-permute-start(bf16[8,3,2048]{2,1,0:T(4,128)(2,1)S(1)} %pad_maximum_fusion.4.qa_ref), channel_id=1, source_target_pairs={{0,8},{1,9},{2,10},{3,11},{4,12},{5,13},{6,14},{7,15},{8,0},{9,1},... | collective-permute-start | bytes 294920 | tf_op jit(solution)/shard_map/ppermute | solution.py:314
  21.7 6.9 %shard_map.130 = (f32[2048,1024]{1,0:T(8,128)}, f32[2048,4]{1,0:T(8,128)}, bf16[640,2048]{1,0:T(8,128)(2,1)}) custom-call(s32[1]{0:T(128)S(6)} %copy.27.tlen_ref, s32[1,31]{1,0:T(1,128)} %labels_ref.7, bf16[64,640]{1,0:T(8,128)(2,1)} %bitcast.19, bf16[32,640]{1,0:T(8,128)(2,1)} %bitcast.22, ...), custom_call_target="tpu_custom_call", output_to_operand_aliasing={{0}: (6, {}), {1}: (7, {}), {2}: (8, {})} | custom-call | flops 1342177280 | bytes 8388608 | tf_op jit(solution)/shard_map/pallas_call | solution.py:198
  28.6 0.6 copy-done.2
  29.2 17.3 %shard_map.131 = (bf16[2048,1024]{1,0:T(8,128)(2,1)}, f32[8,128]{1,0:T(8,128)}, bf16[656,512]{1,0:T(8,128)(2,1)}, f32[640,512]{1,0:T(8,128)}, f32[1,512]{1,0:T(1,128)}) custom-call(s32[3]{0:T(128)} %pad_add_fusion.pick_ref, s32[1]{0:T(128)S(6)} %copy.26.flen_ref, s32[1]{0:T(128)S(6)} %copy.27.tlen_ref, s32[1,31]{1,0:T(1,128)} %labels_ref.7, ...), custom_call_target="tpu_custom_call" | custom-call | flops 2684354560 | bytes 16777216 | tf_op jit(solution)/shard_map/pallas_call | solution.py:254
  46.7 2.3 %collective-permute-done.4 = bf16[656,512]{1,0:T(8,128)(2,1)S(1)} collective-permute-done((bf16[656,512]{1,0:T(8,128)(2,1)}, bf16[656,512]{1,0:T(8,128)(2,1)S(1)}, u32[]{:S(2)}, u32[]{:S(2)}) %collective-permute-start.4) | collective-permute-done | bytes 671776 | tf_op jit(solution)/shard_map/ppermute | solution.py:314
  49.0 0.7 reduce-precision_convert_fusion.3
  49.7 1.5 %convert_add_fusion = f32[640,512]{1,0:T(8,128)S(1)} fusion(f32[640,512]{1,0:T(8,128)} %get-tuple-element.59, bf16[656,512]{1,0:T(8,128)(2,1)S(1)} %collective-permute-done.4), kind=kLoop, calls=%fused_computation.2 | loop fusion | flops 655360 | bytes 3276800 | tf_op jit(solution)/shard_map/add | solution.py:348
  51.3 0.6 collective-permute-start.5
  52.1 0.6 slice_bitcast_fusion
  52.7 0.6 broadcast_in_dim.9.base_ref
  53.3 5.2 %shard_map.132 = (bf16[32,640]{1,0:T(8,128)(2,1)}, f32[32,640]{1,0:T(8,128)}) custom-call(bf16[32,640]{1,0:T(8,128)(2,1)} %get-tuple-element.86.enc_ref, bf16[32,640]{1,0:T(8,128)(2,1)} %bitcast.23, bf16[2048,1024]{1,0:T(8,128)(2,1)} %get-tuple-element.69.d_ref, bf16[640,1024]{1,0:T(8,128)(2,1)} %w_ref.9, f32[32,640]{1,0:T(8,128)} %broadcast_in_dim.9.base_ref), custom_call_target="tpu_custom_call" | custom-call | flops 1342177280 | bytes 4194304 | tf_op jit(solution)/shard_map/pallas_call | solution.py:274
  58.9 0.5 collective-permute-start.6
  59.4 5.2 %shard_map.133 = (bf16[32,640]{1,0:T(8,128)(2,1)}, f32[32,640]{1,0:T(8,128)}) custom-call(bf16[32,640]{1,0:T(8,128)(2,1)} %get-tuple-element.85.enc_ref, bf16[32,640]{1,0:T(8,128)(2,1)} %bitcast.24, bf16[2048,1024]{1,0:T(8,128)(2,1)} %get-tuple-element.69.d_ref, bf16[640,1024]{1,0:T(8,128)(2,1)} %w_ref.9, f32[32,640]{1,0:T(8,128)} %get-tuple-element.70.base_ref), custom_call_target="tpu_custom_call" | custom-call | flops 1342177280 | bytes 4194304 | tf_op jit(solution)/shard_map/pallas_call | solution.py:274
  64.8 2.2 %collective-permute-start.7 = (bf16[176,512]{1,0:T(8,128)(2,1)S(1)}, bf16[176,512]{1,0:T(8,128)(2,1)S(1)}, u32[]{:S(2)}, u32[]{:S(2)}) collective-permute-start(bf16[176,512]{1,0:T(8,128)(2,1)S(1)} %pad_maximum_fusion.2), channel_id=1, source_target_pairs={{0,8},{1,9},{2,10},{3,11},{4,12},{5,13},{6,14},{7,15},{8,0},{9,1},... | collective-permute-start | bytes 540680 | tf_op jit(solution)/shard_map/ppermute | solution.py:314
  67.0 8.9 %collective-permute-done.7 = bf16[176,512]{1,0:T(8,128)(2,1)S(1)} collective-permute-done((bf16[176,512]{1,0:T(8,128)(2,1)S(1)}, bf16[176,512]{1,0:T(8,128)(2,1)S(1)}, u32[]{:S(2)}, u32[]{:S(2)}) %collective-permute-start.7) | collective-permute-done | bytes 180256 | tf_op jit(solution)/shard_map/ppermute | solution.py:314
  76.1 5.3 %collective-permute-done.8 = bf16[160,512]{1,0:T(8,128)(2,1)S(1)} collective-permute-done((bf16[160,512]{1,0:T(8,128)(2,1)S(1)}, bf16[160,512]{1,0:T(8,128)(2,1)S(1)}, u32[]{:S(2)}, u32[]{:S(2)}) %collective-permute-start.8) | collective-permute-done | bytes 163872 | tf_op jit(solution)/shard_map/ppermute | solution.py:314
  81.5 1.6 %collective-permute-start.9 = (bf16[320,512]{1,0:T(8,128)(2,1)S(1)}, bf16[320,512]{1,0:T(8,128)(2,1)S(1)}, u32[]{:S(2)}, u32[]{:S(2)}) collective-permute-start(bf16[320,512]{1,0:T(8,128)(2,1)S(1)} %maximum_select_fusion.2), channel_id=1, source_target_pairs={{0,2},{1,5},{2,0},{3,7},{4,6},{5,1},{6,4},{7,3},{8,10},{9,13},{10,... | collective-permute-start | bytes 983048 | tf_op jit(solution)/shard_map/ppermute | solution.py:314
  83.1 5.5 %collective-permute-done.9 = bf16[320,512]{1,0:T(8,128)(2,1)S(1)} collective-permute-done((bf16[320,512]{1,0:T(8,128)(2,1)S(1)}, bf16[320,512]{1,0:T(8,128)(2,1)S(1)}, u32[]{:S(2)}, u32[]{:S(2)}) %collective-permute-start.9) | collective-permute-done | bytes 327712 | tf_op jit(solution)/shard_map/ppermute | solution.py:314
  88.7 0.3 maximum_select_fusion.1
  89.1 1.2 %slice.87 = f32[1,1]{1,0:T(1,128)} slice(f32[8,128]{1,0:T(8,128)} %get-tuple-element.58), slice={[0:1], [0:1]} | slice | bytes 8 | tf_op jit(solution)/shard_map/slice | solution.py:402
  90.3 0.6 maximum_bitcast_fusion
  90.9 0.6 convert_bitcast_fusion
  91.6 1.9 %fusion = f32[640,1024]{1,0:T(8,128)} fusion(bf16[640,512]{1,0:T(8,128)(2,1)S(1)} %slice.121, bf16[640,512]{1,0:T(8,128)(2,1)S(1)} %maximum_select_fusion.1, pred[]{:T(512)S(6)} %eq.2), kind=kLoop, calls=%fused_computation.1 | loop fusion | flops 6553600 | bytes 3932161 | tf_op jit(solution)/shard_map/convert_element_type | solution.py:394
  93.5 0.6 maximum_select_fusion.3
  (43 shorter events, 1.4 us)
Async XLA Ops:
  0.6 3.7 %collective-permute-start = (bf16[1,3,2048]{2,1,0:T(4,128)(2,1)}, bf16[1,3,2048]{2,1,0:T(4,128)(2,1)S(1)}, u32[]{:S(2)}, u32[]{:S(2)}) collective-permute-start(bf16[1,3,2048]{2,1,0:T(4,128)(2,1)} %param.9), channel_id=1, source_target_pairs={{0,1},{1,0},{2,3},{3,2},{4,5},{5,4},{6,7},{7,6},{8,9},{9,8},{10,11... | collective-permute-start | bytes 36872 | tf_op jit(solution)/shard_map/ppermute | solution.py:314
  5.0 7.7 %collective-permute-start.1 = (bf16[2,3,2048]{2,1,0:T(4,128)(2,1)S(1)}, bf16[2,3,2048]{2,1,0:T(4,128)(2,1)S(1)}, u32[]{:S(2)}, u32[]{:S(2)}) collective-permute-start(bf16[2,3,2048]{2,1,0:T(4,128)(2,1)S(1)} %pad_maximum_fusion.6), channel_id=1, source_target_pairs={{0,2},{1,3},{2,0},{3,1},{4,6},{5,7},{6,4},{7,5},{8,10},{9,11},{10,... | collective-permute-start | bytes 73736 | tf_op jit(solution)/shard_map/ppermute | solution.py:314
  12.8 6.1 %collective-permute-start.2 = (bf16[4,3,2048]{2,1,0:T(4,128)(2,1)S(1)}, bf16[4,3,2048]{2,1,0:T(4,128)(2,1)S(1)}, u32[]{:S(2)}, u32[]{:S(2)}) collective-permute-start(bf16[4,3,2048]{2,1,0:T(4,128)(2,1)S(1)} %pad_maximum_fusion.5), channel_id=1, source_target_pairs={{0,4},{1,5},{2,6},{3,7},{4,0},{5,1},{6,2},{7,3},{8,12},{9,13},{10,... | collective-permute-start | bytes 147464 | tf_op jit(solution)/shard_map/ppermute | solution.py:314
  19.1 9.5 %copy-start.1 = (bf16[8,3,2048]{2,1,0:T(4,128)(2,1)}, bf16[8,3,2048]{2,1,0:T(4,128)(2,1)S(1)}, u32[]{:S(2)}) copy-start(bf16[8,3,2048]{2,1,0:T(4,128)(2,1)S(1)} %pad_maximum_fusion.4.qa_ref) | copy-start | bytes 294916
  19.1 9.5 %collective-permute-start.3 = (bf16[8,3,2048]{2,1,0:T(4,128)(2,1)S(1)}, bf16[8,3,2048]{2,1,0:T(4,128)(2,1)S(1)}, u32[]{:S(2)}, u32[]{:S(2)}) collective-permute-start(bf16[8,3,2048]{2,1,0:T(4,128)(2,1)S(1)} %pad_maximum_fusion.4.qa_ref), channel_id=1, source_target_pairs={{0,8},{1,9},{2,10},{3,11},{4,12},{5,13},{6,14},{7,15},{8,0},{9,1},... | collective-permute-start | bytes 294920 | tf_op jit(solution)/shard_map/ppermute | solution.py:314
  28.6 0.6 copy-start.2
  46.6 2.4 %collective-permute-start.4 = (bf16[656,512]{1,0:T(8,128)(2,1)}, bf16[656,512]{1,0:T(8,128)(2,1)S(1)}, u32[]{:S(2)}, u32[]{:S(2)}) collective-permute-start(bf16[656,512]{1,0:T(8,128)(2,1)} %get-tuple-element.60), channel_id=1, source_target_pairs={{0,1},{1,0},{2,3},{3,2},{4,5},{5,4},{6,7},{7,6},{8,9},{9,8},{10,11... | collective-permute-start | bytes 2015240 | tf_op jit(solution)/shard_map/ppermute | solution.py:314
  51.2 0.9 copy-start
  51.3 7.3 %collective-permute-start.5 = (bf16[336,512]{1,0:T(8,128)(2,1)S(1)}, bf16[336,512]{1,0:T(8,128)(2,1)S(1)}, u32[]{:S(2)}, u32[]{:S(2)}) collective-permute-start(bf16[336,512]{1,0:T(8,128)(2,1)S(1)} %pad_maximum_fusion.1), channel_id=1, source_target_pairs={{0,2},{1,5},{2,0},{3,7},{4,6},{5,1},{6,4},{7,3},{8,10},{9,13},{10,... | collective-permute-start | bytes 1032200 | tf_op jit(solution)/shard_map/ppermute | solution.py:314
  58.9 5.8 %collective-permute-start.6 = (bf16[176,512]{1,0:T(8,128)(2,1)S(1)}, bf16[176,512]{1,0:T(8,128)(2,1)S(1)}, u32[]{:S(2)}, u32[]{:S(2)}) collective-permute-start(bf16[176,512]{1,0:T(8,128)(2,1)S(1)} %pad_maximum_fusion.3), channel_id=1, source_target_pairs={{0,4},{1,3},{2,6},{3,1},{4,0},{5,7},{6,2},{7,5},{8,12},{9,11},{10,... | collective-permute-start | bytes 540680 | tf_op jit(solution)/shard_map/ppermute | solution.py:314
  64.8 11.2 %collective-permute-start.7 = (bf16[176,512]{1,0:T(8,128)(2,1)S(1)}, bf16[176,512]{1,0:T(8,128)(2,1)S(1)}, u32[]{:S(2)}, u32[]{:S(2)}) collective-permute-start(bf16[176,512]{1,0:T(8,128)(2,1)S(1)} %pad_maximum_fusion.2), channel_id=1, source_target_pairs={{0,8},{1,9},{2,10},{3,11},{4,12},{5,13},{6,14},{7,15},{8,0},{9,1},... | collective-permute-start | bytes 540680 | tf_op jit(solution)/shard_map/ppermute | solution.py:314
  76.0 5.4 %collective-permute-start.8 = (bf16[160,512]{1,0:T(8,128)(2,1)S(1)}, bf16[160,512]{1,0:T(8,128)(2,1)S(1)}, u32[]{:S(2)}, u32[]{:S(2)}) collective-permute-start(bf16[160,512]{1,0:T(8,128)(2,1)S(1)} %add_convert_fusion), channel_id=1, source_target_pairs={{0,4},{1,3},{2,6},{3,1},{4,0},{5,7},{6,2},{7,5},{8,12},{9,11},{10,... | collective-permute-start | bytes 491528 | tf_op jit(solution)/shard_map/ppermute | solution.py:314
  81.5 8.8 %copy-start.4 = (bf16[32,640]{1,0:T(8,128)(2,1)S(1)}, bf16[32,640]{1,0:T(8,128)(2,1)}, u32[]{:S(2)}) copy-start(bf16[32,640]{1,0:T(8,128)(2,1)} %get-tuple-element.74) | copy-start | bytes 122884
  81.5 8.8 %copy-start.5 = (bf16[32,640]{1,0:T(8,128)(2,1)S(1)}, bf16[32,640]{1,0:T(8,128)(2,1)}, u32[]{:S(2)}) copy-start(bf16[32,640]{1,0:T(8,128)(2,1)} %get-tuple-element.75) | copy-start | bytes 122884
  81.5 7.1 %collective-permute-start.9 = (bf16[320,512]{1,0:T(8,128)(2,1)S(1)}, bf16[320,512]{1,0:T(8,128)(2,1)S(1)}, u32[]{:S(2)}, u32[]{:S(2)}) collective-permute-start(bf16[320,512]{1,0:T(8,128)(2,1)S(1)} %maximum_select_fusion.2), channel_id=1, source_target_pairs={{0,2},{1,5},{2,0},{3,7},{4,6},{5,1},{6,4},{7,3},{8,10},{9,13},{10,... | collective-permute-start | bytes 983048 | tf_op jit(solution)/shard_map/ppermute | solution.py:314
  83.1 7.8 %copy-start.3 = (f32[32,640]{1,0:T(8,128)S(1)}, f32[32,640]{1,0:T(8,128)}, u32[]{:S(2)}) copy-start(f32[32,640]{1,0:T(8,128)} %get-tuple-element.76) | copy-start | bytes 245764
  89.0 2.6 %collective-permute-start.10 = (bf16[656,512]{1,0:T(8,128)(2,1)S(1)}, bf16[656,512]{1,0:T(8,128)(2,1)S(1)}, u32[]{:S(2)}, u32[]{:S(2)}) collective-permute-start(bf16[656,512]{1,0:T(8,128)(2,1)S(1)} %pad_maximum_fusion), channel_id=1, source_target_pairs={{0,1},{1,0},{2,3},{3,2},{4,5},{5,4},{6,7},{7,6},{8,9},{9,8},{10,11... | collective-permute-start | bytes 2015240 | tf_op jit(solution)/shard_map/ppermute | solution.py:314

commit v3 on v2

--- a/solution.py
+++ b/solution.py
@@ -11,7 +11,7 @@
 BF16 = jnp.bfloat16
 LANES = 128
 EXTRA = 16
-VMEM_LIMIT = 56 * 1024 * 1024
+VMEM_LIMIT = 24 * 1024 * 1024
 
 
 def params():
@@ -32,8 +32,11 @@
     return whole.reshape(reps * tok_slots, 1)
 
 
+SUB = 256
+
+
 def forward_kernel(begin, tlen_ref, labels_ref, enc_ref, pred_ref, w_ref, b_ref, *refs):
-    e_ref, st_ref, jt_ref, enc_scr = refs[-4:]
+    e_ref, st_ref, jt_ref, enc_scr, logit_scr = refs[-5:]
     step = pl.program_id(0)
     rows, vocab = e_ref.shape
     tok_slots, width = pred_ref.shape
@@ -46,36 +49,54 @@
     first = pl.multiple_of((begin + step) * block_frames, block_frames)
     enc = enc_scr[pl.ds(first, block_frames), :]
     pred = pred_ref[...].astype(F32)
-    act = jnp.tanh(enc[:, None, :] + pred[None, :, :]).reshape(rows, width)
-    joint_in = act.astype(BF16)
-    jt_ref[...] = joint_in.T
-    logits = jnp.dot(joint_in, w_ref[...], preferred_element_type=F32) + b_ref[...]
-    row_max = jnp.max(logits, axis=1, keepdims=True)
-    target = target_column(labels_ref, tlen_ref[0], tok_slots, block_frames)
-    lane = lax.broadcasted_iota(jnp.int32, (rows, LANES), 1)
-    rest_acc = jnp.zeros((rows, LANES), F32)
-    label_acc = jnp.zeros((rows, LANES), F32)
-    for j in range(vocab // LANES):
-        shifted = logits[:, j * LANES : (j + 1) * LANES] - row_max
-        e = jnp.exp(shifted)
-        e_ref[:, j * LANES : (j + 1) * LANES] = e
-        hot = lane == target - j * LANES
-        rest = jnp.where(hot, 0.0, e)
-        if j == 0:
-            z_blank = shifted[:, 0:1]
-            rest = jnp.where(lane == 0, 0.0, rest)
-        rest_acc = rest_acc + rest
-        label_acc = label_acc + jnp.where(hot, shifted, 0.0)
-    rest_sum = jnp.sum(rest_acc, axis=1, keepdims=True)
-    z_label = jnp.sum(label_acc, axis=1, keepdims=True)
-    e_label = jnp.where(target >= 0, jnp.exp(z_label), 0.0)
-    total = rest_sum + jnp.exp(z_blank) + e_label
-    st_ref[...] = jnp.concatenate([total, rest_sum, z_blank, z_label], axis=1)
+    sub_frames = SUB // tok_slots
+    target = target_column(labels_ref, tlen_ref[0], tok_slots, sub_frames)
+    lane = lax.broadcasted_iota(jnp.int32, (SUB, LANES), 1)
+    parts = rows // SUB
+
+    def multiply(k):
+        place = slice(k * SUB, (k + 1) * SUB)
+        act = jnp.tanh(enc[k * sub_frames : (k + 1) * sub_frames, None, :] + pred[None, :, :])
+        joint_in = act.reshape(SUB, width).astype(BF16)
+        jt_ref[:, place] = joint_in.T
+        logit_scr[k % 2] = jnp.dot(joint_in, w_ref[...], preferred_element_type=F32)
+
+    def collapse(k):
+        place = slice(k * SUB, (k + 1) * SUB)
+        tops = jnp.full((SUB, LANES), -jnp.inf, F32)
+        for j in range(vocab // LANES):
+            cols = slice(j * LANES, (j + 1) * LANES)
+            tops = jnp.maximum(tops, logit_scr[k % 2, :, cols] + b_ref[:, cols])
+        row_max = jnp.max(tops, axis=1, keepdims=True)
+        rest_acc = jnp.zeros((SUB, LANES), F32)
+        label_acc = jnp.zeros((SUB, LANES), F32)
+        for j in range(vocab // LANES):
+            cols = slice(j * LANES, (j + 1) * LANES)
+            shifted = logit_scr[k % 2, :, cols] + b_ref[:, cols] - row_max
+            e = jnp.exp(shifted)
+            e_ref[place, cols] = e
+            hot = lane == target - j * LANES
+            rest = jnp.where(hot, 0.0, e)
+            if j == 0:
+                z_blank = shifted[:, 0:1]
+                rest = jnp.where(lane == 0, 0.0, rest)
+            rest_acc = rest_acc + rest
+            label_acc = label_acc + jnp.where(hot, shifted, 0.0)
+        rest_sum = jnp.sum(rest_acc, axis=1, keepdims=True)
+        z_label = jnp.sum(label_acc, axis=1, keepdims=True)
+        packed = jnp.where(lane == 0, rest_sum, jnp.where(lane == 1, z_blank, z_label))
+        st_ref[:, place] = packed.T[:8]
+
+    multiply(0)
+    for k in range(parts):
+        if k + 1 < parts:
+            multiply(k + 1)
+        collapse(k)
 
 
 def grad_kernel(
     pick_ref, flen_ref, tlen_ref, labels_ref, qa_ref, qb_ref, e_ref, st_ref, jt_ref,
-    d_ref, loss_ref, send_ref, keep_ref, keepb_ref, d_scr, gb_scr, loss_scr,
+    d_ref, loss_ref, send_ref, keep_ref, keepb_ref, d_scr, gb_scr, loss_scr, target_scr,
 ):
     step = pl.program_id(0)
     steps = pl.num_programs(0)
@@ -83,48 +104,55 @@
     tok_slots = labels_ref.shape[1] + 1
     block_frames = rows // tok_slots
     width = jt_ref.shape[0]
+    frame_len, token_len = flen_ref[0], tlen_ref[0]
 
     @pl.when(step == 0)
     def _():
         gb_scr[...] = jnp.zeros_like(gb_scr)
         loss_scr[...] = jnp.zeros_like(loss_scr)
+        column = target_column(labels_ref, token_len, tok_slots, block_frames)
+        target_scr[...] = jnp.broadcast_to(column, (rows, LANES))
 
     half_count = pick_ref[1]
-    chosen = jnp.where(pick_ref[0] < half_count, qa_ref[0].astype(F32), qb_ref[0].astype(F32))
-    padded = jnp.concatenate([chosen, jnp.zeros((5, rows), F32)], axis=0)
-    q = padded.T
-    frame_len, token_len = flen_ref[0], tlen_ref[0]
-    row = lax.broadcasted_iota(jnp.int32, (block_frames, tok_slots, 1), 0).reshape(rows, 1)
-    frame = row + step * block_frames
-    token = lax.broadcasted_iota(jnp.int32, (block_frames, tok_slots, 1), 1).reshape(rows, 1)
-    count = (frame_len * (token_len + 1)).astype(F32)
+    q = jnp.where(pick_ref[0] < half_count, qa_ref[0].astype(F32), qb_ref[0].astype(F32))
+    cell = lax.broadcasted_iota(jnp.int32, (1, rows), 1)
+    frame = lax.div(cell, tok_slots) + step * block_frames
+    token = lax.rem(cell, tok_slots)
+    has_label = token < token_len
+    count = jnp.full((1, rows), frame_len * (token_len + 1), jnp.int32).astype(F32)
     weight = jnp.where((frame < frame_len) & (token <= token_len), 1.0 / count, 0.0)
-    q_blank = q[:, 0:1]
-    q_label = jnp.where(token < token_len, q[:, 1:2], 0.0)
-    q_rest = q[:, 2:3]
-    total = st_ref[:, 0:1]
-    rest_sum = st_ref[:, 1:2]
-    z_blank = st_ref[:, 2:3]
-    z_label = st_ref[:, 3:4]
+    q_blank = q[0:1]
+    q_label = jnp.where(has_label, q[1:2], 0.0)
+    q_rest = q[2:3]
+    rest_sum = st_ref[0:1]
+    z_blank = st_ref[1:2]
+    z_label = st_ref[2:3]
+    e_blank = jnp.exp(z_blank)
+    e_label = jnp.exp(z_label)
+    total = rest_sum + e_blank + jnp.where(has_label, e_label, 0.0)
     log_total = jnp.log(total)
     cell_loss = -(
         q_blank * (z_blank - log_total)
         + q_label * (z_label - log_total)
         + q_rest * (jnp.log(rest_sum) - log_total)
     )
-    loss_scr[...] += jnp.sum((cell_loss * weight).reshape(rows // 8, 8, 1), axis=0)
+    loss_scr[...] += cell_loss * weight
     soft = weight * (q_blank + q_label + q_rest) / total
     scale = soft - weight * q_rest / rest_sum
-    d_blank = soft * jnp.exp(z_blank) - weight * q_blank
-    d_label = soft * jnp.exp(z_label) - weight * q_label
-    target = target_column(labels_ref, token_len, tok_slots, block_frames)
+    d_blank = soft * e_blank - weight * q_blank
+    d_label = soft * e_label - weight * q_label
+    place = lax.broadcasted_iota(jnp.int32, (8, rows), 0)
+    packed = jnp.where(place == 0, scale, jnp.where(place == 1, d_label, d_blank))
+    columns = packed.T
+    scale = jnp.broadcast_to(columns[:, 0:1], (rows, LANES))
+    d_label = jnp.broadcast_to(columns[:, 1:2], (rows, LANES))
     lane = lax.broadcasted_iota(jnp.int32, (rows, LANES), 1)
     base = pl.multiple_of(step * rows, rows)
     for j in range(vocab // LANES):
         cols = slice(j * LANES, (j + 1) * LANES)
-        d = jnp.where(lane == target - j * LANES, d_label, e_ref[:, cols] * scale)
+        d = jnp.where(lane + j * LANES == target_scr[...], d_label, e_ref[:, cols] * scale)
         if j == 0:
-            d = jnp.where(lane == 0, d_blank, d)
+            d = jnp.where(lane == 0, columns[:, 2:3], d)
         low = d.astype(BF16)
         d_ref[:, cols] = low
         d_scr[pl.ds(base, rows), cols] = low
@@ -132,18 +160,14 @@
 
     @pl.when(step == steps - 1)
     def _():
-        loss_ref[...] = jnp.broadcast_to(jnp.sum(loss_scr[...], axis=0, keepdims=True), loss_ref.shape)
+        loss_ref[...] = jnp.broadcast_to(jnp.sum(loss_scr[...], axis=1, keepdims=True), loss_ref.shape)
         part = vocab // 2
-        tile = part // 2
         core = pick_ref[2]
-        for j in range(2):
-            col = pl.multiple_of((1 - core) * part + j * tile, tile)
-            dw = jnp.dot(jt_ref[...], d_scr[:, pl.ds(col, tile)], preferred_element_type=F32)
-            send_ref[:width, j * tile : (j + 1) * tile] = dw.astype(BF16)
-        for j in range(2):
-            col = pl.multiple_of(core * part + j * tile, tile)
-            dw = jnp.dot(jt_ref[...], d_scr[:, pl.ds(col, tile)], preferred_element_type=F32)
-            keep_ref[:, j * tile : (j + 1) * tile] = dw
+        col = pl.multiple_of((1 - core) * part, part)
+        dw = jnp.dot(jt_ref[...], d_scr[:, pl.ds(col, part)], preferred_element_type=F32)
+        send_ref[:width, :] = dw.astype(BF16)
+        col = pl.multiple_of(core * part, part)
+        keep_ref[...] = jnp.dot(jt_ref[...], d_scr[:, pl.ds(col, part)], preferred_element_type=F32)
         bias = jnp.sum(gb_scr[...], axis=0, keepdims=True)
         first, second = bias[:, :part], bias[:, part:]
         mine = jnp.where(core == 0, first, second)
@@ -204,15 +228,15 @@
         ] + [pl.BlockSpec(memory_space=pl.ANY)] * len(before),
         out_specs=[
             pl.BlockSpec((rows, vocab), lambda i: (i + begin, 0)),
-            pl.BlockSpec((rows, 4), lambda i: (i + begin, 0)),
+            pl.BlockSpec((8, rows), lambda i: (0, i + begin)),
             pl.BlockSpec((width, rows), lambda i: (0, i + begin)),
         ],
         out_shape=[
             jax.ShapeDtypeStruct((cells, vocab), F32),
-            jax.ShapeDtypeStruct((cells, 4), F32),
+            jax.ShapeDtypeStruct((8, cells), F32),
             jax.ShapeDtypeStruct((width, cells), BF16),
         ],
-        scratch_shapes=[pltpu.VMEM((frames, width), F32)],
+        scratch_shapes=[pltpu.VMEM((frames, width), F32), pltpu.VMEM((2, SUB, vocab), F32)],
         input_output_aliases={6 + k: k for k in range(len(before))},
         compiler_params=params(),
         cost_estimate=pl.CostEstimate(
@@ -235,7 +259,7 @@
             pl.BlockSpec((1, 3, rows), lambda i, pick: (lax.rem(pick[0], pick[1]), 0, i)),
             pl.BlockSpec((1, 3, rows), lambda i, pick: (lax.rem(pick[0], pick[1]), 0, i)),
             pl.BlockSpec((rows, vocab), lambda i, pick: (i, 0)),
-            pl.BlockSpec((rows, 4), lambda i, pick: (i, 0)),
+            pl.BlockSpec((8, rows), lambda i, pick: (0, i)),
             whole(jt.shape),
         ],
         out_specs=[
@@ -248,7 +272,8 @@
         scratch_shapes=[
             pltpu.VMEM((cells, vocab), BF16),
             pltpu.VMEM((8, vocab), F32),
-            pltpu.VMEM((8, 1), F32),
+            pltpu.VMEM((1, rows), F32),
+            pltpu.VMEM((rows, LANES), jnp.int32),
         ],
     )
     return pl.pallas_call(
@@ -305,7 +330,7 @@
     core = own & 1
     masks = [1 << k for k in range(dp.bit_length() - 1)]
     enc, pred = encoder_out[0], predictor_out[0]
-    rows = 8 * pred.shape[0]
+    rows = 16 * pred.shape[0]
     width, vocab = out_weight.shape
     part = vocab // 2
 

time: 94.9 us -> 79.2 us (0.83)
  Pallas kernels: 43.6 us -> 18.8 us
  waiting for transfers between devices: 22.2 us -> 28.4 us
  local copies, waits for them, and re-layouts: 4.55 us -> 10.6 us
  other arithmetic: 8.38 us -> 5.86 us
    pallas_call x1, Pallas kernels: 17.3 us -> 6.61 us  [gradients(): pl.pallas_call(grad_kernel, grid_spec=grid_spec, out_shape=[jax.ShapeDtyp...]
    pallas_call x3, Pallas kernels: 15.9 us -> 7.78 us  [forward(): pl.pallas_call(functools.partial(forward_kernel, begin), grid=(blocks,),...]
    unnamed x12 -> x20, local copies, waits for them, and re-layouts: 0.79 us -> 8.77 us
    ppermute x11, waiting for transfers between devices: 22.2 us -> 28.4 us  [exchange(): return lax.ppermute(value, 'dp', pairs)]
    pallas_call x2, Pallas kernels: 10.5 us -> 4.44 us  [input_gradients(): pl.pallas_call(input_kernel, grid=(cells // rows,), in_specs=[whole(enc.s...]
    add x1, other arithmetic: 1.51 us -> 0.19 us  [on_device(): acc = keep + got[:width].astype(F32)]
  transfers between devices with their start and end apart: 11 -> 11, of which waited for: 5 -> 9; matrix products, arithmetic and copies ran while one was open for 6% -> 4% of each run, Pallas kernels for 28% -> 16%
where the time goes in v3:
time: 79.2 us; the launch traced here: 78.7 us
  waiting for transfers between devices  28.4 us (36%)
  Pallas kernels  18.8 us (24%)
  starting transfers between devices  12.2 us (15%)
  local copies, waits for them, and re-layouts  10.6 us (13%)
  other arithmetic  5.86 us (7%)
  between operations  2.85 us (4%)
    ppermute x11, waiting for transfers between devices, exchange(): return lax.ppermute(value, 'dp', pairs)  28.4 us
    ppermute x11, starting transfers between devices, exchange(): return lax.ppermute(value, 'dp', pairs)  12.2 us
    unnamed x20, local copies, waits for them, and re-layouts  8.77 us
    pallas_call x3, Pallas kernels, forward(): pl.pallas_call(functools.partial(forward_kernel, begin), grid=(blocks,),...  7.78 us
    pallas_call x1, Pallas kernels, gradients(): pl.pallas_call(grad_kernel, grid_spec=grid_spec, out_shape=[jax.ShapeDtyp...  6.61 us
    pallas_call x2, Pallas kernels, input_gradients(): pl.pallas_call(input_kernel, grid=(cells // rows,), in_specs=[whole(enc.s...  4.44 us
    convert_element_type x1, other arithmetic, on_device(): grad_weight = jnp.where(core == 0, jnp.concatenate([have, other], axis=1)...  1.86 us
  transfers between devices with their start and end apart: 11, of which 9 were waited for; matrix products, arithmetic and copies ran while one was open for 4% of the time, Pallas kernels for 16%

profile of v3, /device:TPU:0, one launch (start us, length us, event | category | flops | bytes accessed | tf_op | source)
XLA Modules:
  0.0 78.7 jit_solution(4610621546606722682)
XLA Ops:
  1.1 1.2 %dynamic_slice.4 = s32[1]{0:T(128)} dynamic-slice(s32[16]{0:T(128)} %param.10, s32[]{:T(128)S(6)} %select_n.70), dynamic_slice_sizes={1} | dynamic-slice | bytes 12 | tf_op jit(solution)/shard_map/jit(dynamic_index_in_dim)/dynamic_slice | solution.py:359
  3.8 0.7 pad_maximum_fusion.6
  4.5 2.6 %collective-permute-start.1 = (bf16[2,3,2048]{2,1,0:T(4,128)(2,1)S(1)}, bf16[2,3,2048]{2,1,0:T(4,128)(2,1)S(1)}, u32[]{:S(2)}, u32[]{:S(2)}) collective-permute-start(bf16[2,3,2048]{2,1,0:T(4,128)(2,1)S(1)} %pad_maximum_fusion.6), channel_id=1, source_target_pairs={{0,2},{1,3},{2,0},{3,1},{4,6},{5,7},{6,4},{7,5},{8,10},{9,11},{10,... | collective-permute-start | bytes 73736 | tf_op jit(solution)/shard_map/ppermute | solution.py:339
  7.1 1.3 %copy-done = bf16[640,1024]{1,0:T(8,128)(2,1)S(1)} copy-done((bf16[640,1024]{1,0:T(8,128)(2,1)S(1)}, bf16[640,1024]{1,0:T(8,128)(2,1)}, u32[]{:S(2)}) %copy-start) | copy-done | bytes 1310744
  8.4 0.9 %copy-done.4 = bf16[1,64,640]{2,1,0:T(8,128)(2,1)S(1)} copy-done((bf16[1,64,640]{2,1,0:T(8,128)(2,1)S(1)}, bf16[1,64,640]{2,1,0:T(8,128)(2,1)}, u32[]{:S(2)}) %copy-start.4) | copy-done | bytes 81944
  9.3 0.8 copy-done.6
  10.1 0.7 copy-done.8
  10.8 0.7 copy-done.9
  11.4 1.9 %shard_map.128 = (f32[2048,1024]{1,0:T(8,128)S(1)}, f32[8,2048]{1,0:T(8,128)S(1)}, bf16[640,2048]{1,0:T(8,128)(2,1)S(1)}) custom-call(s32[1]{0:T(128)S(6)} %copy.27.tlen_ref, s32[1,31]{1,0:T(1,128)S(1)} %copy-done.9, bf16[64,640]{1,0:T(8,128)(2,1)S(1)} %bitcast.17, bf16[32,640]{1,0:T(8,128)(2,1)S(1)} %bitcast.20, bf16[640,1024]{1,0:T(8,128)(2,1)S(1)} %copy-done, ...), custom_call_target="tpu_custom_call" | custom-call | flops 671088640 | bytes 4194304 | tf_op jit(solution)/shard_map/pallas_call | solution.py:222
  14.1 1.6 %collective-permute-start.2 = (bf16[4,3,2048]{2,1,0:T(4,128)(2,1)S(1)}, bf16[4,3,2048]{2,1,0:T(4,128)(2,1)S(1)}, u32[]{:S(2)}, u32[]{:S(2)}) collective-permute-start(bf16[4,3,2048]{2,1,0:T(4,128)(2,1)S(1)} %pad_maximum_fusion.5), channel_id=1, source_target_pairs={{0,4},{1,5},{2,6},{3,7},{4,0},{5,1},{6,2},{7,3},{8,12},{9,13},{10,... | collective-permute-start | bytes 147464 | tf_op jit(solution)/shard_map/ppermute | solution.py:339
  15.7 1.9 %shard_map.129 = (f32[2048,1024]{1,0:T(8,128)S(1)}, f32[8,2048]{1,0:T(8,128)S(1)}, bf16[640,2048]{1,0:T(8,128)(2,1)S(1)}) custom-call(s32[1]{0:T(128)S(6)} %copy.27.tlen_ref, s32[1,31]{1,0:T(1,128)S(1)} %copy-done.9, bf16[64,640]{1,0:T(8,128)(2,1)S(1)} %bitcast.18, ...), custom_call_target="tpu_custom_call", output_to_operand_aliasing={{0}: (6, {}), {1}: (7, {}), {2}: (8, {})} | custom-call | flops 671088640 | bytes 4194304 | tf_op jit(solution)/shard_map/pallas_call | solution.py:222
  17.7 0.7 collective-permute-done.2
  18.5 2.6 %collective-permute-start.3 = (bf16[8,3,2048]{2,1,0:T(4,128)(2,1)S(1)}, bf16[8,3,2048]{2,1,0:T(4,128)(2,1)S(1)}, u32[]{:S(2)}, u32[]{:S(2)}) collective-permute-start(bf16[8,3,2048]{2,1,0:T(4,128)(2,1)S(1)} %pad_maximum_fusion.4.qa_ref), channel_id=1, source_target_pairs={{0,8},{1,9},{2,10},{3,11},{4,12},{5,13},{6,14},{7,15},{8,0},{9,1},... | collective-permute-start | bytes 294920 | tf_op jit(solution)/shard_map/ppermute | solution.py:339
  21.2 3.9 %shard_map.130 = (f32[2048,1024]{1,0:T(8,128)S(1)}, f32[8,2048]{1,0:T(8,128)S(1)}, bf16[640,2048]{1,0:T(8,128)(2,1)S(1)}) custom-call(s32[1]{0:T(128)S(6)} %copy.27.tlen_ref, s32[1,31]{1,0:T(1,128)S(1)} %copy-done.9, bf16[64,640]{1,0:T(8,128)(2,1)S(1)} %bitcast.19, ...), custom_call_target="tpu_custom_call", output_to_operand_aliasing={{0}: (6, {}), {1}: (7, {}), {2}: (8, {})} | custom-call | flops 1342177280 | bytes 8388608 | tf_op jit(solution)/shard_map/pallas_call | solution.py:222
  25.1 1.8 %collective-permute-done.3.qb_ref = bf16[8,3,2048]{2,1,0:T(4,128)(2,1)S(1)} collective-permute-done((bf16[8,3,2048]{2,1,0:T(4,128)(2,1)S(1)}, bf16[8,3,2048]{2,1,0:T(4,128)(2,1)S(1)}, u32[]{:S(2)}, u32[]{:S(2)}) %collective-permute-start.3) | collective-permute-done | bytes 98336 | tf_op jit(solution)/shard_map/ppermute | solution.py:339
  26.9 6.6 %shard_map.131 = (bf16[2048,1024]{1,0:T(8,128)(2,1)S(1)}, f32[8,128]{1,0:T(8,128)S(1)}, bf16[656,512]{1,0:T(8,128)(2,1)S(1)}, f32[640,512]{1,0:T(8,128)S(1)}, f32[1,512]{1,0:T(1,128)S(1)}) custom-call(s32[3]{0:T(128)S(1)} %pad_add_fusion.pick_ref, s32[1]{0:T(128)S(6)} %copy.26.flen_ref, s32[1]{0:T(128)S(6)} %copy.27.tlen_ref, s32[1,31]{1,0:T(1,128)S(1)} %copy-done.9, ...), custom_call_target="tpu_custom_call" | custom-call | flops 2684354560 | bytes 16777216 | tf_op jit(solution)/shard_map/pallas_call | solution.py:279
  33.5 2.0 %copy-done.2 = bf16[2048,1024]{1,0:T(8,128)(2,1)} copy-done((bf16[2048,1024]{1,0:T(8,128)(2,1)}, bf16[2048,1024]{1,0:T(8,128)(2,1)S(1)}, u32[]{:S(2)}) %copy-start.2) | copy-done | bytes 4194328
  35.5 2.1 %collective-permute-done.4 = bf16[656,512]{1,0:T(8,128)(2,1)S(1)} collective-permute-done((bf16[656,512]{1,0:T(8,128)(2,1)S(1)}, bf16[656,512]{1,0:T(8,128)(2,1)S(1)}, u32[]{:S(2)}, u32[]{:S(2)}) %collective-permute-start.4) | collective-permute-done | bytes 671776 | tf_op jit(solution)/shard_map/ppermute | solution.py:339
  38.0 0.9 %collective-permute-start.5 = (bf16[336,512]{1,0:T(8,128)(2,1)S(1)}, bf16[336,512]{1,0:T(8,128)(2,1)S(1)}, u32[]{:S(2)}, u32[]{:S(2)}) collective-permute-start(bf16[336,512]{1,0:T(8,128)(2,1)S(1)} %pad_maximum_fusion.1), channel_id=1, source_target_pairs={{0,2},{1,5},{2,0},{3,7},{4,6},{5,1},{6,4},{7,3},{8,10},{9,13},{10,... | collective-permute-start | bytes 1032200 | tf_op jit(solution)/shard_map/ppermute | solution.py:339
  39.2 2.2 %copy-done.3 = bf16[2048,1024]{1,0:T(8,128)(2,1)S(1)} copy-done((bf16[2048,1024]{1,0:T(8,128)(2,1)S(1)}, bf16[2048,1024]{1,0:T(8,128)(2,1)}, u32[]{:S(2)}) %copy-start.3) | copy-done | bytes 4194328
  41.4 2.2 %shard_map.132 = (bf16[32,640]{1,0:T(8,128)(2,1)S(1)}, f32[32,640]{1,0:T(8,128)S(1)}) custom-call(bf16[32,640]{1,0:T(8,128)(2,1)S(1)} %get-tuple-element.86.enc_ref, bf16[32,640]{1,0:T(8,128)(2,1)S(1)} %bitcast.23, bf16[2048,1024]{1,0:T(8,128)(2,1)S(1)} %copy-done.3, bf16[640,1024]{1,0:T(8,128)(2,1)S(1)} %copy-done.1, f32[32,640]{1,0:T(8,128)S(1)} %broadcast_in_dim.9.base_ref), custom_call_target="tpu_custom_call" | custom-call | flops 1342177280 | bytes 4194304 | tf_op jit(solution)/shard_map/pallas_call | solution.py:299
  43.6 1.7 %collective-permute-done.5 = bf16[336,512]{1,0:T(8,128)(2,1)S(1)} collective-permute-done((bf16[336,512]{1,0:T(8,128)(2,1)S(1)}, bf16[336,512]{1,0:T(8,128)(2,1)S(1)}, u32[]{:S(2)}, u32[]{:S(2)}) %collective-permute-start.5) | collective-permute-done | bytes 344096 | tf_op jit(solution)/shard_map/ppermute | solution.py:339
  45.5 0.7 collective-permute-start.6
  46.3 2.2 %shard_map.133 = (bf16[32,640]{1,0:T(8,128)(2,1)S(1)}, f32[32,640]{1,0:T(8,128)S(1)}) custom-call(bf16[32,640]{1,0:T(8,128)(2,1)S(1)} %get-tuple-element.85.enc_ref, bf16[32,640]{1,0:T(8,128)(2,1)S(1)} %bitcast.24, bf16[2048,1024]{1,0:T(8,128)(2,1)S(1)} %copy-done.3, bf16[640,1024]{1,0:T(8,128)(2,1)S(1)} %copy-done.1, f32[32,640]{1,0:T(8,128)S(1)} %get-tuple-element.70.base_ref), custom_call_target="tpu_custom_call" | custom-call | flops 1342177280 | bytes 4194304 | tf_op jit(solution)/shard_map/pallas_call | solution.py:299
  48.5 2.6 %collective-permute-done.6 = bf16[176,512]{1,0:T(8,128)(2,1)S(1)} collective-permute-done((bf16[176,512]{1,0:T(8,128)(2,1)S(1)}, bf16[176,512]{1,0:T(8,128)(2,1)S(1)}, u32[]{:S(2)}, u32[]{:S(2)}) %collective-permute-start.6) | collective-permute-done | bytes 180256 | tf_op jit(solution)/shard_map/ppermute | solution.py:339
  51.2 2.1 %collective-permute-start.7 = (bf16[176,512]{1,0:T(8,128)(2,1)S(1)}, bf16[176,512]{1,0:T(8,128)(2,1)S(1)}, u32[]{:S(2)}, u32[]{:S(2)}) collective-permute-start(bf16[176,512]{1,0:T(8,128)(2,1)S(1)} %pad_maximum_fusion.2), channel_id=1, source_target_pairs={{0,8},{1,9},{2,10},{3,11},{4,12},{5,13},{6,14},{7,15},{8,0},{9,1},... | collective-permute-start | bytes 540680 | tf_op jit(solution)/shard_map/ppermute | solution.py:339
  53.3 7.6 %collective-permute-done.7 = bf16[176,512]{1,0:T(8,128)(2,1)S(1)} collective-permute-done((bf16[176,512]{1,0:T(8,128)(2,1)S(1)}, bf16[176,512]{1,0:T(8,128)(2,1)S(1)}, u32[]{:S(2)}, u32[]{:S(2)}) %collective-permute-start.7) | collective-permute-done | bytes 180256 | tf_op jit(solution)/shard_map/ppermute | solution.py:339
  61.2 5.2 %collective-permute-done.8 = bf16[160,512]{1,0:T(8,128)(2,1)S(1)} collective-permute-done((bf16[160,512]{1,0:T(8,128)(2,1)S(1)}, bf16[160,512]{1,0:T(8,128)(2,1)S(1)}, u32[]{:S(2)}, u32[]{:S(2)}) %collective-permute-start.8) | collective-permute-done | bytes 163872 | tf_op jit(solution)/shard_map/ppermute | solution.py:339
  66.5 0.9 %collective-permute-start.9 = (bf16[320,512]{1,0:T(8,128)(2,1)S(1)}, bf16[320,512]{1,0:T(8,128)(2,1)S(1)}, u32[]{:S(2)}, u32[]{:S(2)}) collective-permute-start(bf16[320,512]{1,0:T(8,128)(2,1)S(1)} %maximum_select_fusion.2), channel_id=1, source_target_pairs={{0,2},{1,5},{2,0},{3,7},{4,6},{5,1},{6,4},{7,3},{8,10},{9,13},{10,... | collective-permute-start | bytes 983048 | tf_op jit(solution)/shard_map/ppermute | solution.py:339
  67.5 6.2 %collective-permute-done.9 = bf16[320,512]{1,0:T(8,128)(2,1)S(1)} collective-permute-done((bf16[320,512]{1,0:T(8,128)(2,1)S(1)}, bf16[320,512]{1,0:T(8,128)(2,1)S(1)}, u32[]{:S(2)}, u32[]{:S(2)}) %collective-permute-start.9) | collective-permute-done | bytes 327712 | tf_op jit(solution)/shard_map/ppermute | solution.py:339
  74.6 0.6 maximum_bitcast_fusion
  76.2 1.9 %fusion = f32[640,1024]{1,0:T(8,128)} fusion(bf16[640,512]{1,0:T(8,128)(2,1)S(1)} %slice.121, bf16[640,512]{1,0:T(8,128)(2,1)S(1)} %maximum_select_fusion.1, pred[]{:T(512)S(6)} %eq.2), kind=kLoop, calls=%fused_computation.1 | loop fusion | flops 6553600 | bytes 3932161 | tf_op jit(solution)/shard_map/convert_element_type | solution.py:419
  (51 shorter events, 4.6 us)
Async XLA Ops:
  0.6 3.1 %collective-permute-start = (bf16[1,3,2048]{2,1,0:T(4,128)(2,1)}, bf16[1,3,2048]{2,1,0:T(4,128)(2,1)S(1)}, u32[]{:S(2)}, u32[]{:S(2)}) collective-permute-start(bf16[1,3,2048]{2,1,0:T(4,128)(2,1)} %param.9), channel_id=1, source_target_pairs={{0,1},{1,0},{2,3},{3,2},{4,5},{5,4},{6,7},{7,6},{8,9},{9,8},{10,11... | collective-permute-start | bytes 36872 | tf_op jit(solution)/shard_map/ppermute | solution.py:339
  4.5 9.5 %collective-permute-start.1 = (bf16[2,3,2048]{2,1,0:T(4,128)(2,1)S(1)}, bf16[2,3,2048]{2,1,0:T(4,128)(2,1)S(1)}, u32[]{:S(2)}, u32[]{:S(2)}) collective-permute-start(bf16[2,3,2048]{2,1,0:T(4,128)(2,1)S(1)} %pad_maximum_fusion.6), channel_id=1, source_target_pairs={{0,2},{1,3},{2,0},{3,1},{4,6},{5,7},{6,4},{7,5},{8,10},{9,11},{10,... | collective-permute-start | bytes 73736 | tf_op jit(solution)/shard_map/ppermute | solution.py:339
  7.1 1.3 %copy-start = (bf16[640,1024]{1,0:T(8,128)(2,1)S(1)}, bf16[640,1024]{1,0:T(8,128)(2,1)}, u32[]{:S(2)}) copy-start(bf16[640,1024]{1,0:T(8,128)(2,1)} %w_ref.9) | copy-start | bytes 3932164
  8.4 0.9 %copy-start.4 = (bf16[1,64,640]{2,1,0:T(8,128)(2,1)S(1)}, bf16[1,64,640]{2,1,0:T(8,128)(2,1)}, u32[]{:S(2)}) copy-start(bf16[1,64,640]{2,1,0:T(8,128)(2,1)} %param.11) | copy-start | bytes 245764
  9.3 0.8 copy-start.6
  10.1 0.7 copy-start.8
  10.8 0.7 copy-start.9
  14.1 4.3 %collective-permute-start.2 = (bf16[4,3,2048]{2,1,0:T(4,128)(2,1)S(1)}, bf16[4,3,2048]{2,1,0:T(4,128)(2,1)S(1)}, u32[]{:S(2)}, u32[]{:S(2)}) collective-permute-start(bf16[4,3,2048]{2,1,0:T(4,128)(2,1)S(1)} %pad_maximum_fusion.5), channel_id=1, source_target_pairs={{0,4},{1,5},{2,6},{3,7},{4,0},{5,1},{6,2},{7,3},{8,12},{9,13},{10,... | collective-permute-start | bytes 147464 | tf_op jit(solution)/shard_map/ppermute | solution.py:339
  18.5 8.4 %collective-permute-start.3 = (bf16[8,3,2048]{2,1,0:T(4,128)(2,1)S(1)}, bf16[8,3,2048]{2,1,0:T(4,128)(2,1)S(1)}, u32[]{:S(2)}, u32[]{:S(2)}) collective-permute-start(bf16[8,3,2048]{2,1,0:T(4,128)(2,1)S(1)} %pad_maximum_fusion.4.qa_ref), channel_id=1, source_target_pairs={{0,8},{1,9},{2,10},{3,11},{4,12},{5,13},{6,14},{7,15},{8,0},{9,1},... | collective-permute-start | bytes 294920 | tf_op jit(solution)/shard_map/ppermute | solution.py:339
  33.5 2.0 %copy-start.2 = (bf16[2048,1024]{1,0:T(8,128)(2,1)}, bf16[2048,1024]{1,0:T(8,128)(2,1)S(1)}, u32[]{:S(2)}) copy-start(bf16[2048,1024]{1,0:T(8,128)(2,1)S(1)} %get-tuple-element.69.d_ref) | copy-start | bytes 12582916
  35.5 2.1 %collective-permute-start.4 = (bf16[656,512]{1,0:T(8,128)(2,1)S(1)}, bf16[656,512]{1,0:T(8,128)(2,1)S(1)}, u32[]{:S(2)}, u32[]{:S(2)}) collective-permute-start(bf16[656,512]{1,0:T(8,128)(2,1)S(1)} %get-tuple-element.60), channel_id=1, source_target_pairs={{0,1},{1,0},{2,3},{3,2},{4,5},{5,4},{6,7},{7,6},{8,9},{9,8},{10,11... | collective-permute-start | bytes 2015240 | tf_op jit(solution)/shard_map/ppermute | solution.py:339
  37.8 1.0 %copy-start.5 = (bf16[1,64,640]{2,1,0:T(8,128)(2,1)S(1)}, bf16[1,64,640]{2,1,0:T(8,128)(2,1)}, u32[]{:S(2)}) copy-start(bf16[1,64,640]{2,1,0:T(8,128)(2,1)} %param.11) | copy-start | bytes 245764
  37.8 1.4 %copy-start.1 = (bf16[640,1024]{1,0:T(8,128)(2,1)S(1)}, bf16[640,1024]{1,0:T(8,128)(2,1)}, u32[]{:S(2)}) copy-start(bf16[640,1024]{1,0:T(8,128)(2,1)} %w_ref.9) | copy-start | bytes 3932164
  37.8 1.3 %copy-start.7 = (bf16[1,32,640]{2,1,0:T(8,128)(2,1)S(1)}, bf16[1,32,640]{2,1,0:T(8,128)(2,1)}, u32[]{:S(2)}) copy-start(bf16[1,32,640]{2,1,0:T(8,128)(2,1)} %param.12) | copy-start | bytes 122884
  38.0 7.3 %collective-permute-start.5 = (bf16[336,512]{1,0:T(8,128)(2,1)S(1)}, bf16[336,512]{1,0:T(8,128)(2,1)S(1)}, u32[]{:S(2)}, u32[]{:S(2)}) collective-permute-start(bf16[336,512]{1,0:T(8,128)(2,1)S(1)} %pad_maximum_fusion.1), channel_id=1, source_target_pairs={{0,2},{1,5},{2,0},{3,7},{4,6},{5,1},{6,4},{7,3},{8,10},{9,13},{10,... | collective-permute-start | bytes 1032200 | tf_op jit(solution)/shard_map/ppermute | solution.py:339
  39.2 2.2 %copy-start.3 = (bf16[2048,1024]{1,0:T(8,128)(2,1)S(1)}, bf16[2048,1024]{1,0:T(8,128)(2,1)}, u32[]{:S(2)}) copy-start(bf16[2048,1024]{1,0:T(8,128)(2,1)} %copy-done.2) | copy-start | bytes 12582916
  45.5 5.6 %collective-permute-start.6 = (bf16[176,512]{1,0:T(8,128)(2,1)S(1)}, bf16[176,512]{1,0:T(8,128)(2,1)S(1)}, u32[]{:S(2)}, u32[]{:S(2)}) collective-permute-start(bf16[176,512]{1,0:T(8,128)(2,1)S(1)} %pad_maximum_fusion.3), channel_id=1, source_target_pairs={{0,4},{1,3},{2,6},{3,1},{4,0},{5,7},{6,2},{7,5},{8,12},{9,11},{10,... | collective-permute-start | bytes 540680 | tf_op jit(solution)/shard_map/ppermute | solution.py:339
  51.2 9.7 %collective-permute-start.7 = (bf16[176,512]{1,0:T(8,128)(2,1)S(1)}, bf16[176,512]{1,0:T(8,128)(2,1)S(1)}, u32[]{:S(2)}, u32[]{:S(2)}) collective-permute-start(bf16[176,512]{1,0:T(8,128)(2,1)S(1)} %pad_maximum_fusion.2), channel_id=1, source_target_pairs={{0,8},{1,9},{2,10},{3,11},{4,12},{5,13},{6,14},{7,15},{8,0},{9,1},... | collective-permute-start | bytes 540680 | tf_op jit(solution)/shard_map/ppermute | solution.py:339
  61.1 5.4 %collective-permute-start.8 = (bf16[160,512]{1,0:T(8,128)(2,1)S(1)}, bf16[160,512]{1,0:T(8,128)(2,1)S(1)}, u32[]{:S(2)}, u32[]{:S(2)}) collective-permute-start(bf16[160,512]{1,0:T(8,128)(2,1)S(1)} %add_convert_fusion), channel_id=1, source_target_pairs={{0,4},{1,3},{2,6},{3,1},{4,0},{5,7},{6,2},{7,5},{8,12},{9,11},{10,... | collective-permute-start | bytes 491528 | tf_op jit(solution)/shard_map/ppermute | solution.py:339
  66.5 7.1 %collective-permute-start.9 = (bf16[320,512]{1,0:T(8,128)(2,1)S(1)}, bf16[320,512]{1,0:T(8,128)(2,1)S(1)}, u32[]{:S(2)}, u32[]{:S(2)}) collective-permute-start(bf16[320,512]{1,0:T(8,128)(2,1)S(1)} %maximum_select_fusion.2), channel_id=1, source_target_pairs={{0,2},{1,5},{2,0},{3,7},{4,6},{5,1},{6,4},{7,3},{8,10},{9,13},{10,... | collective-permute-start | bytes 983048 | tf_op jit(solution)/shard_map/ppermute | solution.py:339
  74.0 2.2 %collective-permute-start.10 = (bf16[656,512]{1,0:T(8,128)(2,1)S(1)}, bf16[656,512]{1,0:T(8,128)(2,1)S(1)}, u32[]{:S(2)}, u32[]{:S(2)}) collective-permute-start(bf16[656,512]{1,0:T(8,128)(2,1)S(1)} %pad_maximum_fusion), channel_id=1, source_target_pairs={{0,1},{1,0},{2,3},{3,2},{4,5},{5,4},{6,7},{7,6},{8,9},{9,8},{10,11... | collective-permute-start | bytes 2015240 | tf_op jit(solution)/shard_map/ppermute | solution.py:339

commit v4 on v3

--- a/solution.py
+++ b/solution.py
@@ -11,12 +11,11 @@
 BF16 = jnp.bfloat16
 LANES = 128
 EXTRA = 16
-VMEM_LIMIT = 24 * 1024 * 1024
-
-
-def params():
+
+
+def params(mib):
     return pltpu.CompilerParams(
-        dimension_semantics=("arbitrary",), vmem_limit_bytes=VMEM_LIMIT
+        dimension_semantics=("arbitrary",), vmem_limit_bytes=mib * 1024 * 1024
     )
 
 
@@ -30,6 +29,41 @@
     column = jnp.where(token < token_len, column, -1.0).astype(jnp.int32)
     whole = jnp.broadcast_to(column[None], (reps, tok_slots, 1))
     return whole.reshape(reps * tok_slots, 1)
+
+
+def stage_kernel(assignment_ref, *refs):
+    count = (len(refs) - 2) // 2
+    sources, targets, pick_ref, sems = refs[:count], refs[count : 2 * count], refs[-2], refs[-1]
+    copies = [
+        pltpu.make_async_copy(source, target, sems.at[k])
+        for k, (source, target) in enumerate(zip(sources, targets))
+    ]
+    for copy in copies:
+        copy.start()
+    own = lax.axis_index("dp")
+    pick_ref[0] = assignment_ref[own] ^ own
+    pick_ref[1] = assignment_ref.shape[0] // 2
+    pick_ref[2] = own & 1
+    for copy in copies:
+        copy.wait()
+
+
+def stage(assignment, *arrays):
+    anywhere = pl.BlockSpec(memory_space=pl.ANY)
+    smem = pl.BlockSpec(memory_space=pltpu.SMEM)
+    return pl.pallas_call(
+        stage_kernel,
+        in_specs=[smem] + [anywhere] * len(arrays),
+        out_specs=[anywhere] * len(arrays) + [smem],
+        out_shape=[jax.ShapeDtypeStruct(x.shape, x.dtype) for x in arrays]
+        + [jax.ShapeDtypeStruct((3,), jnp.int32)],
+        scratch_shapes=[pltpu.SemaphoreType.DMA((len(arrays),))],
+        compiler_params=pltpu.CompilerParams(vmem_limit_bytes=4 * 1024 * 1024),
+    )(assignment, *[pltpu.with_memory_space_constraint(x, pltpu.HBM) for x in arrays])
+
+
+def in_vmem(x):
+    return x
 
 
 SUB = 256
@@ -96,7 +130,7 @@
 
 def grad_kernel(
     pick_ref, flen_ref, tlen_ref, labels_ref, qa_ref, qb_ref, e_ref, st_ref, jt_ref,
-    d_ref, loss_ref, send_ref, keep_ref, keepb_ref, d_scr, gb_scr, loss_scr, target_scr,
+    d_ref, loss_ref, send_ref, keep_ref, d_scr, gb_scr, loss_scr, target_scr,
 ):
     step = pl.program_id(0)
     steps = pl.num_programs(0)
@@ -160,19 +194,19 @@
 
     @pl.when(step == steps - 1)
     def _():
-        loss_ref[...] = jnp.broadcast_to(jnp.sum(loss_scr[...], axis=1, keepdims=True), loss_ref.shape)
+        loss_ref[...] = jnp.sum(loss_scr[...], axis=1, keepdims=True)
         part = vocab // 2
         core = pick_ref[2]
         col = pl.multiple_of((1 - core) * part, part)
         dw = jnp.dot(jt_ref[...], d_scr[:, pl.ds(col, part)], preferred_element_type=F32)
         send_ref[:width, :] = dw.astype(BF16)
         col = pl.multiple_of(core * part, part)
-        keep_ref[...] = jnp.dot(jt_ref[...], d_scr[:, pl.ds(col, part)], preferred_element_type=F32)
+        keep_ref[:width, :] = jnp.dot(jt_ref[...], d_scr[:, pl.ds(col, part)], preferred_element_type=F32)
         bias = jnp.sum(gb_scr[...], axis=0, keepdims=True)
         first, second = bias[:, :part], bias[:, part:]
         mine = jnp.where(core == 0, first, second)
         other = jnp.where(core == 0, second, first)
-        keepb_ref[...] = mine
+        keep_ref[width:, :] = jnp.broadcast_to(mine, (EXTRA, part))
         high = other.astype(BF16)
         low = (other - high.astype(F32)).astype(BF16)
         place = lax.broadcasted_iota(jnp.int32, (EXTRA, part), 0)
@@ -180,7 +214,8 @@
         send_ref[width:, :] = packed.astype(BF16)
 
 
-def input_kernel(enc_ref, pred_ref, d_ref, w_ref, base_ref, ge_ref, gp_ref, enc_scr, ge_scr):
+def input_kernel(begin, last, enc_ref, pred_ref, d_ref, w_ref, *refs):
+    ge_ref, gp_ref, enc_scr, ge_scr, gp_scr = refs[-5:]
     step = pl.program_id(0)
     steps = pl.num_programs(0)
     rows = d_ref.shape[0]
@@ -190,21 +225,66 @@
     @pl.when(step == 0)
     def _():
         enc_scr[...] = enc_ref[...].astype(F32)
-        gp_ref[...] = base_ref[...]
+        gp_scr[...] = jnp.zeros_like(gp_scr) if begin == 0 else refs[0][...]
 
     first = pl.multiple_of(step * block_frames, block_frames)
     d_hidden = lax.dot_general(
         d_ref[...], w_ref[...], (((1,), (1,)), ((), ())), preferred_element_type=F32
     )
-    enc = enc_scr[pl.ds(first, block_frames), :]
+    enc = enc_scr[pl.ds(begin * block_frames + first, block_frames), :]
     act = jnp.tanh(enc[:, None, :] + pred_ref[...].astype(F32)[None, :, :])
     d_pre = d_hidden.reshape(block_frames, tok_slots, width) * (1.0 - act * act)
     ge_scr[pl.ds(first, block_frames), :] = jnp.sum(d_pre, axis=1)
-    gp_ref[...] += jnp.sum(d_pre, axis=0)
+    gp_scr[...] += jnp.sum(d_pre, axis=0)
 
     @pl.when(step == steps - 1)
     def _():
         ge_ref[...] = ge_scr[...].astype(BF16)
+        gp_ref[...] = gp_scr[...].astype(gp_ref.dtype)
+
+
+def final_kernel(with_bias, core_ref, have_ref, *refs):
+    out_ref = refs[-2] if with_bias else refs[-1]
+    out_ref[...] = have_ref[...].astype(F32)
+    if with_bias:
+        mine_ref, rows_ref, bias_ref = refs[1], refs[2], refs[-1]
+        mine = mine_ref[...]
+        other = rows_ref[0:1, :].astype(F32) + rows_ref[1:2, :].astype(F32)
+        core = core_ref[2]
+        bias_ref[...] = jnp.concatenate(
+            [jnp.where(core == 0, mine, other), jnp.where(core == 0, other, mine)], axis=1
+        )
+
+
+def widen(pick, have, width, before=(), mine=None):
+    part = have.shape[1]
+    rows = width // 2
+    with_bias = mine is not None
+    if with_bias:
+        place = lambda i, pick: (i, 1 - pick[2])
+    else:
+        place = lambda i, pick: (i, pick[2])
+    in_specs = [pl.BlockSpec((rows, part), lambda i, pick: (i, 0))]
+    out_specs = [pl.BlockSpec((rows, part), place)]
+    out_shape = [jax.ShapeDtypeStruct((width, 2 * part), F32)]
+    extra = ()
+    if with_bias:
+        in_specs += [
+            pl.BlockSpec(memory_space=pl.ANY), whole(mine.shape),
+            pl.BlockSpec((EXTRA, part), lambda i, pick: (width // EXTRA, 0)),
+        ]
+        out_specs += [whole((1, 2 * part))]
+        out_shape += [jax.ShapeDtypeStruct((1, 2 * part), F32)]
+        extra = (*before, mine, have)
+    return pl.pallas_call(
+        functools.partial(final_kernel, with_bias),
+        grid_spec=pltpu.PrefetchScalarGridSpec(
+            num_scalar_prefetch=1, grid=(width // rows,), in_specs=in_specs, out_specs=out_specs
+        ),
+        out_shape=out_shape,
+        input_output_aliases={2: 0} if with_bias else {},
+        compiler_params=params(8),
+    )(pick, have, *extra)
 
 
 def whole(shape):
@@ -238,12 +318,8 @@
         ],
         scratch_shapes=[pltpu.VMEM((frames, width), F32), pltpu.VMEM((2, SUB, vocab), F32)],
         input_output_aliases={6 + k: k for k in range(len(before))},
-        compiler_params=params(),
-        cost_estimate=pl.CostEstimate(
-            flops=2 * blocks * rows * width * vocab, bytes_accessed=blocks * rows * vocab * 8,
-            transcendentals=blocks * rows * (width + vocab),
-        ),
-    )(tlen, labels, enc, pred, w, bias, *before)
+        compiler_params=params(16),
+    )(tlen, in_vmem(labels), in_vmem(enc), in_vmem(pred), in_vmem(w), in_vmem(bias), *before)
 
 
 def gradients(pick, flen, tlen, labels, qa, qb, e, st, jt, rows):
@@ -264,10 +340,9 @@
         ],
         out_specs=[
             pl.BlockSpec((rows, vocab), lambda i, pick: (i, 0)),
-            whole((8, LANES)),
+            whole((1, 1)),
             whole((width + EXTRA, part)),
-            whole((width, part)),
-            whole((1, part)),
+            whole((width + EXTRA, part)),
         ],
         scratch_shapes=[
             pltpu.VMEM((cells, vocab), BF16),
@@ -280,41 +355,39 @@
         grad_kernel,
         grid_spec=grid_spec,
         out_shape=[
-            jax.ShapeDtypeStruct((cells, vocab), BF16),
-            jax.ShapeDtypeStruct((8, LANES), F32),
+            pltpu.HBM((cells, vocab), BF16),
+            jax.ShapeDtypeStruct((1, 1), F32),
             jax.ShapeDtypeStruct((width + EXTRA, part), BF16),
-            jax.ShapeDtypeStruct((width, part), F32),
-            jax.ShapeDtypeStruct((1, part), F32),
-        ],
-        compiler_params=params(),
-        cost_estimate=pl.CostEstimate(
-            flops=2 * cells * width * vocab, bytes_accessed=16 * 1024 * 1024, transcendentals=cells * 8
-        ),
-    )(pick, flen, tlen, labels, qa, qb, e, st, jt)
-
-
-def input_gradients(enc, pred, d_low, w, base, rows, begin):
+            jax.ShapeDtypeStruct((width + EXTRA, part), F32),
+        ],
+        compiler_params=params(20),
+    )(pick, flen, tlen, in_vmem(labels), qa, qb, e, st, jt)
+
+
+def input_gradients(enc, pred, d_low, w, rows, begin, last, before):
+    frames, width = enc.shape
     vocab = d_low.shape[1]
-    cells = enc.shape[0] * pred.shape[0]
+    cells = frames // 2 * pred.shape[0]
+    half = (frames // 2, width)
+    extra = () if not before else (before[1], before[0])
     return pl.pallas_call(
-        input_kernel,
+        functools.partial(input_kernel, begin, last),
         grid=(cells // rows,),
         in_specs=[
             whole(enc.shape), whole(pred.shape),
-            pl.BlockSpec((rows, vocab), lambda i: (i + begin, 0)), whole(w.shape), whole(base.shape),
-        ],
-        out_specs=[whole(enc.shape), whole(pred.shape)],
+            pl.BlockSpec((rows, vocab), lambda i: (i + begin, 0)), whole(w.shape),
+        ] + ([whole(pred.shape), pl.BlockSpec(memory_space=pl.ANY)] if before else []),
+        out_specs=[pl.BlockSpec(half, lambda i: (1 if last else 0, 0)), whole(pred.shape)],
         out_shape=[
             jax.ShapeDtypeStruct(enc.shape, BF16),
-            jax.ShapeDtypeStruct(pred.shape, F32),
-        ],
-        scratch_shapes=[pltpu.VMEM(enc.shape, F32), pltpu.VMEM(enc.shape, F32)],
-        compiler_params=params(),
-        cost_estimate=pl.CostEstimate(
-            flops=2 * cells * w.shape[0] * vocab, bytes_accessed=cells * vocab * 4,
-            transcendentals=cells * w.shape[0],
-        ),
-    )(enc, pred, d_low, w, base)
+            jax.ShapeDtypeStruct(pred.shape, BF16 if last else F32),
+        ],
+        scratch_shapes=[
+            pltpu.VMEM(enc.shape, F32), pltpu.VMEM(half, F32), pltpu.VMEM(pred.shape, F32)
+        ],
+        input_output_aliases={5: 0} if before else {},
+        compiler_params=params(12),
+    )(in_vmem(enc), in_vmem(pred), pltpu.with_memory_space_constraint(d_low, pltpu.HBM), in_vmem(w), *extra)
 
 
 def split_two(value):
@@ -329,8 +402,8 @@
     own = lax.axis_index("dp")
     core = own & 1
     masks = [1 << k for k in range(dp.bit_length() - 1)]
-    enc, pred = encoder_out[0], predictor_out[0]
-    rows = 16 * pred.shape[0]
+    tok_slots = predictor_out.shape[1]
+    rows = 16 * tok_slots
     width, vocab = out_weight.shape
     part = vocab // 2
 
@@ -338,28 +411,29 @@
         pairs = [(k, k ^ (odd if k & 1 else even)) for k in range(dp)]
         return lax.ppermute(value, "dp", pairs)
 
-    blocks = enc.shape[0] * pred.shape[0] // rows
+    blocks = encoder_out.shape[1] * tok_slots // rows
     quarter = blocks // 4
     shares = [(0, quarter), (quarter, quarter), (2 * quarter, blocks - 2 * quarter)]
-    bias_row = out_bias.reshape(1, vocab)
     held, made = teacher_post, ()
+    staged = stage(
+        assignment, out_weight, encoder_out[0], predictor_out[0], out_bias.reshape(1, vocab), labels
+    )
     for k, mask in enumerate(masks):
         got = exchange(held, mask, mask)
         part_no = k - (len(masks) - len(shares))
         if part_no >= 0:
             begin, number = shares[part_no]
             made = tuple(forward(
-                token_lengths, labels, enc, pred, out_weight, bias_row, rows, begin, number, made
+                token_lengths, label_row, enc, pred, weight, bias_row, rows, begin, number, made
             ))
         if k < len(masks) - 1:
             held = jnp.concatenate([held, got], axis=0)
-            held, made = lax.optimization_barrier((held, made))
+            held, made, staged = lax.optimization_barrier((held, made, staged))
+            weight, enc, pred, bias_row, label_row, pick = staged
     far = got
     e, st, jt = made
-    place = lax.dynamic_index_in_dim(assignment, own, keepdims=False) ^ own
-    pick = jnp.stack([place, jnp.int32(dp // 2), core]).astype(jnp.int32)
-    d_low, loss, send, keep, bias = gradients(
-        pick, frame_lengths, token_lengths, labels, held, far, e, st, jt, rows
+    d_low, loss, send, keep = gradients(
+        pick, frame_lengths, token_lengths, label_row, held, far, e, st, jt, rows
     )
     got = exchange(send, 1, 1)
 
@@ -370,16 +444,15 @@
         filler = jnp.zeros((EXTRA - 2, part), BF16)
         return jnp.concatenate([high.astype(BF16), low.astype(BF16), filler], axis=0)
 
-    acc = keep + got[:width].astype(F32)
-    bias = bias + got_bias(got[width:])
+    acc = keep[:width] + got[:width].astype(F32)
+    bias = keep[width : width + 1] + got_bias(got[width:])
     rest = masks[1:]
     even_order = rest
     odd_order = rest[1:2] + rest[:1] + rest[2:]
     orders = list(zip(even_order, odd_order))
     sides = []
     count = width
-    frames = enc.shape[0]
-    grad_enc, grad_pred = [], jnp.zeros(pred.shape, F32)
+    done = ()
     for k, (even, odd) in enumerate(orders):
         high, low = split_two(bias)
         if k < len(orders) - 1:
@@ -394,15 +467,13 @@
             acc = lax.reduce_precision(acc, 8, 7)
         send = jnp.concatenate([send, bias_rows(high, low)], axis=0)
         if k < 2:
-            send, d_low = lax.optimization_barrier((send, d_low))
+            send, acc, d_low = lax.optimization_barrier((send, acc, d_low))
         got = exchange(send, even, odd)
         if k < 2:
-            piece = enc[k * (frames // 2) : (k + 1) * (frames // 2)]
-            grad_rows, grad_pred = input_gradients(
-                piece, pred, d_low, out_weight, grad_pred, rows, k * (blocks // 2)
+            done = input_gradients(
+                enc, pred, d_low, weight, rows, k * (blocks // 2), k == 1, done
             )
-            got, grad_rows, grad_pred = lax.optimization_barrier((got, grad_rows, grad_pred))
-            grad_enc.append(grad_rows)
+            got, done = lax.optimization_barrier((got, done))
         acc = acc + got[:count].astype(F32)
         bias = (high + low) + got_bias(got[count:])
     have = acc.astype(BF16)
@@ -413,20 +484,10 @@
         )
     high, low = split_two(bias)
     got = exchange(jnp.concatenate([have, bias_rows(high, low)], axis=0), 1, 1)
-    other = got[:width]
-    grad_weight = jnp.where(
-        core == 0, jnp.concatenate([have, other], axis=1), jnp.concatenate([other, have], axis=1)
-    ).astype(F32)
-    bias, other_bias = high + low, got_bias(got[width:])
-    grad_bias = jnp.where(
-        core == 0,
-        jnp.concatenate([bias, other_bias], axis=1),
-        jnp.concatenate([other_bias, bias], axis=1),
-    ).reshape(vocab)
-    return (
-        loss[0, 0:1], grad_weight, grad_bias, jnp.concatenate(grad_enc, axis=0)[None],
-        grad_pred.astype(BF16)[None],
-    )
+    half = widen(pick, have, width)
+    got, half = lax.optimization_barrier((got, half))
+    grad_weight, grad_bias = widen(pick, got, width, half, high + low)
+    return (loss.reshape(1), grad_weight, grad_bias.reshape(vocab), done[0][None], done[1][None])
 
 
 def solution(mesh):

time: 79.2 us -> 75 us (0.947)
  Pallas kernels: 18.8 us -> 29.7 us
  local copies, waits for them, and re-layouts: 10.6 us -> 0.66 us
  other arithmetic: 5.86 us -> 3.21 us
  waiting for transfers between devices: 28.4 us -> 26.1 us
    pallas_call x3 -> x6, Pallas kernels: 11.1 us -> 21.9 us  [the longest x2 8.12 us: input_gradients(): pl.pallas_call(functools.partial(input_kernel, begin, last), grid=(cells...]
    unnamed x20 -> x4, local copies, waits for them, and re-layouts: 8.77 us -> 0.66 us
    ppermute x11, waiting for transfers between devices: 28.4 us -> 26.1 us  [exchange(): return lax.ppermute(value, 'dp', pairs)]
    convert_element_type x1 -> x0, other arithmetic: 1.86 us -> none  [on_device(): grad_weight = jnp.where(core == 0, jnp.concatenate([have, other], axis=1)...]
    broadcast_in_dim x2 -> x0, other arithmetic: 1.27 us -> none  [the longest x1 0.64 us: on_device(): jnp.concatenate(grad_enc, axis=0)[None]]
    dynamic_slice x1 -> x0, local copies, waits for them, and re-layouts: 1.24 us -> none  [on_device(): place = lax.dynamic_index_in_dim(assignment, own, keepdims=False) ^ own]
    add x3 -> x2, other arithmetic: 0.21 us -> 1.3 us  [the longest x1 1.29 us: on_device(): acc = keep[:width] + got[:width].astype(F32)]
  transfers between devices with their start and end apart: 11 -> 11, of which waited for: 9 -> 9; matrix products, arithmetic and copies ran while one was open for 4% -> 0% of each run, Pallas kernels for 16% -> 27%
where the time goes in v4:
time: 75 us; the launch traced here: 74.7 us
  Pallas kernels  29.7 us (40%)
  waiting for transfers between devices  26.1 us (35%)
  starting transfers between devices  12.9 us (17%)
  other arithmetic  3.21 us (4%)
  between operations  2.14 us (3%)
    ppermute x11, waiting for transfers between devices, exchange(): return lax.ppermute(value, 'dp', pairs)  26.1 us
    ppermute x11, starting transfers between devices, exchange(): return lax.ppermute(value, 'dp', pairs)  12.9 us
    pallas_call x2, Pallas kernels, input_gradients(): pl.pallas_call(functools.partial(input_kernel, begin, last), grid=(cells...  8.12 us
    pallas_call x1, Pallas kernels, gradients(): pl.pallas_call(grad_kernel, grid_spec=grid_spec, out_shape=[pltpu.HBM((ce...  7.96 us
    pallas_call x3, Pallas kernels, forward(): pl.pallas_call(functools.partial(forward_kernel, begin), grid=(blocks,),...  7.78 us
    pallas_call x2, Pallas kernels, widen(): pl.pallas_call(functools.partial(final_kernel, with_bias), grid_spec=pltp...  3.32 us
    pallas_call x1, Pallas kernels, stage(): pl.pallas_call(stage_kernel, in_specs=[smem] + [anywhere] * len(arrays),...  2.5 us
  transfers between devices with their start and end apart: 11, of which 9 were waited for; matrix products, arithmetic and copies ran while one was open for 0% of the time, Pallas kernels for 27%

profile of v4, /device:TPU:0, one launch (start us, length us, event | category | flops | bytes accessed | tf_op | source)
XLA Modules:
  0.0 74.7 jit_solution(14888517207881353370)
XLA Ops:
  0.6 0.5 collective-permute-start
  1.2 0.7 copy-done
  1.8 2.5 %shard_map.128 = (bf16[640,1024]{1,0:T(8,128)(2,1)S(1)}, bf16[64,640]{1,0:T(8,128)(2,1)S(1)}, bf16[32,640]{1,0:T(8,128)(2,1)S(1)}, f32[1,1024]{1,0:T(1,128)S(1)}, s32[1,31]{1,0:T(1,128)S(1)}, /*index=5*/s32[3]{0:T(128)S(1)}) custom-call(s32[16]{0:T(128)S(1)} %copy-done, bf16[640,1024]{1,0:T(8,128)(2,1)} %refs_0_.1, bf16[64,640]{1,0:T(8,128)(2,1)} %bitcast.7, ...), custom_call_target="tpu_custom_call" | custom-call | tf_op jit(solution)/shard_map/pallas_call | solution.py:54
  4.4 2.6 %collective-permute-start.1 = (bf16[2,3,2048]{2,1,0:T(4,128)(2,1)S(1)}, bf16[2,3,2048]{2,1,0:T(4,128)(2,1)S(1)}, u32[]{:S(2)}, u32[]{:S(2)}) collective-permute-start(bf16[2,3,2048]{2,1,0:T(4,128)(2,1)S(1)} %pad_maximum_fusion.6), channel_id=1, source_target_pairs={{0,2},{1,3},{2,0},{3,1},{4,6},{5,7},{6,4},{7,5},{8,10},{9,11},{10,... | collective-permute-start | bytes 73736 | tf_op jit(solution)/shard_map/ppermute | solution.py:412
  7.6 1.9 %shard_map.129 = (f32[2048,1024]{1,0:T(8,128)S(1)}, f32[8,2048]{1,0:T(8,128)S(1)}, bf16[640,2048]{1,0:T(8,128)(2,1)S(1)}) custom-call(s32[1]{0:T(128)S(6)} %copy.31.tlen_ref, s32[1,31]{1,0:T(1,128)S(1)} %get-tuple-element.101.labels_ref, bf16[64,640]{1,0:T(8,128)(2,1)S(1)} %get-tuple-element.103.enc_ref, bf16[32,640]{1,0:T(8,128)(2,1)S(1)} %get-tuple-element.104.pred_ref, ...), custom_call_target="tpu_custom_call" | custom-call | tf_op jit(solution)/shard_map/pallas_call | solution.py:302
  9.6 1.6 %collective-permute-start.2 = (bf16[4,3,2048]{2,1,0:T(4,128)(2,1)S(1)}, bf16[4,3,2048]{2,1,0:T(4,128)(2,1)S(1)}, u32[]{:S(2)}, u32[]{:S(2)}) collective-permute-start(bf16[4,3,2048]{2,1,0:T(4,128)(2,1)S(1)} %pad_maximum_fusion.5), channel_id=1, source_target_pairs={{0,4},{1,5},{2,6},{3,7},{4,0},{5,1},{6,2},{7,3},{8,12},{9,13},{10,... | collective-permute-start | bytes 147464 | tf_op jit(solution)/shard_map/ppermute | solution.py:412
  11.2 1.9 %shard_map.130 = (f32[2048,1024]{1,0:T(8,128)S(1)}, f32[8,2048]{1,0:T(8,128)S(1)}, bf16[640,2048]{1,0:T(8,128)(2,1)S(1)}) custom-call(s32[1]{0:T(128)S(6)} %copy.31.tlen_ref, s32[1,31]{1,0:T(1,128)S(1)} %get-tuple-element.101.labels_ref, bf16[64,640]{1,0:T(8,128)(2,1)S(1)} %get-tuple-element.103.enc_ref, ...), custom_call_target="tpu_custom_call", output_to_operand_aliasing={{0}: (6, {}), {1}: (7, {}), {2}: (8, {})} | custom-call | tf_op jit(solution)/shard_map/pallas_call | solution.py:302
  13.2 0.8 %collective-permute-done.2 = bf16[4,3,2048]{2,1,0:T(4,128)(2,1)S(1)} collective-permute-done((bf16[4,3,2048]{2,1,0:T(4,128)(2,1)S(1)}, bf16[4,3,2048]{2,1,0:T(4,128)(2,1)S(1)}, u32[]{:S(2)}, u32[]{:S(2)}) %collective-permute-start.2) | collective-permute-done | bytes 49184 | tf_op jit(solution)/shard_map/ppermute | solution.py:412
  14.0 2.7 %collective-permute-start.3 = (bf16[8,3,2048]{2,1,0:T(4,128)(2,1)S(1)}, bf16[8,3,2048]{2,1,0:T(4,128)(2,1)S(1)}, u32[]{:S(2)}, u32[]{:S(2)}) collective-permute-start(bf16[8,3,2048]{2,1,0:T(4,128)(2,1)S(1)} %pad_maximum_fusion.4.qa_ref), channel_id=1, source_target_pairs={{0,8},{1,9},{2,10},{3,11},{4,12},{5,13},{6,14},{7,15},{8,0},{9,1},... | collective-permute-start | bytes 294920 | tf_op jit(solution)/shard_map/ppermute | solution.py:412
  17.3 3.9 %shard_map.131 = (f32[2048,1024]{1,0:T(8,128)S(1)}, f32[8,2048]{1,0:T(8,128)S(1)}, bf16[640,2048]{1,0:T(8,128)(2,1)S(1)}) custom-call(s32[1]{0:T(128)S(6)} %copy.31.tlen_ref, s32[1,31]{1,0:T(1,128)S(1)} %get-tuple-element.101.labels_ref, bf16[64,640]{1,0:T(8,128)(2,1)S(1)} %get-tuple-element.103.enc_ref, ...), custom_call_target="tpu_custom_call", output_to_operand_aliasing={{0}: (6, {}), {1}: (7, {}), {2}: (8, {})} | custom-call | tf_op jit(solution)/shard_map/pallas_call | solution.py:302
  21.2 1.1 %collective-permute-done.3.qb_ref = bf16[8,3,2048]{2,1,0:T(4,128)(2,1)S(1)} collective-permute-done((bf16[8,3,2048]{2,1,0:T(4,128)(2,1)S(1)}, bf16[8,3,2048]{2,1,0:T(4,128)(2,1)S(1)}, u32[]{:S(2)}, u32[]{:S(2)}) %collective-permute-start.3) | collective-permute-done | bytes 98336 | tf_op jit(solution)/shard_map/ppermute | solution.py:412
  22.4 8.0 %shard_map.132 = (bf16[2048,1024]{1,0:T(8,128)(2,1)}, f32[1,1]{1,0:T(1,128)}, bf16[656,512]{1,0:T(8,128)(2,1)S(1)}, f32[656,512]{1,0:T(8,128)S(1)}) custom-call(s32[3]{0:T(128)S(1)} %get-tuple-element.100.pick_ref.core_ref, s32[1]{0:T(128)S(6)} %copy.30.flen_ref, s32[1]{0:T(128)S(6)} %copy.31.tlen_ref, s32[1,31]{1,0:T(1,128)S(1)} %get-tuple-element.101.labels_ref, ...), custom_call_target="tpu_custom_call" | custom-call | tf_op jit(solution)/shard_map/pallas_call | solution.py:354
  30.3 2.2 %collective-permute-done.4 = bf16[656,512]{1,0:T(8,128)(2,1)} collective-permute-done((bf16[656,512]{1,0:T(8,128)(2,1)S(1)}, bf16[656,512]{1,0:T(8,128)(2,1)}, u32[]{:S(2)}, u32[]{:S(2)}) %collective-permute-start.4) | collective-permute-done | bytes 671776 | tf_op jit(solution)/shard_map/ppermute | solution.py:412
  32.6 1.3 %convert_add_fusion = f32[640,512]{1,0:T(8,128)S(1)} fusion(f32[656,512]{1,0:T(8,128)S(1)} %get-tuple-element.114, bf16[656,512]{1,0:T(8,128)(2,1)} %collective-permute-done.4), kind=kLoop, calls=%fused_computation | loop fusion | flops 655360 | bytes 3276800 | tf_op jit(solution)/shard_map/add | solution.py:447
  34.0 0.1 slice_select_fusion
  34.1 0.8 %reduce-precision_convert_fusion.3 = (bf16[1,512]{1,0:T(2,128)(2,1)S(1)}, f32[1,512]{1,0:T(1,128)S(1)}) fusion(bf16[656,512]{1,0:T(8,128)(2,1)} %collective-permute-done.4, f32[656,512]{1,0:T(8,128)S(1)} %get-tuple-element.114), kind=kLoop, calls=%fused_computation.36 | loop fusion | flops 3072 | bytes 7168 | tf_op jit(solution)/shard_map/convert_element_type | solution.py:445
  34.9 0.6 collective-permute-start.5
  35.5 4.0 %shard_map.133 = (bf16[64,640]{1,0:T(8,128)(2,1)}, f32[32,640]{1,0:T(8,128)S(1)}) custom-call(bf16[64,640]{1,0:T(8,128)(2,1)S(1)} %get-tuple-element.103.enc_ref, bf16[32,640]{1,0:T(8,128)(2,1)S(1)} %get-tuple-element.104.pred_ref, bf16[2048,1024]{1,0:T(8,128)(2,1)} %get-tuple-element.125.d_ref, bf16[640,1024]{1,0:T(8,128)(2,1)S(1)} %get-tuple-element.105.w_ref), custom_call_target="tpu_custom_call" | custom-call | tf_op jit(solution)/shard_map/pallas_call | solution.py:373
  39.6 2.7 %collective-permute-done.5 = bf16[336,512]{1,0:T(8,128)(2,1)S(1)} collective-permute-done((bf16[336,512]{1,0:T(8,128)(2,1)S(1)}, bf16[336,512]{1,0:T(8,128)(2,1)S(1)}, u32[]{:S(2)}, u32[]{:S(2)}) %collective-permute-start.5) | collective-permute-done | bytes 344096 | tf_op jit(solution)/shard_map/ppermute | solution.py:412
  42.5 0.7 collective-permute-start.6
  43.2 4.1 %shard_map.134 = (bf16[64,640]{1,0:T(8,128)(2,1)}, bf16[32,640]{1,0:T(8,128)(2,1)}) custom-call(bf16[64,640]{1,0:T(8,128)(2,1)S(1)} %get-tuple-element.103.enc_ref, bf16[32,640]{1,0:T(8,128)(2,1)S(1)} %get-tuple-element.104.pred_ref, bf16[2048,1024]{1,0:T(8,128)(2,1)} %get-tuple-element.125.d_ref, ...), custom_call_target="tpu_custom_call", output_to_operand_aliasing={{0}: (5, {})} | custom-call | tf_op jit(solution)/shard_map/pallas_call | solution.py:373
  47.3 0.8 %collective-permute-done.6 = bf16[176,512]{1,0:T(8,128)(2,1)S(1)} collective-permute-done((bf16[176,512]{1,0:T(8,128)(2,1)S(1)}, bf16[176,512]{1,0:T(8,128)(2,1)S(1)}, u32[]{:S(2)}, u32[]{:S(2)}) %collective-permute-start.6) | collective-permute-done | bytes 180256 | tf_op jit(solution)/shard_map/ppermute | solution.py:412
  48.1 2.7 %collective-permute-start.7 = (bf16[176,512]{1,0:T(8,128)(2,1)S(1)}, bf16[176,512]{1,0:T(8,128)(2,1)S(1)}, u32[]{:S(2)}, u32[]{:S(2)}) collective-permute-start(bf16[176,512]{1,0:T(8,128)(2,1)S(1)} %pad_maximum_fusion.2), channel_id=1, source_target_pairs={{0,8},{1,9},{2,10},{3,11},{4,12},{5,13},{6,14},{7,15},{8,0},{9,1},... | collective-permute-start | bytes 540680 | tf_op jit(solution)/shard_map/ppermute | solution.py:412
  50.8 7.0 %collective-permute-done.7 = bf16[176,512]{1,0:T(8,128)(2,1)S(1)} collective-permute-done((bf16[176,512]{1,0:T(8,128)(2,1)S(1)}, bf16[176,512]{1,0:T(8,128)(2,1)S(1)}, u32[]{:S(2)}, u32[]{:S(2)}) %collective-permute-start.7) | collective-permute-done | bytes 180256 | tf_op jit(solution)/shard_map/ppermute | solution.py:412
  57.9 0.2 collective-permute-start.8
  58.1 5.2 %collective-permute-done.8 = bf16[160,512]{1,0:T(8,128)(2,1)S(1)} collective-permute-done((bf16[160,512]{1,0:T(8,128)(2,1)S(1)}, bf16[160,512]{1,0:T(8,128)(2,1)S(1)}, u32[]{:S(2)}, u32[]{:S(2)}) %collective-permute-start.8) | collective-permute-done | bytes 163872 | tf_op jit(solution)/shard_map/ppermute | solution.py:412
  63.4 1.2 %collective-permute-start.9 = (bf16[320,512]{1,0:T(8,128)(2,1)S(1)}, bf16[320,512]{1,0:T(8,128)(2,1)S(1)}, u32[]{:S(2)}, u32[]{:S(2)}) collective-permute-start(bf16[320,512]{1,0:T(8,128)(2,1)S(1)} %maximum_select_fusion.1), channel_id=1, source_target_pairs={{0,2},{1,5},{2,0},{3,7},{4,6},{5,1},{6,4},{7,3},{8,10},{9,13},{10,... | collective-permute-start | bytes 983048 | tf_op jit(solution)/shard_map/ppermute | solution.py:412
  64.7 5.9 %collective-permute-done.9 = bf16[320,512]{1,0:T(8,128)(2,1)S(1)} collective-permute-done((bf16[320,512]{1,0:T(8,128)(2,1)S(1)}, bf16[320,512]{1,0:T(8,128)(2,1)S(1)}, u32[]{:S(2)}, u32[]{:S(2)}) %collective-permute-start.9) | collective-permute-done | bytes 327712 | tf_op jit(solution)/shard_map/ppermute | solution.py:412
  70.5 0.2 maximum_select_fusion.have_ref
  70.9 1.7 %shard_map.135.refs_0_ = f32[640,1024]{1,0:T(8,128)} custom-call(s32[3]{0:T(128)S(1)} %get-tuple-element.100.pick_ref.core_ref, bf16[640,512]{1,0:T(8,128)(2,1)S(1)} %maximum_select_fusion.have_ref), custom_call_target="tpu_custom_call" | custom-call | tf_op jit(solution)/shard_map/pallas_call | solution.py:279
  72.6 0.4 collective-permute-done.10.have_ref.refs_2_
  73.0 1.7 %shard_map.136 = (f32[640,1024]{1,0:T(8,128)}, f32[1,1024]{1,0:T(1,128)}) custom-call(s32[3]{0:T(128)S(1)} %get-tuple-element.100.pick_ref.core_ref, bf16[656,512]{1,0:T(8,128)(2,1)S(1)} %collective-permute-done.10.have_ref.refs_2_, f32[640,1024]{1,0:T(8,128)} %shard_map.135.refs_0_, ...), custom_call_target="tpu_custom_call", output_to_operand_aliasing={{0}: (2, {})} | custom-call | tf_op jit(solution)/shard_map/pallas_call | solution.py:279
  (29 shorter events, 0.9 us)
Async XLA Ops:
  0.6 3.7 %collective-permute-start = (bf16[1,3,2048]{2,1,0:T(4,128)(2,1)}, bf16[1,3,2048]{2,1,0:T(4,128)(2,1)S(1)}, u32[]{:S(2)}, u32[]{:S(2)}) collective-permute-start(bf16[1,3,2048]{2,1,0:T(4,128)(2,1)} %param.9), channel_id=1, source_target_pairs={{0,1},{1,0},{2,3},{3,2},{4,5},{5,4},{6,7},{7,6},{8,9},{9,8},{10,11... | collective-permute-start | bytes 36872 | tf_op jit(solution)/shard_map/ppermute | solution.py:412
  1.2 0.7 copy-start
  1.8 2.5 %copy-start.1 = (bf16[1,3,2048]{2,1,0:T(4,128)(2,1)S(1)}, bf16[1,3,2048]{2,1,0:T(4,128)(2,1)}, u32[]{:S(2)}) copy-start(bf16[1,3,2048]{2,1,0:T(4,128)(2,1)} %param.9) | copy-start | bytes 36868
  4.4 5.2 %collective-permute-start.1 = (bf16[2,3,2048]{2,1,0:T(4,128)(2,1)S(1)}, bf16[2,3,2048]{2,1,0:T(4,128)(2,1)S(1)}, u32[]{:S(2)}, u32[]{:S(2)}) collective-permute-start(bf16[2,3,2048]{2,1,0:T(4,128)(2,1)S(1)} %pad_maximum_fusion.6), channel_id=1, source_target_pairs={{0,2},{1,3},{2,0},{3,1},{4,6},{5,7},{6,4},{7,5},{8,10},{9,11},{10,... | collective-permute-start | bytes 73736 | tf_op jit(solution)/shard_map/ppermute | solution.py:412
  9.6 4.3 %collective-permute-start.2 = (bf16[4,3,2048]{2,1,0:T(4,128)(2,1)S(1)}, bf16[4,3,2048]{2,1,0:T(4,128)(2,1)S(1)}, u32[]{:S(2)}, u32[]{:S(2)}) collective-permute-start(bf16[4,3,2048]{2,1,0:T(4,128)(2,1)S(1)} %pad_maximum_fusion.5), channel_id=1, source_target_pairs={{0,4},{1,5},{2,6},{3,7},{4,0},{5,1},{6,2},{7,3},{8,12},{9,13},{10,... | collective-permute-start | bytes 147464 | tf_op jit(solution)/shard_map/ppermute | solution.py:412
  14.0 8.4 %collective-permute-start.3 = (bf16[8,3,2048]{2,1,0:T(4,128)(2,1)S(1)}, bf16[8,3,2048]{2,1,0:T(4,128)(2,1)S(1)}, u32[]{:S(2)}, u32[]{:S(2)}) collective-permute-start(bf16[8,3,2048]{2,1,0:T(4,128)(2,1)S(1)} %pad_maximum_fusion.4.qa_ref), channel_id=1, source_target_pairs={{0,8},{1,9},{2,10},{3,11},{4,12},{5,13},{6,14},{7,15},{8,0},{9,1},... | collective-permute-start | bytes 294920 | tf_op jit(solution)/shard_map/ppermute | solution.py:412
  30.3 2.3 %collective-permute-start.4 = (bf16[656,512]{1,0:T(8,128)(2,1)S(1)}, bf16[656,512]{1,0:T(8,128)(2,1)}, u32[]{:S(2)}, u32[]{:S(2)}) collective-permute-start(bf16[656,512]{1,0:T(8,128)(2,1)S(1)} %get-tuple-element.115), channel_id=1, source_target_pairs={{0,1},{1,0},{2,3},{3,2},{4,5},{5,4},{6,7},{7,6},{8,9},{9,8},{10,11... | collective-permute-start | bytes 2015240 | tf_op jit(solution)/shard_map/ppermute | solution.py:412
  34.9 7.3 %collective-permute-start.5 = (bf16[336,512]{1,0:T(8,128)(2,1)S(1)}, bf16[336,512]{1,0:T(8,128)(2,1)S(1)}, u32[]{:S(2)}, u32[]{:S(2)}) collective-permute-start(bf16[336,512]{1,0:T(8,128)(2,1)S(1)} %pad_maximum_fusion.1), channel_id=1, source_target_pairs={{0,2},{1,5},{2,0},{3,7},{4,6},{5,1},{6,4},{7,3},{8,10},{9,13},{10,... | collective-permute-start | bytes 1032200 | tf_op jit(solution)/shard_map/ppermute | solution.py:412
  42.5 5.6 %collective-permute-start.6 = (bf16[176,512]{1,0:T(8,128)(2,1)S(1)}, bf16[176,512]{1,0:T(8,128)(2,1)S(1)}, u32[]{:S(2)}, u32[]{:S(2)}) collective-permute-start(bf16[176,512]{1,0:T(8,128)(2,1)S(1)} %pad_maximum_fusion.3), channel_id=1, source_target_pairs={{0,4},{1,3},{2,6},{3,1},{4,0},{5,7},{6,2},{7,5},{8,12},{9,11},{10,... | collective-permute-start | bytes 540680 | tf_op jit(solution)/shard_map/ppermute | solution.py:412
  48.1 9.7 %collective-permute-start.7 = (bf16[176,512]{1,0:T(8,128)(2,1)S(1)}, bf16[176,512]{1,0:T(8,128)(2,1)S(1)}, u32[]{:S(2)}, u32[]{:S(2)}) collective-permute-start(bf16[176,512]{1,0:T(8,128)(2,1)S(1)} %pad_maximum_fusion.2), channel_id=1, source_target_pairs={{0,8},{1,9},{2,10},{3,11},{4,12},{5,13},{6,14},{7,15},{8,0},{9,1},... | collective-permute-start | bytes 540680 | tf_op jit(solution)/shard_map/ppermute | solution.py:412
  57.9 5.4 %collective-permute-start.8 = (bf16[160,512]{1,0:T(8,128)(2,1)S(1)}, bf16[160,512]{1,0:T(8,128)(2,1)S(1)}, u32[]{:S(2)}, u32[]{:S(2)}) collective-permute-start(bf16[160,512]{1,0:T(8,128)(2,1)S(1)} %add_convert_fusion), channel_id=1, source_target_pairs={{0,4},{1,3},{2,6},{3,1},{4,0},{5,7},{6,2},{7,5},{8,12},{9,11},{10,... | collective-permute-start | bytes 491528 | tf_op jit(solution)/shard_map/ppermute | solution.py:412
  63.4 7.1 %collective-permute-start.9 = (bf16[320,512]{1,0:T(8,128)(2,1)S(1)}, bf16[320,512]{1,0:T(8,128)(2,1)S(1)}, u32[]{:S(2)}, u32[]{:S(2)}) collective-permute-start(bf16[320,512]{1,0:T(8,128)(2,1)S(1)} %maximum_select_fusion.1), channel_id=1, source_target_pairs={{0,2},{1,5},{2,0},{3,7},{4,6},{5,1},{6,4},{7,3},{8,10},{9,13},{10,... | collective-permute-start | bytes 983048 | tf_op jit(solution)/shard_map/ppermute | solution.py:412
  70.8 2.2 %collective-permute-start.10 = (bf16[656,512]{1,0:T(8,128)(2,1)S(1)}, bf16[656,512]{1,0:T(8,128)(2,1)S(1)}, u32[]{:S(2)}, u32[]{:S(2)}) collective-permute-start(bf16[656,512]{1,0:T(8,128)(2,1)S(1)} %pad_maximum_fusion), channel_id=1, source_target_pairs={{0,1},{1,0},{2,3},{3,2},{4,5},{5,4},{6,7},{7,6},{8,9},{9,8},{10,11... | collective-permute-start | bytes 2015240 | tf_op jit(solution)/shard_map/ppermute | solution.py:412

commit v5 on v4

--- a/solution.py
+++ b/solution.py
@@ -11,6 +11,7 @@
 BF16 = jnp.bfloat16
 LANES = 128
 EXTRA = 16
+CHAINS = 2
 
 
 def params(mib):
@@ -59,7 +60,7 @@
         + [jax.ShapeDtypeStruct((3,), jnp.int32)],
         scratch_shapes=[pltpu.SemaphoreType.DMA((len(arrays),))],
         compiler_params=pltpu.CompilerParams(vmem_limit_bytes=4 * 1024 * 1024),
-    )(assignment, *[pltpu.with_memory_space_constraint(x, pltpu.HBM) for x in arrays])
+    )(*[pltpu.with_memory_space_constraint(x, pltpu.HBM) for x in (assignment, *arrays)])
 
 
 def in_vmem(x):
@@ -243,48 +244,44 @@
         gp_ref[...] = gp_scr[...].astype(gp_ref.dtype)
 
 
-def final_kernel(with_bias, core_ref, have_ref, *refs):
-    out_ref = refs[-2] if with_bias else refs[-1]
-    out_ref[...] = have_ref[...].astype(F32)
-    if with_bias:
-        mine_ref, rows_ref, bias_ref = refs[1], refs[2], refs[-1]
-        mine = mine_ref[...]
-        other = rows_ref[0:1, :].astype(F32) + rows_ref[1:2, :].astype(F32)
-        core = core_ref[2]
-        bias_ref[...] = jnp.concatenate(
-            [jnp.where(core == 0, mine, other), jnp.where(core == 0, other, mine)], axis=1
-        )
-
-
-def widen(pick, have, width, before=(), mine=None):
-    part = have.shape[1]
+def final_kernel(pick_ref, *refs):
+    out_ref, bias_ref = refs[-2:]
+    for c in range(CHAINS):
+        source_ref, rows_ref = refs[2 * c], refs[2 * c + 1]
+        span = source_ref.shape[1]
+        cols = slice(c * span, (c + 1) * span)
+        out_ref[:, cols] = source_ref[...].astype(F32)
+        bias_ref[:, cols] = rows_ref[0:1, :].astype(F32) + rows_ref[1:2, :].astype(F32)
+
+
+def widen(pick, sources, width, vocab, mine, before):
+    span = sources[0].shape[1]
     rows = width // 2
-    with_bias = mine is not None
-    if with_bias:
-        place = lambda i, pick: (i, 1 - pick[2])
-    else:
-        place = lambda i, pick: (i, pick[2])
-    in_specs = [pl.BlockSpec((rows, part), lambda i, pick: (i, 0))]
-    out_specs = [pl.BlockSpec((rows, part), place)]
-    out_shape = [jax.ShapeDtypeStruct((width, 2 * part), F32)]
-    extra = ()
-    if with_bias:
-        in_specs += [
-            pl.BlockSpec(memory_space=pl.ANY), whole(mine.shape),
-            pl.BlockSpec((EXTRA, part), lambda i, pick: (width // EXTRA, 0)),
-        ]
-        out_specs += [whole((1, 2 * part))]
-        out_shape += [jax.ShapeDtypeStruct((1, 2 * part), F32)]
-        extra = (*before, mine, have)
+
+    def column(pick):
+        return pick[2] if mine else 1 - pick[2]
+
+    pair = [
+        pl.BlockSpec((rows, span), lambda i, pick: (i, 0)),
+        pl.BlockSpec((EXTRA, span), lambda i, pick: (width // EXTRA, 0)),
+    ]
     return pl.pallas_call(
-        functools.partial(final_kernel, with_bias),
+        final_kernel,
         grid_spec=pltpu.PrefetchScalarGridSpec(
-            num_scalar_prefetch=1, grid=(width // rows,), in_specs=in_specs, out_specs=out_specs
+            num_scalar_prefetch=1,
+            grid=(width // rows,),
+            in_specs=pair * CHAINS + [pl.BlockSpec(memory_space=pl.ANY)] * len(before),
+            out_specs=[
+                pl.BlockSpec((rows, vocab // 2), lambda i, pick: (i, column(pick))),
+                pl.BlockSpec((1, vocab // 2), lambda i, pick: (0, column(pick))),
+            ],
         ),
-        out_shape=out_shape,
-        input_output_aliases={2: 0} if with_bias else {},
+        out_shape=[
+            jax.ShapeDtypeStruct((width, vocab), F32), jax.ShapeDtypeStruct((1, vocab), F32)
+        ],
+        input_output_aliases={1 + 2 * CHAINS + k: k for k in range(len(before))},
         compiler_params=params(8),
-    )(pick, have, *extra)
+    )(pick, *[s for source in sources for s in (source, source)], *before)
 
 
 def whole(shape):
@@ -441,7 +438,7 @@
         return rows_of[0:1].astype(F32) + rows_of[1:2].astype(F32)
 
     def bias_rows(high, low):
-        filler = jnp.zeros((EXTRA - 2, part), BF16)
+        filler = jnp.zeros((EXTRA - 2, high.shape[1]), BF16)
         return jnp.concatenate([high.astype(BF16), low.astype(BF16), filler], axis=0)
 
     acc = keep[:width] + got[:width].astype(F32)
@@ -453,18 +450,14 @@
     sides = []
     count = width
     done = ()
-    for k, (even, odd) in enumerate(orders):
+    for k, (even, odd) in enumerate(orders[:-1]):
         high, low = split_two(bias)
-        if k < len(orders) - 1:
-            side = (own & jnp.where(core == 0, even, odd)) != 0
-            sides.append(side)
-            count //= 2
-            top, bottom = acc[:count], acc[count:]
-            send = jnp.where(side, top, bottom).astype(BF16)
-            acc = jnp.where(side, bottom, top)
-        else:
-            send = acc.astype(BF16)
-            acc = lax.reduce_precision(acc, 8, 7)
+        side = (own & jnp.where(core == 0, even, odd)) != 0
+        sides.append(side)
+        count //= 2
+        top, bottom = acc[:count], acc[count:]
+        send = jnp.where(side, top, bottom).astype(BF16)
+        acc = jnp.where(side, bottom, top)
         send = jnp.concatenate([send, bias_rows(high, low)], axis=0)
         if k < 2:
             send, acc, d_low = lax.optimization_barrier((send, acc, d_low))
@@ -476,17 +469,43 @@
             got, done = lax.optimization_barrier((got, done))
         acc = acc + got[:count].astype(F32)
         bias = (high + low) + got_bias(got[count:])
-    have = acc.astype(BF16)
+    chains = range(CHAINS)
+    span = part // CHAINS
+    even, odd = orders[-1]
+    sums, kept, parts = [], [], []
+    for c in chains:
+        cols = slice(c * span, (c + 1) * span)
+        high, low = split_two(bias[:, cols])
+        sums.append((high, low))
+        sent = acc[:, cols].astype(BF16)
+        kept.append(lax.reduce_precision(acc[:, cols], 8, 7))
+        parts.append(exchange(jnp.concatenate([sent, bias_rows(high, low)], axis=0), even, odd))
+    have = []
+    for c in chains:
+        got = parts[c]
+        if c:
+            got, have = lax.optimization_barrier((got, have))
+        have.append((kept[c] + got[:count].astype(F32)).astype(BF16))
+        high, low = sums[c]
+        sums[c] = split_two((high + low) + got_bias(got[count:]))
     for (even, odd), side in list(zip(orders, sides))[::-1]:
-        got = exchange(have, even, odd)
-        have = jnp.where(
-            side, jnp.concatenate([got, have], axis=0), jnp.concatenate([have, got], axis=0)
-        )
-    high, low = split_two(bias)
-    got = exchange(jnp.concatenate([have, bias_rows(high, low)], axis=0), 1, 1)
-    half = widen(pick, have, width)
-    got, half = lax.optimization_barrier((got, half))
-    grad_weight, grad_bias = widen(pick, got, width, half, high + low)
+        parts = [exchange(have[c], even, odd) for c in chains]
+        joined = []
+        for c in chains:
+            if c:
+                parts[c], joined = lax.optimization_barrier((parts[c], joined))
+            joined.append(jnp.where(
+                side,
+                jnp.concatenate([parts[c], have[c]], axis=0),
+                jnp.concatenate([have[c], parts[c]], axis=0),
+            ))
+        have = joined
+    sent = [jnp.concatenate([have[c], bias_rows(*sums[c])], axis=0) for c in chains]
+    others = [exchange(sent[c], 1, 1) for c in chains]
+    result = tuple(widen(pick, sent, width, vocab, True, ()))
+    others, result = lax.optimization_barrier((others, result))
+    result = tuple(widen(pick, others, width, vocab, False, result))
+    grad_weight, grad_bias = result
     return (loss.reshape(1), grad_weight, grad_bias.reshape(vocab), done[0][None], done[1][None])
 
 

time: 75 us -> 74.2 us (0.989)
  waiting for transfers between devices: 26.1 us -> 22 us
  starting transfers between devices: 12.9 us -> 16.5 us
    ppermute x11 -> x15, waiting for transfers between devices: 26.1 us -> 22 us  [exchange(): return lax.ppermute(value, 'dp', pairs)]
    ppermute x11 -> x15, starting transfers between devices: 12.9 us -> 16.5 us  [exchange(): return lax.ppermute(value, 'dp', pairs)]
  transfers between devices with their start and end apart: 11 -> 15, of which waited for: 9 -> 11; matrix products, arithmetic and copies ran while one was open for 0% -> 0% of each run, Pallas kernels for 27% -> 28%
where the time goes in v5:
time: 74.2 us; the launch traced here: 73.9 us
  Pallas kernels  30 us (40%)
  waiting for transfers between devices  22 us (30%)
  starting transfers between devices  16.5 us (22%)
  other arithmetic  3.19 us (4%)
  between operations  2.17 us (3%)
    ppermute x15, waiting for transfers between devices, exchange(): return lax.ppermute(value, 'dp', pairs)  22 us
    ppermute x15, starting transfers between devices, exchange(): return lax.ppermute(value, 'dp', pairs)  16.5 us
    pallas_call x2, Pallas kernels, input_gradients(): pl.pallas_call(functools.partial(input_kernel, begin, last), grid=(cells...  8.12 us
    pallas_call x3, Pallas kernels, forward(): pl.pallas_call(functools.partial(forward_kernel, begin), grid=(blocks,),...  7.96 us
    pallas_call x1, Pallas kernels, gradients(): pl.pallas_call(grad_kernel, grid_spec=grid_spec, out_shape=[pltpu.HBM((ce...  7.94 us
    pallas_call x2, Pallas kernels, widen(): pl.pallas_call(final_kernel, grid_spec=pltpu.PrefetchScalarGridSpec(num_s...  3.34 us
    pallas_call x1, Pallas kernels, stage(): pl.pallas_call(stage_kernel, in_specs=[smem] + [anywhere] * len(arrays),...  2.62 us
  transfers between devices with their start and end apart: 15, of which 11 were waited for; matrix products, arithmetic and copies ran while one was open for 0% of the time, Pallas kernels for 28%

profile of v5, /device:TPU:0, one launch (start us, length us, event | category | flops | bytes accessed | tf_op | source)
XLA Modules:
  0.0 73.9 jit_solution(544101048693882343)
XLA Ops:
  0.6 0.5 collective-permute-start
  1.2 2.6 %shard_map.128 = (bf16[640,1024]{1,0:T(8,128)(2,1)S(1)}, bf16[64,640]{1,0:T(8,128)(2,1)S(1)}, bf16[32,640]{1,0:T(8,128)(2,1)S(1)}, f32[1,1024]{1,0:T(1,128)S(1)}, s32[1,31]{1,0:T(1,128)S(1)}, /*index=5*/s32[3]{0:T(128)S(1)}) custom-call(s32[16]{0:T(128)} %assignment_ref.1, bf16[640,1024]{1,0:T(8,128)(2,1)} %refs_0_.1, bf16[64,640]{1,0:T(8,128)(2,1)} %bitcast.7, ...), custom_call_target="tpu_custom_call" | custom-call | tf_op jit(solution)/shard_map/pallas_call | solution.py:55
  3.8 2.6 %collective-permute-start.1 = (bf16[2,3,2048]{2,1,0:T(4,128)(2,1)S(1)}, bf16[2,3,2048]{2,1,0:T(4,128)(2,1)S(1)}, u32[]{:S(2)}, u32[]{:S(2)}) collective-permute-start(bf16[2,3,2048]{2,1,0:T(4,128)(2,1)S(1)} %pad_maximum_fusion.8), channel_id=1, source_target_pairs={{0,2},{1,3},{2,0},{3,1},{4,6},{5,7},{6,4},{7,5},{8,10},{9,11},{10,... | collective-permute-start | bytes 73736 | tf_op jit(solution)/shard_map/ppermute | solution.py:409
  7.1 1.9 %shard_map.129 = (f32[2048,1024]{1,0:T(8,128)S(1)}, f32[8,2048]{1,0:T(8,128)S(1)}, bf16[640,2048]{1,0:T(8,128)(2,1)S(1)}) custom-call(s32[1]{0:T(128)S(6)} %copy.33.tlen_ref, s32[1,31]{1,0:T(1,128)S(1)} %get-tuple-element.111.labels_ref, bf16[64,640]{1,0:T(8,128)(2,1)S(1)} %get-tuple-element.113.enc_ref, bf16[32,640]{1,0:T(8,128)(2,1)S(1)} %get-tuple-element.114.pred_ref, ...), custom_call_target="tpu_custom_call" | custom-call | tf_op jit(solution)/shard_map/pallas_call | solution.py:299
  9.1 1.6 %collective-permute-start.2 = (bf16[4,3,2048]{2,1,0:T(4,128)(2,1)S(1)}, bf16[4,3,2048]{2,1,0:T(4,128)(2,1)S(1)}, u32[]{:S(2)}, u32[]{:S(2)}) collective-permute-start(bf16[4,3,2048]{2,1,0:T(4,128)(2,1)S(1)} %pad_maximum_fusion.7), channel_id=1, source_target_pairs={{0,4},{1,5},{2,6},{3,7},{4,0},{5,1},{6,2},{7,3},{8,12},{9,13},{10,... | collective-permute-start | bytes 147464 | tf_op jit(solution)/shard_map/ppermute | solution.py:409
  10.7 1.9 %shard_map.130 = (f32[2048,1024]{1,0:T(8,128)S(1)}, f32[8,2048]{1,0:T(8,128)S(1)}, bf16[640,2048]{1,0:T(8,128)(2,1)S(1)}) custom-call(s32[1]{0:T(128)S(6)} %copy.33.tlen_ref, s32[1,31]{1,0:T(1,128)S(1)} %get-tuple-element.111.labels_ref, bf16[64,640]{1,0:T(8,128)(2,1)S(1)} %get-tuple-element.113.enc_ref, ...), custom_call_target="tpu_custom_call", output_to_operand_aliasing={{0}: (6, {}), {1}: (7, {}), {2}: (8, {})} | custom-call | tf_op jit(solution)/shard_map/pallas_call | solution.py:299
  12.6 0.8 %collective-permute-done.2 = bf16[4,3,2048]{2,1,0:T(4,128)(2,1)S(1)} collective-permute-done((bf16[4,3,2048]{2,1,0:T(4,128)(2,1)S(1)}, bf16[4,3,2048]{2,1,0:T(4,128)(2,1)S(1)}, u32[]{:S(2)}, u32[]{:S(2)}) %collective-permute-start.2) | collective-permute-done | bytes 49184 | tf_op jit(solution)/shard_map/ppermute | solution.py:409
  13.5 2.7 %collective-permute-start.3 = (bf16[8,3,2048]{2,1,0:T(4,128)(2,1)S(1)}, bf16[8,3,2048]{2,1,0:T(4,128)(2,1)S(1)}, u32[]{:S(2)}, u32[]{:S(2)}) collective-permute-start(bf16[8,3,2048]{2,1,0:T(4,128)(2,1)S(1)} %pad_maximum_fusion.4.qa_ref), channel_id=1, source_target_pairs={{0,8},{1,9},{2,10},{3,11},{4,12},{5,13},{6,14},{7,15},{8,0},{9,1},... | collective-permute-start | bytes 294920 | tf_op jit(solution)/shard_map/ppermute | solution.py:409
  16.8 4.1 %shard_map.131 = (f32[2048,1024]{1,0:T(8,128)S(1)}, f32[8,2048]{1,0:T(8,128)S(1)}, bf16[640,2048]{1,0:T(8,128)(2,1)S(1)}) custom-call(s32[1]{0:T(128)S(6)} %copy.33.tlen_ref, s32[1,31]{1,0:T(1,128)S(1)} %get-tuple-element.111.labels_ref, bf16[64,640]{1,0:T(8,128)(2,1)S(1)} %get-tuple-element.113.enc_ref, ...), custom_call_target="tpu_custom_call", output_to_operand_aliasing={{0}: (6, {}), {1}: (7, {}), {2}: (8, {})} | custom-call | tf_op jit(solution)/shard_map/pallas_call | solution.py:299
  20.9 1.0 %collective-permute-done.3.qb_ref = bf16[8,3,2048]{2,1,0:T(4,128)(2,1)S(1)} collective-permute-done((bf16[8,3,2048]{2,1,0:T(4,128)(2,1)S(1)}, bf16[8,3,2048]{2,1,0:T(4,128)(2,1)S(1)}, u32[]{:S(2)}, u32[]{:S(2)}) %collective-permute-start.3) | collective-permute-done | bytes 98336 | tf_op jit(solution)/shard_map/ppermute | solution.py:409
  21.9 7.9 %shard_map.132 = (bf16[2048,1024]{1,0:T(8,128)(2,1)}, f32[1,1]{1,0:T(1,128)}, bf16[656,512]{1,0:T(8,128)(2,1)S(1)}, f32[656,512]{1,0:T(8,128)S(1)}) custom-call(s32[3]{0:T(128)S(1)} %get-tuple-element.110.pick_ref, s32[1]{0:T(128)S(6)} %copy.32.flen_ref, s32[1]{0:T(128)S(6)} %copy.33.tlen_ref, s32[1,31]{1,0:T(1,128)S(1)} %get-tuple-element.111.labels_ref, ...), custom_call_target="tpu_custom_call" | custom-call | tf_op jit(solution)/shard_map/pallas_call | solution.py:351
  29.8 2.2 %collective-permute-done.4 = bf16[656,512]{1,0:T(8,128)(2,1)} collective-permute-done((bf16[656,512]{1,0:T(8,128)(2,1)S(1)}, bf16[656,512]{1,0:T(8,128)(2,1)}, u32[]{:S(2)}, u32[]{:S(2)}) %collective-permute-start.4) | collective-permute-done | bytes 671776 | tf_op jit(solution)/shard_map/ppermute | solution.py:409
  32.0 1.3 %convert_add_fusion = f32[640,512]{1,0:T(8,128)S(1)} fusion(f32[656,512]{1,0:T(8,128)S(1)} %get-tuple-element.124, bf16[656,512]{1,0:T(8,128)(2,1)} %collective-permute-done.4), kind=kLoop, calls=%fused_computation | loop fusion | flops 655360 | bytes 3276800 | tf_op jit(solution)/shard_map/add | solution.py:444
  33.5 0.8 %reduce-precision_convert_fusion.1 = (bf16[1,512]{1,0:T(2,128)(2,1)S(1)}, f32[1,512]{1,0:T(1,128)S(1)}) fusion(bf16[656,512]{1,0:T(8,128)(2,1)} %collective-permute-done.4, f32[656,512]{1,0:T(8,128)S(1)} %get-tuple-element.124), kind=kLoop, calls=%fused_computation.33 | loop fusion | flops 3072 | bytes 7168 | tf_op jit(solution)/shard_map/convert_element_type | solution.py:442
  34.4 0.6 collective-permute-start.5
  35.0 4.0 %shard_map.133 = (bf16[64,640]{1,0:T(8,128)(2,1)}, f32[32,640]{1,0:T(8,128)S(1)}) custom-call(bf16[64,640]{1,0:T(8,128)(2,1)S(1)} %get-tuple-element.113.enc_ref, bf16[32,640]{1,0:T(8,128)(2,1)S(1)} %get-tuple-element.114.pred_ref, bf16[2048,1024]{1,0:T(8,128)(2,1)} %get-tuple-element.135.d_ref, bf16[640,1024]{1,0:T(8,128)(2,1)S(1)} %get-tuple-element.115.w_ref), custom_call_target="tpu_custom_call" | custom-call | tf_op jit(solution)/shard_map/pallas_call | solution.py:370
  39.0 2.7 %collective-permute-done.5 = bf16[336,512]{1,0:T(8,128)(2,1)S(1)} collective-permute-done((bf16[336,512]{1,0:T(8,128)(2,1)S(1)}, bf16[336,512]{1,0:T(8,128)(2,1)S(1)}, u32[]{:S(2)}, u32[]{:S(2)}) %collective-permute-start.5) | collective-permute-done | bytes 344096 | tf_op jit(solution)/shard_map/ppermute | solution.py:409
  41.9 0.7 collective-permute-start.6
  42.7 4.1 %shard_map.134 = (bf16[64,640]{1,0:T(8,128)(2,1)}, bf16[32,640]{1,0:T(8,128)(2,1)}) custom-call(bf16[64,640]{1,0:T(8,128)(2,1)S(1)} %get-tuple-element.113.enc_ref, bf16[32,640]{1,0:T(8,128)(2,1)S(1)} %get-tuple-element.114.pred_ref, bf16[2048,1024]{1,0:T(8,128)(2,1)} %get-tuple-element.135.d_ref, ...), custom_call_target="tpu_custom_call", output_to_operand_aliasing={{0}: (5, {})} | custom-call | tf_op jit(solution)/shard_map/pallas_call | solution.py:370
  46.7 0.8 %collective-permute-done.6 = bf16[176,512]{1,0:T(8,128)(2,1)S(1)} collective-permute-done((bf16[176,512]{1,0:T(8,128)(2,1)S(1)}, bf16[176,512]{1,0:T(8,128)(2,1)S(1)}, u32[]{:S(2)}, u32[]{:S(2)}) %collective-permute-start.6) | collective-permute-done | bytes 180256 | tf_op jit(solution)/shard_map/ppermute | solution.py:409
  47.6 2.7 %collective-permute-start.8 = (bf16[176,256]{1,0:T(8,128)(2,1)S(1)}, bf16[176,256]{1,0:T(8,128)(2,1)S(1)}, u32[]{:S(2)}, u32[]{:S(2)}) collective-permute-start(bf16[176,256]{1,0:T(8,128)(2,1)S(1)} %get-tuple-element.170), channel_id=1, source_target_pairs={{0,8},{1,9},{2,10},{3,11},{4,12},{5,13},{6,14},{7,15},{8,0},{9,1},... | collective-permute-start | bytes 270344 | tf_op jit(solution)/shard_map/ppermute | solution.py:409
  50.6 4.8 %collective-permute-done.8 = bf16[176,256]{1,0:T(8,128)(2,1)S(1)} collective-permute-done((bf16[176,256]{1,0:T(8,128)(2,1)S(1)}, bf16[176,256]{1,0:T(8,128)(2,1)S(1)}, u32[]{:S(2)}, u32[]{:S(2)}) %collective-permute-start.8) | collective-permute-done | bytes 90144 | tf_op jit(solution)/shard_map/ppermute | solution.py:409
  55.4 1.9 %collective-permute-done.7 = bf16[176,256]{1,0:T(8,128)(2,1)S(1)} collective-permute-done((bf16[176,256]{1,0:T(8,128)(2,1)S(1)}, bf16[176,256]{1,0:T(8,128)(2,1)S(1)}, u32[]{:S(2)}, u32[]{:S(2)}) %collective-permute-start.7) | collective-permute-done | bytes 90144 | tf_op jit(solution)/shard_map/ppermute | solution.py:409
  57.5 2.0 %collective-permute-start.9 = (bf16[160,256]{1,0:T(8,128)(2,1)S(1)}, bf16[160,256]{1,0:T(8,128)(2,1)S(1)}, u32[]{:S(2)}, u32[]{:S(2)}) collective-permute-start(bf16[160,256]{1,0:T(8,128)(2,1)S(1)} %add_convert_fusion), channel_id=1, source_target_pairs={{0,4},{1,3},{2,6},{3,1},{4,0},{5,7},{6,2},{7,5},{8,12},{9,11},{10,... | collective-permute-start | bytes 245768 | tf_op jit(solution)/shard_map/ppermute | solution.py:409
  59.5 2.3 %collective-permute-done.10 = bf16[160,256]{1,0:T(8,128)(2,1)S(1)} collective-permute-done((bf16[160,256]{1,0:T(8,128)(2,1)S(1)}, bf16[160,256]{1,0:T(8,128)(2,1)S(1)}, u32[]{:S(2)}, u32[]{:S(2)}) %collective-permute-start.10) | collective-permute-done | bytes 81952 | tf_op jit(solution)/shard_map/ppermute | solution.py:409
  61.8 0.8 %collective-permute-done.9 = bf16[160,256]{1,0:T(8,128)(2,1)S(1)} collective-permute-done((bf16[160,256]{1,0:T(8,128)(2,1)S(1)}, bf16[160,256]{1,0:T(8,128)(2,1)S(1)}, u32[]{:S(2)}, u32[]{:S(2)}) %collective-permute-start.9) | collective-permute-done | bytes 81952 | tf_op jit(solution)/shard_map/ppermute | solution.py:409
  62.7 1.2 %collective-permute-start.12 = (bf16[320,256]{1,0:T(8,128)(2,1)S(1)}, bf16[320,256]{1,0:T(8,128)(2,1)S(1)}, u32[]{:S(2)}, u32[]{:S(2)}) collective-permute-start(bf16[320,256]{1,0:T(8,128)(2,1)S(1)} %maximum_select_fusion.2), channel_id=1, source_target_pairs={{0,2},{1,5},{2,0},{3,7},{4,6},{5,1},{6,4},{7,3},{8,10},{9,13},{10,... | collective-permute-start | bytes 491528 | tf_op jit(solution)/shard_map/ppermute | solution.py:409
  63.9 0.9 %collective-permute-start.11 = (bf16[320,256]{1,0:T(8,128)(2,1)S(1)}, bf16[320,256]{1,0:T(8,128)(2,1)S(1)}, u32[]{:S(2)}, u32[]{:S(2)}) collective-permute-start(bf16[320,256]{1,0:T(8,128)(2,1)S(1)} %maximum_select_fusion.3), channel_id=1, source_target_pairs={{0,2},{1,5},{2,0},{3,7},{4,6},{5,1},{6,4},{7,3},{8,10},{9,13},{10,... | collective-permute-start | bytes 491528 | tf_op jit(solution)/shard_map/ppermute | solution.py:409
  64.8 3.2 %collective-permute-done.12 = bf16[320,256]{1,0:T(8,128)(2,1)S(1)} collective-permute-done((bf16[320,256]{1,0:T(8,128)(2,1)S(1)}, bf16[320,256]{1,0:T(8,128)(2,1)S(1)}, u32[]{:S(2)}, u32[]{:S(2)}) %collective-permute-start.12) | collective-permute-done | bytes 163872 | tf_op jit(solution)/shard_map/ppermute | solution.py:409
  68.1 1.6 %collective-permute-done.11 = bf16[320,256]{1,0:T(8,128)(2,1)S(1)} collective-permute-done((bf16[320,256]{1,0:T(8,128)(2,1)S(1)}, bf16[320,256]{1,0:T(8,128)(2,1)S(1)}, u32[]{:S(2)}, u32[]{:S(2)}) %collective-permute-start.11) | collective-permute-done | bytes 163872 | tf_op jit(solution)/shard_map/ppermute | solution.py:409
  70.5 1.7 %shard_map.135 = (f32[640,1024]{1,0:T(8,128)}, f32[1,1024]{1,0:T(1,128)}) custom-call(s32[3]{0:T(128)S(1)} %get-tuple-element.110.pick_ref, bf16[656,256]{1,0:T(8,128)(2,1)S(1)} %get-tuple-element.168.refs_0_.refs_1_, bf16[656,256]{1,0:T(8,128)(2,1)S(1)} %get-tuple-element.168.refs_0_.refs_1_, bf16[656,256]{1,0:T(8,128)(2,1)S(1)} %get-tuple-element.167.refs_2_.refs_3_, ...), custom_call_target="tpu_custom_call" | custom-call | tf_op jit(solution)/shard_map/pallas_call | solution.py:268
  72.2 1.7 %shard_map.136 = (f32[640,1024]{1,0:T(8,128)}, f32[1,1024]{1,0:T(1,128)}) custom-call(s32[3]{0:T(128)S(1)} %get-tuple-element.110.pick_ref, bf16[656,256]{1,0:T(8,128)(2,1)S(1)} %collective-permute-done.13.refs_0_.refs_1_, bf16[656,256]{1,0:T(8,128)(2,1)S(1)} %collective-permute-done.13.refs_0_.refs_1_, ...), custom_call_target="tpu_custom_call", output_to_operand_aliasing={{0}: (5, {}), {1}: (6, {})} | custom-call | tf_op jit(solution)/shard_map/pallas_call | solution.py:268
  (40 shorter events, 2.1 us)
Async XLA Ops:
  0.6 3.2 %copy-start = (bf16[1,3,2048]{2,1,0:T(4,128)(2,1)S(1)}, bf16[1,3,2048]{2,1,0:T(4,128)(2,1)}, u32[]{:S(2)}) copy-start(bf16[1,3,2048]{2,1,0:T(4,128)(2,1)} %param.9) | copy-start | bytes 36868
  0.6 3.1 %collective-permute-start = (bf16[1,3,2048]{2,1,0:T(4,128)(2,1)}, bf16[1,3,2048]{2,1,0:T(4,128)(2,1)S(1)}, u32[]{:S(2)}, u32[]{:S(2)}) collective-permute-start(bf16[1,3,2048]{2,1,0:T(4,128)(2,1)} %param.9), channel_id=1, source_target_pairs={{0,1},{1,0},{2,3},{3,2},{4,5},{5,4},{6,7},{7,6},{8,9},{9,8},{10,11... | collective-permute-start | bytes 36872 | tf_op jit(solution)/shard_map/ppermute | solution.py:409
  3.8 5.2 %collective-permute-start.1 = (bf16[2,3,2048]{2,1,0:T(4,128)(2,1)S(1)}, bf16[2,3,2048]{2,1,0:T(4,128)(2,1)S(1)}, u32[]{:S(2)}, u32[]{:S(2)}) collective-permute-start(bf16[2,3,2048]{2,1,0:T(4,128)(2,1)S(1)} %pad_maximum_fusion.8), channel_id=1, source_target_pairs={{0,2},{1,3},{2,0},{3,1},{4,6},{5,7},{6,4},{7,5},{8,10},{9,11},{10,... | collective-permute-start | bytes 73736 | tf_op jit(solution)/shard_map/ppermute | solution.py:409
  9.1 4.3 %collective-permute-start.2 = (bf16[4,3,2048]{2,1,0:T(4,128)(2,1)S(1)}, bf16[4,3,2048]{2,1,0:T(4,128)(2,1)S(1)}, u32[]{:S(2)}, u32[]{:S(2)}) collective-permute-start(bf16[4,3,2048]{2,1,0:T(4,128)(2,1)S(1)} %pad_maximum_fusion.7), channel_id=1, source_target_pairs={{0,4},{1,5},{2,6},{3,7},{4,0},{5,1},{6,2},{7,3},{8,12},{9,13},{10,... | collective-permute-start | bytes 147464 | tf_op jit(solution)/shard_map/ppermute | solution.py:409
  13.5 8.4 %collective-permute-start.3 = (bf16[8,3,2048]{2,1,0:T(4,128)(2,1)S(1)}, bf16[8,3,2048]{2,1,0:T(4,128)(2,1)S(1)}, u32[]{:S(2)}, u32[]{:S(2)}) collective-permute-start(bf16[8,3,2048]{2,1,0:T(4,128)(2,1)S(1)} %pad_maximum_fusion.4.qa_ref), channel_id=1, source_target_pairs={{0,8},{1,9},{2,10},{3,11},{4,12},{5,13},{6,14},{7,15},{8,0},{9,1},... | collective-permute-start | bytes 294920 | tf_op jit(solution)/shard_map/ppermute | solution.py:409
  29.8 2.3 %collective-permute-start.4 = (bf16[656,512]{1,0:T(8,128)(2,1)S(1)}, bf16[656,512]{1,0:T(8,128)(2,1)}, u32[]{:S(2)}, u32[]{:S(2)}) collective-permute-start(bf16[656,512]{1,0:T(8,128)(2,1)S(1)} %get-tuple-element.125), channel_id=1, source_target_pairs={{0,1},{1,0},{2,3},{3,2},{4,5},{5,4},{6,7},{7,6},{8,9},{9,8},{10,11... | collective-permute-start | bytes 2015240 | tf_op jit(solution)/shard_map/ppermute | solution.py:409
  34.4 7.3 %collective-permute-start.5 = (bf16[336,512]{1,0:T(8,128)(2,1)S(1)}, bf16[336,512]{1,0:T(8,128)(2,1)S(1)}, u32[]{:S(2)}, u32[]{:S(2)}) collective-permute-start(bf16[336,512]{1,0:T(8,128)(2,1)S(1)} %pad_maximum_fusion.2), channel_id=1, source_target_pairs={{0,2},{1,5},{2,0},{3,7},{4,6},{5,1},{6,4},{7,3},{8,10},{9,13},{10,... | collective-permute-start | bytes 1032200 | tf_op jit(solution)/shard_map/ppermute | solution.py:409
  41.9 5.6 %collective-permute-start.6 = (bf16[176,512]{1,0:T(8,128)(2,1)S(1)}, bf16[176,512]{1,0:T(8,128)(2,1)S(1)}, u32[]{:S(2)}, u32[]{:S(2)}) collective-permute-start(bf16[176,512]{1,0:T(8,128)(2,1)S(1)} %pad_maximum_fusion.3), channel_id=1, source_target_pairs={{0,4},{1,3},{2,6},{3,1},{4,0},{5,7},{6,2},{7,5},{8,12},{9,11},{10,... | collective-permute-start | bytes 540680 | tf_op jit(solution)/shard_map/ppermute | solution.py:409
  47.6 7.8 %collective-permute-start.8 = (bf16[176,256]{1,0:T(8,128)(2,1)S(1)}, bf16[176,256]{1,0:T(8,128)(2,1)S(1)}, u32[]{:S(2)}, u32[]{:S(2)}) collective-permute-start(bf16[176,256]{1,0:T(8,128)(2,1)S(1)} %get-tuple-element.170), channel_id=1, source_target_pairs={{0,8},{1,9},{2,10},{3,11},{4,12},{5,13},{6,14},{7,15},{8,0},{9,1},... | collective-permute-start | bytes 270344 | tf_op jit(solution)/shard_map/ppermute | solution.py:409
  50.3 7.0 %collective-permute-start.7 = (bf16[176,256]{1,0:T(8,128)(2,1)S(1)}, bf16[176,256]{1,0:T(8,128)(2,1)S(1)}, u32[]{:S(2)}, u32[]{:S(2)}) collective-permute-start(bf16[176,256]{1,0:T(8,128)(2,1)S(1)} %get-tuple-element.169), channel_id=1, source_target_pairs={{0,8},{1,9},{2,10},{3,11},{4,12},{5,13},{6,14},{7,15},{8,0},{9,1},... | collective-permute-start | bytes 270344 | tf_op jit(solution)/shard_map/ppermute | solution.py:409
  57.3 4.4 %collective-permute-start.10 = (bf16[160,256]{1,0:T(8,128)(2,1)S(1)}, bf16[160,256]{1,0:T(8,128)(2,1)S(1)}, u32[]{:S(2)}, u32[]{:S(2)}) collective-permute-start(bf16[160,256]{1,0:T(8,128)(2,1)S(1)} %add_convert_fusion.1), channel_id=1, source_target_pairs={{0,4},{1,3},{2,6},{3,1},{4,0},{5,7},{6,2},{7,5},{8,12},{9,11},{10,... | collective-permute-start | bytes 245768 | tf_op jit(solution)/shard_map/ppermute | solution.py:409
  57.5 5.2 %collective-permute-start.9 = (bf16[160,256]{1,0:T(8,128)(2,1)S(1)}, bf16[160,256]{1,0:T(8,128)(2,1)S(1)}, u32[]{:S(2)}, u32[]{:S(2)}) collective-permute-start(bf16[160,256]{1,0:T(8,128)(2,1)S(1)} %add_convert_fusion), channel_id=1, source_target_pairs={{0,4},{1,3},{2,6},{3,1},{4,0},{5,7},{6,2},{7,5},{8,12},{9,11},{10,... | collective-permute-start | bytes 245768 | tf_op jit(solution)/shard_map/ppermute | solution.py:409
  62.7 5.3 %collective-permute-start.12 = (bf16[320,256]{1,0:T(8,128)(2,1)S(1)}, bf16[320,256]{1,0:T(8,128)(2,1)S(1)}, u32[]{:S(2)}, u32[]{:S(2)}) collective-permute-start(bf16[320,256]{1,0:T(8,128)(2,1)S(1)} %maximum_select_fusion.2), channel_id=1, source_target_pairs={{0,2},{1,5},{2,0},{3,7},{4,6},{5,1},{6,4},{7,3},{8,10},{9,13},{10,... | collective-permute-start | bytes 491528 | tf_op jit(solution)/shard_map/ppermute | solution.py:409
  63.9 5.8 %collective-permute-start.11 = (bf16[320,256]{1,0:T(8,128)(2,1)S(1)}, bf16[320,256]{1,0:T(8,128)(2,1)S(1)}, u32[]{:S(2)}, u32[]{:S(2)}) collective-permute-start(bf16[320,256]{1,0:T(8,128)(2,1)S(1)} %maximum_select_fusion.3), channel_id=1, source_target_pairs={{0,2},{1,5},{2,0},{3,7},{4,6},{5,1},{6,4},{7,3},{8,10},{9,13},{10,... | collective-permute-start | bytes 491528 | tf_op jit(solution)/shard_map/ppermute | solution.py:409
  69.9 2.2 %collective-permute-start.13 = (bf16[656,256]{1,0:T(8,128)(2,1)S(1)}, bf16[656,256]{1,0:T(8,128)(2,1)S(1)}, u32[]{:S(2)}, u32[]{:S(2)}) collective-permute-start(bf16[656,256]{1,0:T(8,128)(2,1)S(1)} %get-tuple-element.168.refs_0_.refs_1_), channel_id=1, source_target_pairs={{0,1},{1,0},{2,3},{3,2},{4,5},{5,4},{6,7},{7,6},{8,9},{9,8},{10,11... | collective-permute-start | bytes 1007624 | tf_op jit(solution)/shard_map/ppermute | solution.py:409
  70.0 2.2 %collective-permute-start.14 = (bf16[656,256]{1,0:T(8,128)(2,1)S(1)}, bf16[656,256]{1,0:T(8,128)(2,1)S(1)}, u32[]{:S(2)}, u32[]{:S(2)}) collective-permute-start(bf16[656,256]{1,0:T(8,128)(2,1)S(1)} %get-tuple-element.167.refs_2_.refs_3_), channel_id=1, source_target_pairs={{0,1},{1,0},{2,3},{3,2},{4,5},{5,4},{6,7},{7,6},{8,9},{9,8},{10,11... | collective-permute-start | bytes 1007624 | tf_op jit(solution)/shard_map/ppermute | solution.py:409

commit v6 on v5

--- a/solution.py
+++ b/solution.py
@@ -130,8 +130,8 @@
 
 
 def grad_kernel(
-    pick_ref, flen_ref, tlen_ref, labels_ref, qa_ref, qb_ref, e_ref, st_ref, jt_ref,
-    d_ref, loss_ref, send_ref, keep_ref, d_scr, gb_scr, loss_scr, target_scr,
+    blocks, pick_ref, flen_ref, tlen_ref, labels_ref, qa_ref, qb_ref, e_ref, st_ref, jt_ref,
+    d_ref, loss_ref, send_ref, keep_ref, low_scr, high_scr, dw_scr, gb_scr, loss_scr, target_scr,
 ):
     step = pl.program_id(0)
     steps = pl.num_programs(0)
@@ -148,50 +148,65 @@
         column = target_column(labels_ref, token_len, tok_slots, block_frames)
         target_scr[...] = jnp.broadcast_to(column, (rows, LANES))
 
-    half_count = pick_ref[1]
-    q = jnp.where(pick_ref[0] < half_count, qa_ref[0].astype(F32), qb_ref[0].astype(F32))
-    cell = lax.broadcasted_iota(jnp.int32, (1, rows), 1)
-    frame = lax.div(cell, tok_slots) + step * block_frames
-    token = lax.rem(cell, tok_slots)
-    has_label = token < token_len
-    count = jnp.full((1, rows), frame_len * (token_len + 1), jnp.int32).astype(F32)
-    weight = jnp.where((frame < frame_len) & (token <= token_len), 1.0 / count, 0.0)
-    q_blank = q[0:1]
-    q_label = jnp.where(has_label, q[1:2], 0.0)
-    q_rest = q[2:3]
-    rest_sum = st_ref[0:1]
-    z_blank = st_ref[1:2]
-    z_label = st_ref[2:3]
-    e_blank = jnp.exp(z_blank)
-    e_label = jnp.exp(z_label)
-    total = rest_sum + e_blank + jnp.where(has_label, e_label, 0.0)
-    log_total = jnp.log(total)
-    cell_loss = -(
-        q_blank * (z_blank - log_total)
-        + q_label * (z_label - log_total)
-        + q_rest * (jnp.log(rest_sum) - log_total)
-    )
-    loss_scr[...] += cell_loss * weight
-    soft = weight * (q_blank + q_label + q_rest) / total
-    scale = soft - weight * q_rest / rest_sum
-    d_blank = soft * e_blank - weight * q_blank
-    d_label = soft * e_label - weight * q_label
-    place = lax.broadcasted_iota(jnp.int32, (8, rows), 0)
-    packed = jnp.where(place == 0, scale, jnp.where(place == 1, d_label, d_blank))
-    columns = packed.T
-    scale = jnp.broadcast_to(columns[:, 0:1], (rows, LANES))
-    d_label = jnp.broadcast_to(columns[:, 1:2], (rows, LANES))
-    lane = lax.broadcasted_iota(jnp.int32, (rows, LANES), 1)
-    base = pl.multiple_of(step * rows, rows)
-    for j in range(vocab // LANES):
-        cols = slice(j * LANES, (j + 1) * LANES)
-        d = jnp.where(lane + j * LANES == target_scr[...], d_label, e_ref[:, cols] * scale)
-        if j == 0:
-            d = jnp.where(lane == 0, columns[:, 2:3], d)
-        low = d.astype(BF16)
-        d_ref[:, cols] = low
-        d_scr[pl.ds(base, rows), cols] = low
-        gb_scr[:, cols] += jnp.sum(d.reshape(rows // 8, 8, LANES), axis=0)
+    def collapse(held_ref):
+        half_count = pick_ref[1]
+        q = jnp.where(pick_ref[0] < half_count, qa_ref[0].astype(F32), qb_ref[0].astype(F32))
+        cell = lax.broadcasted_iota(jnp.int32, (1, rows), 1)
+        frame = lax.div(cell, tok_slots) + step * block_frames
+        token = lax.rem(cell, tok_slots)
+        has_label = token < token_len
+        count = jnp.full((1, rows), frame_len * (token_len + 1), jnp.int32).astype(F32)
+        weight = jnp.where((frame < frame_len) & (token <= token_len), 1.0 / count, 0.0)
+        q_blank = q[0:1]
+        q_label = jnp.where(has_label, q[1:2], 0.0)
+        q_rest = q[2:3]
+        rest_sum = st_ref[0:1]
+        z_blank = st_ref[1:2]
+        z_label = st_ref[2:3]
+        e_blank = jnp.exp(z_blank)
+        e_label = jnp.exp(z_label)
+        total = rest_sum + e_blank + jnp.where(has_label, e_label, 0.0)
+        log_total = jnp.log(total)
+        cell_loss = -(
+            q_blank * (z_blank - log_total)
+            + q_label * (z_label - log_total)
+            + q_rest * (jnp.log(rest_sum) - log_total)
+        )
+        loss_scr[...] += cell_loss * weight
+        soft = weight * (q_blank + q_label + q_rest) / total
+        scale = soft - weight * q_rest / rest_sum
+        d_blank = soft * e_blank - weight * q_blank
+        d_label = soft * e_label - weight * q_label
+        place = lax.broadcasted_iota(jnp.int32, (8, rows), 0)
+        packed = jnp.where(place == 0, scale, jnp.where(place == 1, d_label, d_blank))
+        columns = packed.T
+        scale = jnp.broadcast_to(columns[:, 0:1], (rows, LANES))
+        d_label = jnp.broadcast_to(columns[:, 1:2], (rows, LANES))
+        lane = lax.broadcasted_iota(jnp.int32, (rows, LANES), 1)
+        for j in range(vocab // LANES):
+            cols = slice(j * LANES, (j + 1) * LANES)
+            d = jnp.where(lane + j * LANES == target_scr[...], d_label, e_ref[:, cols] * scale)
+            if j == 0:
+                d = jnp.where(lane == 0, columns[:, 2:3], d)
+            low = d.astype(BF16)
+            d_ref[:, cols] = low
+            held_ref[:, cols] = low
+            gb_scr[:, cols] += jnp.sum(d.reshape(rows // 8, 8, LANES), axis=0)
+
+    slots = (low_scr, high_scr)
+    last_ref = slots[(blocks - 1) % 2]
+
+    @pl.when(step == 0)
+    def _():
+        collapse(slots[0])
+
+    for block in range(1, blocks):
+
+        @pl.when(step == block)
+        def _(block=block):
+            dw = jnp.dot(jt_ref[...], slots[(block - 1) % 2][...], preferred_element_type=F32)
+            dw_scr[...] = dw if block == 1 else dw_scr[...] + dw
+            collapse(slots[block % 2])
 
     @pl.when(step == steps - 1)
     def _():
@@ -199,10 +214,14 @@
         part = vocab // 2
         core = pick_ref[2]
         col = pl.multiple_of((1 - core) * part, part)
-        dw = jnp.dot(jt_ref[...], d_scr[:, pl.ds(col, part)], preferred_element_type=F32)
+        dw = dw_scr[:, pl.ds(col, part)] + jnp.dot(
+            jt_ref[...], last_ref[:, pl.ds(col, part)], preferred_element_type=F32
+        )
         send_ref[:width, :] = dw.astype(BF16)
         col = pl.multiple_of(core * part, part)
-        keep_ref[:width, :] = jnp.dot(jt_ref[...], d_scr[:, pl.ds(col, part)], preferred_element_type=F32)
+        keep_ref[:width, :] = dw_scr[:, pl.ds(col, part)] + jnp.dot(
+            jt_ref[...], last_ref[:, pl.ds(col, part)], preferred_element_type=F32
+        )
         bias = jnp.sum(gb_scr[...], axis=0, keepdims=True)
         first, second = bias[:, :part], bias[:, part:]
         mine = jnp.where(core == 0, first, second)
@@ -323,33 +342,40 @@
     cells, vocab = e.shape
     width = jt.shape[0]
     part = vocab // 2
+    blocks = cells // rows
+
+    def at(i):
+        return jnp.minimum(i, blocks - 1)
+
     smem = pl.BlockSpec(memory_space=pltpu.SMEM)
     grid_spec = pltpu.PrefetchScalarGridSpec(
         num_scalar_prefetch=1,
-        grid=(cells // rows,),
+        grid=(blocks + 1,),
         in_specs=[
             smem, smem, whole(labels.shape),
-            pl.BlockSpec((1, 3, rows), lambda i, pick: (lax.rem(pick[0], pick[1]), 0, i)),
-            pl.BlockSpec((1, 3, rows), lambda i, pick: (lax.rem(pick[0], pick[1]), 0, i)),
-            pl.BlockSpec((rows, vocab), lambda i, pick: (i, 0)),
-            pl.BlockSpec((8, rows), lambda i, pick: (0, i)),
-            whole(jt.shape),
+            pl.BlockSpec((1, 3, rows), lambda i, pick: (lax.rem(pick[0], pick[1]), 0, at(i))),
+            pl.BlockSpec((1, 3, rows), lambda i, pick: (lax.rem(pick[0], pick[1]), 0, at(i))),
+            pl.BlockSpec((rows, vocab), lambda i, pick: (at(i), 0)),
+            pl.BlockSpec((8, rows), lambda i, pick: (0, at(i))),
+            pl.BlockSpec((width, rows), lambda i, pick: (0, jnp.maximum(i - 1, 0))),
         ],
         out_specs=[
-            pl.BlockSpec((rows, vocab), lambda i, pick: (i, 0)),
+            pl.BlockSpec((rows, vocab), lambda i, pick: (at(i), 0)),
             whole((1, 1)),
             whole((width + EXTRA, part)),
             whole((width + EXTRA, part)),
         ],
         scratch_shapes=[
-            pltpu.VMEM((cells, vocab), BF16),
+            pltpu.VMEM((rows, vocab), BF16),
+            pltpu.VMEM((rows, vocab), BF16),
+            pltpu.VMEM((width, vocab), F32),
             pltpu.VMEM((8, vocab), F32),
             pltpu.VMEM((1, rows), F32),
             pltpu.VMEM((rows, LANES), jnp.int32),
         ],
     )
     return pl.pallas_call(
-        grad_kernel,
+        functools.partial(grad_kernel, blocks),
         grid_spec=grid_spec,
         out_shape=[
             pltpu.HBM((cells, vocab), BF16),
@@ -387,6 +413,42 @@
     )(in_vmem(enc), in_vmem(pred), pltpu.with_memory_space_constraint(d_low, pltpu.HBM), in_vmem(w), *extra)
 
 
+def merge_kernel(even, odd, keep_ref, got_ref, acc_ref, send_ref, bias_ref):
+    own = lax.axis_index("dp")
+    mask = jnp.where((own & 1) == 0, even, odd)
+    side = jnp.where((own & mask) != 0, 1, 0)
+    count, part = acc_ref.shape
+    stay = pl.ds(pl.multiple_of(side * count, count), count)
+    leave = pl.ds(pl.multiple_of((1 - side) * count, count), count)
+    send_ref[:count, :] = (keep_ref[leave, :] + got_ref[leave, :].astype(F32)).astype(BF16)
+    acc_ref[...] = keep_ref[stay, :] + got_ref[stay, :].astype(F32)
+    rows = got_ref[2 * count :, :].astype(F32)
+    bias = keep_ref[2 * count : 2 * count + 1, :] + rows[0:1] + rows[1:2]
+    high = bias.astype(BF16).astype(F32)
+    low = (bias - high).astype(BF16).astype(F32)
+    bias_ref[...] = high + low
+    place = lax.broadcasted_iota(jnp.int32, (EXTRA, part), 0)
+    packed = jnp.where(place == 0, high, jnp.where(place == 1, low, 0.0))
+    send_ref[count:, :] = packed.astype(BF16)
+
+
+def merge(keep, got, even, odd):
+    rows, part = got.shape
+    count = (rows - EXTRA) // 2
+    return pl.pallas_call(
+        functools.partial(merge_kernel, even, odd),
+        grid=(1,),
+        in_specs=[whole(keep.shape), whole(got.shape)],
+        out_specs=[whole((count, part)), whole((count + EXTRA, part)), whole((1, part))],
+        out_shape=[
+            jax.ShapeDtypeStruct((count, part), F32),
+            jax.ShapeDtypeStruct((count + EXTRA, part), BF16),
+            jax.ShapeDtypeStruct((1, part), F32),
+        ],
+        compiler_params=params(12),
+    )(keep, got)
+
+
 def split_two(value):
     high = lax.reduce_precision(value, 8, 7)
     return high, lax.reduce_precision(value - high, 8, 7)
@@ -441,8 +503,6 @@
         filler = jnp.zeros((EXTRA - 2, high.shape[1]), BF16)
         return jnp.concatenate([high.astype(BF16), low.astype(BF16), filler], axis=0)
 
-    acc = keep[:width] + got[:width].astype(F32)
-    bias = keep[width : width + 1] + got_bias(got[width:])
     rest = masks[1:]
     even_order = rest
     odd_order = rest[1:2] + rest[:1] + rest[2:]
@@ -450,15 +510,18 @@
     sides = []
     count = width
     done = ()
+    acc, send, bias = merge(keep, got, *orders[0])
     for k, (even, odd) in enumerate(orders[:-1]):
-        high, low = split_two(bias)
         side = (own & jnp.where(core == 0, even, odd)) != 0
         sides.append(side)
         count //= 2
-        top, bottom = acc[:count], acc[count:]
-        send = jnp.where(side, top, bottom).astype(BF16)
-        acc = jnp.where(side, bottom, top)
-        send = jnp.concatenate([send, bias_rows(high, low)], axis=0)
+        if k:
+            high, low = split_two(bias)
+            top, bottom = acc[:count], acc[count:]
+            send = jnp.where(side, top, bottom).astype(BF16)
+            acc = jnp.where(side, bottom, top)
+            send = jnp.concatenate([send, bias_rows(high, low)], axis=0)
+            bias = high + low
         if k < 2:
             send, acc, d_low = lax.optimization_barrier((send, acc, d_low))
         got = exchange(send, even, odd)
@@ -468,7 +531,7 @@
             )
             got, done = lax.optimization_barrier((got, done))
         acc = acc + got[:count].astype(F32)
-        bias = (high + low) + got_bias(got[count:])
+        bias = bias + got_bias(got[count:])
     chains = range(CHAINS)
     span = part // CHAINS
     even, odd = orders[-1]

time: 74.2 us -> 72.1 us (0.972)
  other arithmetic: 3.19 us -> 1.7 us
    add x2 -> x1, other arithmetic: 1.29 us -> 0.01 us  [on_device(): bias = bias + got_bias(got[count:])]
    convert_element_type x4 -> x3, other arithmetic: 0.81 us -> 0.03 us  [bias_rows(): high.astype(BF16)]
    pallas_call x1 -> x2, Pallas kernels: 7.94 us -> 7.61 us  [the longest x1 7.45 us: gradients(): pl.pallas_call(functools.partial(grad_kernel, blocks), grid_spec=grid_spe...]
  transfers between devices with their start and end apart: 15 -> 15, of which waited for: 11 -> 11; matrix products, arithmetic and copies ran while one was open for 0% -> 1% of each run, Pallas kernels for 28% -> 28%
where the time goes in v6:
time: 72.1 us; the launch traced here: 71.8 us
  Pallas kernels  29.6 us (41%)
  waiting for transfers between devices  21.8 us (30%)
  starting transfers between devices  16.5 us (23%)
  between operations  2.11 us (3%)
  other arithmetic  1.7 us (2%)
    ppermute x15, waiting for transfers between devices, exchange(): return lax.ppermute(value, 'dp', pairs)  21.8 us
    ppermute x15, starting transfers between devices, exchange(): return lax.ppermute(value, 'dp', pairs)  16.5 us
    pallas_call x2, Pallas kernels, input_gradients(): pl.pallas_call(functools.partial(input_kernel, begin, last), grid=(cells...  8.12 us
    pallas_call x3, Pallas kernels, forward(): pl.pallas_call(functools.partial(forward_kernel, begin), grid=(blocks,),...  7.95 us
    pallas_call x1, Pallas kernels, gradients(): pl.pallas_call(functools.partial(grad_kernel, blocks), grid_spec=grid_spe...  7.45 us
    pallas_call x2, Pallas kernels, widen(): pl.pallas_call(final_kernel, grid_spec=pltpu.PrefetchScalarGridSpec(num_s...  3.34 us
    pallas_call x1, Pallas kernels, stage(): pl.pallas_call(stage_kernel, in_specs=[smem] + [anywhere] * len(arrays),...  2.62 us
  transfers between devices with their start and end apart: 15, of which 11 were waited for; matrix products, arithmetic and copies ran while one was open for 1% of the time, Pallas kernels for 28%

profile of v6, /device:TPU:0, one launch (start us, length us, event | category | flops | bytes accessed | tf_op | source)
XLA Modules:
  0.0 71.8 jit_solution(15739921331264088826)
XLA Ops:
  0.6 0.5 collective-permute-start
  1.2 2.6 %shard_map.128 = (bf16[640,1024]{1,0:T(8,128)(2,1)S(1)}, bf16[64,640]{1,0:T(8,128)(2,1)S(1)}, bf16[32,640]{1,0:T(8,128)(2,1)S(1)}, f32[1,1024]{1,0:T(1,128)S(1)}, s32[1,31]{1,0:T(1,128)S(1)}, /*index=5*/s32[3]{0:T(128)S(1)}) custom-call(s32[16]{0:T(128)} %assignment_ref.1, bf16[640,1024]{1,0:T(8,128)(2,1)} %refs_0_.1, bf16[64,640]{1,0:T(8,128)(2,1)} %bitcast.7, ...), custom_call_target="tpu_custom_call" | custom-call | tf_op jit(solution)/shard_map/pallas_call | solution.py:55
  3.8 0.7 %pad_maximum_fusion.6 = bf16[2,3,2048]{2,1,0:T(4,128)(2,1)S(1)} fusion(bf16[1,3,2048]{2,1,0:T(4,128)(2,1)S(1)} %collective-permute-done, bf16[1,3,2048]{2,1,0:T(4,128)(2,1)} %param.9), kind=kLoop, calls=%fused_computation.19 | loop fusion | flops 12288 | bytes 49152 | tf_op jit(solution)/shard_map/concatenate | solution.py:489
  4.5 2.6 %collective-permute-start.1 = (bf16[2,3,2048]{2,1,0:T(4,128)(2,1)S(1)}, bf16[2,3,2048]{2,1,0:T(4,128)(2,1)S(1)}, u32[]{:S(2)}, u32[]{:S(2)}) collective-permute-start(bf16[2,3,2048]{2,1,0:T(4,128)(2,1)S(1)} %pad_maximum_fusion.6), channel_id=1, source_target_pairs={{0,2},{1,3},{2,0},{3,1},{4,6},{5,7},{6,4},{7,5},{8,10},{9,11},{10,... | collective-permute-start | bytes 73736 | tf_op jit(solution)/shard_map/ppermute | solution.py:471
  7.8 1.9 %shard_map.129 = (f32[2048,1024]{1,0:T(8,128)S(1)}, f32[8,2048]{1,0:T(8,128)S(1)}, bf16[640,2048]{1,0:T(8,128)(2,1)S(1)}) custom-call(s32[1]{0:T(128)S(6)} %copy.33.tlen_ref, s32[1,31]{1,0:T(1,128)S(1)} %get-tuple-element.114.labels_ref, bf16[64,640]{1,0:T(8,128)(2,1)S(1)} %get-tuple-element.116.enc_ref, bf16[32,640]{1,0:T(8,128)(2,1)S(1)} %get-tuple-element.117.pred_ref, ...), custom_call_target="tpu_custom_call" | custom-call | tf_op jit(solution)/shard_map/pallas_call | solution.py:318
  9.8 1.6 %collective-permute-start.2 = (bf16[4,3,2048]{2,1,0:T(4,128)(2,1)S(1)}, bf16[4,3,2048]{2,1,0:T(4,128)(2,1)S(1)}, u32[]{:S(2)}, u32[]{:S(2)}) collective-permute-start(bf16[4,3,2048]{2,1,0:T(4,128)(2,1)S(1)} %pad_maximum_fusion.5), channel_id=1, source_target_pairs={{0,4},{1,5},{2,6},{3,7},{4,0},{5,1},{6,2},{7,3},{8,12},{9,13},{10,... | collective-permute-start | bytes 147464 | tf_op jit(solution)/shard_map/ppermute | solution.py:471
  11.4 1.9 %shard_map.130 = (f32[2048,1024]{1,0:T(8,128)S(1)}, f32[8,2048]{1,0:T(8,128)S(1)}, bf16[640,2048]{1,0:T(8,128)(2,1)S(1)}) custom-call(s32[1]{0:T(128)S(6)} %copy.33.tlen_ref, s32[1,31]{1,0:T(1,128)S(1)} %get-tuple-element.114.labels_ref, bf16[64,640]{1,0:T(8,128)(2,1)S(1)} %get-tuple-element.116.enc_ref, ...), custom_call_target="tpu_custom_call", output_to_operand_aliasing={{0}: (6, {}), {1}: (7, {}), {2}: (8, {})} | custom-call | tf_op jit(solution)/shard_map/pallas_call | solution.py:318
  13.3 0.8 %collective-permute-done.2 = bf16[4,3,2048]{2,1,0:T(4,128)(2,1)S(1)} collective-permute-done((bf16[4,3,2048]{2,1,0:T(4,128)(2,1)S(1)}, bf16[4,3,2048]{2,1,0:T(4,128)(2,1)S(1)}, u32[]{:S(2)}, u32[]{:S(2)}) %collective-permute-start.2) | collective-permute-done | bytes 49184 | tf_op jit(solution)/shard_map/ppermute | solution.py:471
  14.2 2.7 %collective-permute-start.3 = (bf16[8,3,2048]{2,1,0:T(4,128)(2,1)S(1)}, bf16[8,3,2048]{2,1,0:T(4,128)(2,1)S(1)}, u32[]{:S(2)}, u32[]{:S(2)}) collective-permute-start(bf16[8,3,2048]{2,1,0:T(4,128)(2,1)S(1)} %pad_maximum_fusion.2.qa_ref), channel_id=1, source_target_pairs={{0,8},{1,9},{2,10},{3,11},{4,12},{5,13},{6,14},{7,15},{8,0},{9,1},... | collective-permute-start | bytes 294920 | tf_op jit(solution)/shard_map/ppermute | solution.py:471
  17.5 4.1 %shard_map.131 = (f32[2048,1024]{1,0:T(8,128)S(1)}, f32[8,2048]{1,0:T(8,128)S(1)}, bf16[640,2048]{1,0:T(8,128)(2,1)S(1)}) custom-call(s32[1]{0:T(128)S(6)} %copy.33.tlen_ref, s32[1,31]{1,0:T(1,128)S(1)} %get-tuple-element.114.labels_ref, bf16[64,640]{1,0:T(8,128)(2,1)S(1)} %get-tuple-element.116.enc_ref, ...), custom_call_target="tpu_custom_call", output_to_operand_aliasing={{0}: (6, {}), {1}: (7, {}), {2}: (8, {})} | custom-call | tf_op jit(solution)/shard_map/pallas_call | solution.py:318
  21.6 1.0 %collective-permute-done.3.qb_ref = bf16[8,3,2048]{2,1,0:T(4,128)(2,1)S(1)} collective-permute-done((bf16[8,3,2048]{2,1,0:T(4,128)(2,1)S(1)}, bf16[8,3,2048]{2,1,0:T(4,128)(2,1)S(1)}, u32[]{:S(2)}, u32[]{:S(2)}) %collective-permute-start.3) | collective-permute-done | bytes 98336 | tf_op jit(solution)/shard_map/ppermute | solution.py:471
  22.5 7.4 %shard_map.132 = (bf16[2048,1024]{1,0:T(8,128)(2,1)}, f32[1,1]{1,0:T(1,128)}, bf16[656,512]{1,0:T(8,128)(2,1)S(1)}, f32[656,512]{1,0:T(8,128)S(1)}) custom-call(s32[3]{0:T(128)S(1)} %get-tuple-element.113.pick_ref, s32[1]{0:T(128)S(6)} %copy.32.flen_ref, s32[1]{0:T(128)S(6)} %copy.33.tlen_ref, s32[1,31]{1,0:T(1,128)S(1)} %get-tuple-element.114.labels_ref, ...), custom_call_target="tpu_custom_call" | custom-call | tf_op jit(solution)/shard_map/pallas_call | solution.py:377
  30.0 2.1 %collective-permute-done.4.got_ref = bf16[656,512]{1,0:T(8,128)(2,1)S(1)} collective-permute-done((bf16[656,512]{1,0:T(8,128)(2,1)S(1)}, bf16[656,512]{1,0:T(8,128)(2,1)S(1)}, u32[]{:S(2)}, u32[]{:S(2)}) %collective-permute-start.4) | collective-permute-done | bytes 671776 | tf_op jit(solution)/shard_map/ppermute | solution.py:471
  32.3 0.6 collective-permute-start.5
  33.0 4.1 %shard_map.134 = (bf16[64,640]{1,0:T(8,128)(2,1)}, f32[32,640]{1,0:T(8,128)S(1)}) custom-call(bf16[64,640]{1,0:T(8,128)(2,1)S(1)} %get-tuple-element.116.enc_ref, bf16[32,640]{1,0:T(8,128)(2,1)S(1)} %get-tuple-element.117.pred_ref, bf16[2048,1024]{1,0:T(8,128)(2,1)} %get-tuple-element.141.d_ref, bf16[640,1024]{1,0:T(8,128)(2,1)S(1)} %get-tuple-element.118.w_ref), custom_call_target="tpu_custom_call" | custom-call | tf_op jit(solution)/shard_map/pallas_call | solution.py:396
  37.0 2.6 %collective-permute-done.5 = bf16[336,512]{1,0:T(8,128)(2,1)S(1)} collective-permute-done((bf16[336,512]{1,0:T(8,128)(2,1)S(1)}, bf16[336,512]{1,0:T(8,128)(2,1)S(1)}, u32[]{:S(2)}, u32[]{:S(2)}) %collective-permute-start.5) | collective-permute-done | bytes 344096 | tf_op jit(solution)/shard_map/ppermute | solution.py:471
  39.9 0.8 %collective-permute-start.6 = (bf16[176,512]{1,0:T(8,128)(2,1)S(1)}, bf16[176,512]{1,0:T(8,128)(2,1)S(1)}, u32[]{:S(2)}, u32[]{:S(2)}) collective-permute-start(bf16[176,512]{1,0:T(8,128)(2,1)S(1)} %maximum_maximum_fusion), channel_id=1, source_target_pairs={{0,4},{1,3},{2,6},{3,1},{4,0},{5,7},{6,2},{7,5},{8,12},{9,11},{10,... | collective-permute-start | bytes 540680 | tf_op jit(solution)/shard_map/ppermute | solution.py:471
  40.7 4.1 %shard_map.135 = (bf16[64,640]{1,0:T(8,128)(2,1)}, bf16[32,640]{1,0:T(8,128)(2,1)}) custom-call(bf16[64,640]{1,0:T(8,128)(2,1)S(1)} %get-tuple-element.116.enc_ref, bf16[32,640]{1,0:T(8,128)(2,1)S(1)} %get-tuple-element.117.pred_ref, bf16[2048,1024]{1,0:T(8,128)(2,1)} %get-tuple-element.141.d_ref, ...), custom_call_target="tpu_custom_call", output_to_operand_aliasing={{0}: (5, {})} | custom-call | tf_op jit(solution)/shard_map/pallas_call | solution.py:396
  44.7 0.7 %collective-permute-done.6 = bf16[176,512]{1,0:T(8,128)(2,1)S(1)} collective-permute-done((bf16[176,512]{1,0:T(8,128)(2,1)S(1)}, bf16[176,512]{1,0:T(8,128)(2,1)S(1)}, u32[]{:S(2)}, u32[]{:S(2)}) %collective-permute-start.6) | collective-permute-done | bytes 180256 | tf_op jit(solution)/shard_map/ppermute | solution.py:471
  45.6 2.7 %collective-permute-start.8 = (bf16[176,256]{1,0:T(8,128)(2,1)S(1)}, bf16[176,256]{1,0:T(8,128)(2,1)S(1)}, u32[]{:S(2)}, u32[]{:S(2)}) collective-permute-start(bf16[176,256]{1,0:T(8,128)(2,1)S(1)} %get-tuple-element.174), channel_id=1, source_target_pairs={{0,8},{1,9},{2,10},{3,11},{4,12},{5,13},{6,14},{7,15},{8,0},{9,1},... | collective-permute-start | bytes 270344 | tf_op jit(solution)/shard_map/ppermute | solution.py:471
  48.6 4.8 %collective-permute-done.8 = bf16[176,256]{1,0:T(8,128)(2,1)S(1)} collective-permute-done((bf16[176,256]{1,0:T(8,128)(2,1)S(1)}, bf16[176,256]{1,0:T(8,128)(2,1)S(1)}, u32[]{:S(2)}, u32[]{:S(2)}) %collective-permute-start.8) | collective-permute-done | bytes 90144 | tf_op jit(solution)/shard_map/ppermute | solution.py:471
  53.4 1.9 %collective-permute-done.7 = bf16[176,256]{1,0:T(8,128)(2,1)S(1)} collective-permute-done((bf16[176,256]{1,0:T(8,128)(2,1)S(1)}, bf16[176,256]{1,0:T(8,128)(2,1)S(1)}, u32[]{:S(2)}, u32[]{:S(2)}) %collective-permute-start.7) | collective-permute-done | bytes 90144 | tf_op jit(solution)/shard_map/ppermute | solution.py:471
  55.4 2.0 %collective-permute-start.9 = (bf16[160,256]{1,0:T(8,128)(2,1)S(1)}, bf16[160,256]{1,0:T(8,128)(2,1)S(1)}, u32[]{:S(2)}, u32[]{:S(2)}) collective-permute-start(bf16[160,256]{1,0:T(8,128)(2,1)S(1)} %add_convert_fusion), channel_id=1, source_target_pairs={{0,4},{1,3},{2,6},{3,1},{4,0},{5,7},{6,2},{7,5},{8,12},{9,11},{10,... | collective-permute-start | bytes 245768 | tf_op jit(solution)/shard_map/ppermute | solution.py:471
  57.5 2.3 %collective-permute-done.10 = bf16[160,256]{1,0:T(8,128)(2,1)S(1)} collective-permute-done((bf16[160,256]{1,0:T(8,128)(2,1)S(1)}, bf16[160,256]{1,0:T(8,128)(2,1)S(1)}, u32[]{:S(2)}, u32[]{:S(2)}) %collective-permute-start.10) | collective-permute-done | bytes 81952 | tf_op jit(solution)/shard_map/ppermute | solution.py:471
  59.8 0.8 %collective-permute-done.9 = bf16[160,256]{1,0:T(8,128)(2,1)S(1)} collective-permute-done((bf16[160,256]{1,0:T(8,128)(2,1)S(1)}, bf16[160,256]{1,0:T(8,128)(2,1)S(1)}, u32[]{:S(2)}, u32[]{:S(2)}) %collective-permute-start.9) | collective-permute-done | bytes 81952 | tf_op jit(solution)/shard_map/ppermute | solution.py:471
  60.6 1.2 %collective-permute-start.12 = (bf16[320,256]{1,0:T(8,128)(2,1)S(1)}, bf16[320,256]{1,0:T(8,128)(2,1)S(1)}, u32[]{:S(2)}, u32[]{:S(2)}) collective-permute-start(bf16[320,256]{1,0:T(8,128)(2,1)S(1)} %maximum_select_fusion.2), channel_id=1, source_target_pairs={{0,2},{1,5},{2,0},{3,7},{4,6},{5,1},{6,4},{7,3},{8,10},{9,13},{10,... | collective-permute-start | bytes 491528 | tf_op jit(solution)/shard_map/ppermute | solution.py:471
  61.9 0.9 %collective-permute-start.11 = (bf16[320,256]{1,0:T(8,128)(2,1)S(1)}, bf16[320,256]{1,0:T(8,128)(2,1)S(1)}, u32[]{:S(2)}, u32[]{:S(2)}) collective-permute-start(bf16[320,256]{1,0:T(8,128)(2,1)S(1)} %maximum_select_fusion.3), channel_id=1, source_target_pairs={{0,2},{1,5},{2,0},{3,7},{4,6},{5,1},{6,4},{7,3},{8,10},{9,13},{10,... | collective-permute-start | bytes 491528 | tf_op jit(solution)/shard_map/ppermute | solution.py:471
  62.8 3.2 %collective-permute-done.12 = bf16[320,256]{1,0:T(8,128)(2,1)S(1)} collective-permute-done((bf16[320,256]{1,0:T(8,128)(2,1)S(1)}, bf16[320,256]{1,0:T(8,128)(2,1)S(1)}, u32[]{:S(2)}, u32[]{:S(2)}) %collective-permute-start.12) | collective-permute-done | bytes 163872 | tf_op jit(solution)/shard_map/ppermute | solution.py:471
  66.1 1.6 %collective-permute-done.11 = bf16[320,256]{1,0:T(8,128)(2,1)S(1)} collective-permute-done((bf16[320,256]{1,0:T(8,128)(2,1)S(1)}, bf16[320,256]{1,0:T(8,128)(2,1)S(1)}, u32[]{:S(2)}, u32[]{:S(2)}) %collective-permute-start.11) | collective-permute-done | bytes 163872 | tf_op jit(solution)/shard_map/ppermute | solution.py:471
  68.0 0.5 collective-permute-start.14
  68.5 1.7 %shard_map.136 = (f32[640,1024]{1,0:T(8,128)}, f32[1,1024]{1,0:T(1,128)}) custom-call(s32[3]{0:T(128)S(1)} %get-tuple-element.113.pick_ref, bf16[656,256]{1,0:T(8,128)(2,1)S(1)} %get-tuple-element.172.refs_0_.refs_1_, bf16[656,256]{1,0:T(8,128)(2,1)S(1)} %get-tuple-element.172.refs_0_.refs_1_, bf16[656,256]{1,0:T(8,128)(2,1)S(1)} %get-tuple-element.171.refs_2_.refs_3_, ...), custom_call_target="tpu_custom_call" | custom-call | tf_op jit(solution)/shard_map/pallas_call | solution.py:287
  70.2 1.7 %shard_map.137 = (f32[640,1024]{1,0:T(8,128)}, f32[1,1024]{1,0:T(1,128)}) custom-call(s32[3]{0:T(128)S(1)} %get-tuple-element.113.pick_ref, bf16[656,256]{1,0:T(8,128)(2,1)S(1)} %collective-permute-done.13.refs_0_.refs_1_, bf16[656,256]{1,0:T(8,128)(2,1)S(1)} %collective-permute-done.13.refs_0_.refs_1_, ...), custom_call_target="tpu_custom_call", output_to_operand_aliasing={{0}: (5, {}), {1}: (6, {})} | custom-call | tf_op jit(solution)/shard_map/pallas_call | solution.py:287
  (34 shorter events, 1.7 us)
Async XLA Ops:
  0.6 3.1 %collective-permute-start = (bf16[1,3,2048]{2,1,0:T(4,128)(2,1)}, bf16[1,3,2048]{2,1,0:T(4,128)(2,1)S(1)}, u32[]{:S(2)}, u32[]{:S(2)}) collective-permute-start(bf16[1,3,2048]{2,1,0:T(4,128)(2,1)} %param.9), channel_id=1, source_target_pairs={{0,1},{1,0},{2,3},{3,2},{4,5},{5,4},{6,7},{7,6},{8,9},{9,8},{10,11... | collective-permute-start | bytes 36872 | tf_op jit(solution)/shard_map/ppermute | solution.py:471
  4.5 5.2 %collective-permute-start.1 = (bf16[2,3,2048]{2,1,0:T(4,128)(2,1)S(1)}, bf16[2,3,2048]{2,1,0:T(4,128)(2,1)S(1)}, u32[]{:S(2)}, u32[]{:S(2)}) collective-permute-start(bf16[2,3,2048]{2,1,0:T(4,128)(2,1)S(1)} %pad_maximum_fusion.6), channel_id=1, source_target_pairs={{0,2},{1,3},{2,0},{3,1},{4,6},{5,7},{6,4},{7,5},{8,10},{9,11},{10,... | collective-permute-start | bytes 73736 | tf_op jit(solution)/shard_map/ppermute | solution.py:471
  9.8 4.3 %collective-permute-start.2 = (bf16[4,3,2048]{2,1,0:T(4,128)(2,1)S(1)}, bf16[4,3,2048]{2,1,0:T(4,128)(2,1)S(1)}, u32[]{:S(2)}, u32[]{:S(2)}) collective-permute-start(bf16[4,3,2048]{2,1,0:T(4,128)(2,1)S(1)} %pad_maximum_fusion.5), channel_id=1, source_target_pairs={{0,4},{1,5},{2,6},{3,7},{4,0},{5,1},{6,2},{7,3},{8,12},{9,13},{10,... | collective-permute-start | bytes 147464 | tf_op jit(solution)/shard_map/ppermute | solution.py:471
  14.2 8.4 %collective-permute-start.3 = (bf16[8,3,2048]{2,1,0:T(4,128)(2,1)S(1)}, bf16[8,3,2048]{2,1,0:T(4,128)(2,1)S(1)}, u32[]{:S(2)}, u32[]{:S(2)}) collective-permute-start(bf16[8,3,2048]{2,1,0:T(4,128)(2,1)S(1)} %pad_maximum_fusion.2.qa_ref), channel_id=1, source_target_pairs={{0,8},{1,9},{2,10},{3,11},{4,12},{5,13},{6,14},{7,15},{8,0},{9,1},... | collective-permute-start | bytes 294920 | tf_op jit(solution)/shard_map/ppermute | solution.py:471
  30.0 2.1 %collective-permute-start.4 = (bf16[656,512]{1,0:T(8,128)(2,1)S(1)}, bf16[656,512]{1,0:T(8,128)(2,1)S(1)}, u32[]{:S(2)}, u32[]{:S(2)}) collective-permute-start(bf16[656,512]{1,0:T(8,128)(2,1)S(1)} %get-tuple-element.128), channel_id=1, source_target_pairs={{0,1},{1,0},{2,3},{3,2},{4,5},{5,4},{6,7},{7,6},{8,9},{9,8},{10,11... | collective-permute-start | bytes 2015240 | tf_op jit(solution)/shard_map/ppermute | solution.py:471
  32.3 7.3 %collective-permute-start.5 = (bf16[336,512]{1,0:T(8,128)(2,1)S(1)}, bf16[336,512]{1,0:T(8,128)(2,1)S(1)}, u32[]{:S(2)}, u32[]{:S(2)}) collective-permute-start(bf16[336,512]{1,0:T(8,128)(2,1)S(1)} %get-tuple-element.133), channel_id=1, source_target_pairs={{0,2},{1,5},{2,0},{3,7},{4,6},{5,1},{6,4},{7,3},{8,10},{9,13},{10,... | collective-permute-start | bytes 1032200 | tf_op jit(solution)/shard_map/ppermute | solution.py:471
  39.9 5.6 %collective-permute-start.6 = (bf16[176,512]{1,0:T(8,128)(2,1)S(1)}, bf16[176,512]{1,0:T(8,128)(2,1)S(1)}, u32[]{:S(2)}, u32[]{:S(2)}) collective-permute-start(bf16[176,512]{1,0:T(8,128)(2,1)S(1)} %maximum_maximum_fusion), channel_id=1, source_target_pairs={{0,4},{1,3},{2,6},{3,1},{4,0},{5,7},{6,2},{7,5},{8,12},{9,11},{10,... | collective-permute-start | bytes 540680 | tf_op jit(solution)/shard_map/ppermute | solution.py:471
  45.6 7.8 %collective-permute-start.8 = (bf16[176,256]{1,0:T(8,128)(2,1)S(1)}, bf16[176,256]{1,0:T(8,128)(2,1)S(1)}, u32[]{:S(2)}, u32[]{:S(2)}) collective-permute-start(bf16[176,256]{1,0:T(8,128)(2,1)S(1)} %get-tuple-element.174), channel_id=1, source_target_pairs={{0,8},{1,9},{2,10},{3,11},{4,12},{5,13},{6,14},{7,15},{8,0},{9,1},... | collective-permute-start | bytes 270344 | tf_op jit(solution)/shard_map/ppermute | solution.py:471
  48.3 7.0 %collective-permute-start.7 = (bf16[176,256]{1,0:T(8,128)(2,1)S(1)}, bf16[176,256]{1,0:T(8,128)(2,1)S(1)}, u32[]{:S(2)}, u32[]{:S(2)}) collective-permute-start(bf16[176,256]{1,0:T(8,128)(2,1)S(1)} %get-tuple-element.173), channel_id=1, source_target_pairs={{0,8},{1,9},{2,10},{3,11},{4,12},{5,13},{6,14},{7,15},{8,0},{9,1},... | collective-permute-start | bytes 270344 | tf_op jit(solution)/shard_map/ppermute | solution.py:471
  55.3 4.4 %collective-permute-start.10 = (bf16[160,256]{1,0:T(8,128)(2,1)S(1)}, bf16[160,256]{1,0:T(8,128)(2,1)S(1)}, u32[]{:S(2)}, u32[]{:S(2)}) collective-permute-start(bf16[160,256]{1,0:T(8,128)(2,1)S(1)} %add_convert_fusion.1), channel_id=1, source_target_pairs={{0,4},{1,3},{2,6},{3,1},{4,0},{5,7},{6,2},{7,5},{8,12},{9,11},{10,... | collective-permute-start | bytes 245768 | tf_op jit(solution)/shard_map/ppermute | solution.py:471
  55.4 5.2 %collective-permute-start.9 = (bf16[160,256]{1,0:T(8,128)(2,1)S(1)}, bf16[160,256]{1,0:T(8,128)(2,1)S(1)}, u32[]{:S(2)}, u32[]{:S(2)}) collective-permute-start(bf16[160,256]{1,0:T(8,128)(2,1)S(1)} %add_convert_fusion), channel_id=1, source_target_pairs={{0,4},{1,3},{2,6},{3,1},{4,0},{5,7},{6,2},{7,5},{8,12},{9,11},{10,... | collective-permute-start | bytes 245768 | tf_op jit(solution)/shard_map/ppermute | solution.py:471
  60.6 5.3 %collective-permute-start.12 = (bf16[320,256]{1,0:T(8,128)(2,1)S(1)}, bf16[320,256]{1,0:T(8,128)(2,1)S(1)}, u32[]{:S(2)}, u32[]{:S(2)}) collective-permute-start(bf16[320,256]{1,0:T(8,128)(2,1)S(1)} %maximum_select_fusion.2), channel_id=1, source_target_pairs={{0,2},{1,5},{2,0},{3,7},{4,6},{5,1},{6,4},{7,3},{8,10},{9,13},{10,... | collective-permute-start | bytes 491528 | tf_op jit(solution)/shard_map/ppermute | solution.py:471
  61.9 5.8 %collective-permute-start.11 = (bf16[320,256]{1,0:T(8,128)(2,1)S(1)}, bf16[320,256]{1,0:T(8,128)(2,1)S(1)}, u32[]{:S(2)}, u32[]{:S(2)}) collective-permute-start(bf16[320,256]{1,0:T(8,128)(2,1)S(1)} %maximum_select_fusion.3), channel_id=1, source_target_pairs={{0,2},{1,5},{2,0},{3,7},{4,6},{5,1},{6,4},{7,3},{8,10},{9,13},{10,... | collective-permute-start | bytes 491528 | tf_op jit(solution)/shard_map/ppermute | solution.py:471
  67.9 2.2 %collective-permute-start.13 = (bf16[656,256]{1,0:T(8,128)(2,1)S(1)}, bf16[656,256]{1,0:T(8,128)(2,1)S(1)}, u32[]{:S(2)}, u32[]{:S(2)}) collective-permute-start(bf16[656,256]{1,0:T(8,128)(2,1)S(1)} %get-tuple-element.172.refs_0_.refs_1_), channel_id=1, source_target_pairs={{0,1},{1,0},{2,3},{3,2},{4,5},{5,4},{6,7},{7,6},{8,9},{9,8},{10,11... | collective-permute-start | bytes 1007624 | tf_op jit(solution)/shard_map/ppermute | solution.py:471
  68.0 2.2 %collective-permute-start.14 = (bf16[656,256]{1,0:T(8,128)(2,1)S(1)}, bf16[656,256]{1,0:T(8,128)(2,1)S(1)}, u32[]{:S(2)}, u32[]{:S(2)}) collective-permute-start(bf16[656,256]{1,0:T(8,128)(2,1)S(1)} %get-tuple-element.171.refs_2_.refs_3_), channel_id=1, source_target_pairs={{0,1},{1,0},{2,3},{3,2},{4,5},{5,4},{6,7},{7,6},{8,9},{9,8},{10,11... | collective-permute-start | bytes 1007624 | tf_op jit(solution)/shard_map/ppermute | solution.py:471

commit v7 on v6

--- a/solution.py
+++ b/solution.py
@@ -33,19 +33,23 @@
 
 
 def stage_kernel(assignment_ref, *refs):
-    count = (len(refs) - 2) // 2
-    sources, targets, pick_ref, sems = refs[:count], refs[count : 2 * count], refs[-2], refs[-1]
+    count = (len(refs) - 3) // 2
+    sources, targets = refs[:count], refs[count : 2 * count]
+    pick_ref, order_ref, sems = refs[2 * count :]
     copies = [
         pltpu.make_async_copy(source, target, sems.at[k])
-        for k, (source, target) in enumerate(zip(sources, targets))
+        for k, (source, target) in enumerate(
+            zip((assignment_ref, *sources), (order_ref, *targets))
+        )
     ]
     for copy in copies:
         copy.start()
     own = lax.axis_index("dp")
-    pick_ref[0] = assignment_ref[own] ^ own
+    copies[0].wait()
+    pick_ref[0] = order_ref[own] ^ own
     pick_ref[1] = assignment_ref.shape[0] // 2
     pick_ref[2] = own & 1
-    for copy in copies:
+    for copy in copies[1:]:
         copy.wait()
 
 
@@ -54,11 +58,13 @@
     smem = pl.BlockSpec(memory_space=pltpu.SMEM)
     return pl.pallas_call(
         stage_kernel,
-        in_specs=[smem] + [anywhere] * len(arrays),
+        in_specs=[anywhere] * (1 + len(arrays)),
         out_specs=[anywhere] * len(arrays) + [smem],
         out_shape=[jax.ShapeDtypeStruct(x.shape, x.dtype) for x in arrays]
         + [jax.ShapeDtypeStruct((3,), jnp.int32)],
-        scratch_shapes=[pltpu.SemaphoreType.DMA((len(arrays),))],
+        scratch_shapes=[
+            pltpu.SMEM(assignment.shape, jnp.int32), pltpu.SemaphoreType.DMA((1 + len(arrays),))
+        ],
         compiler_params=pltpu.CompilerParams(vmem_limit_bytes=4 * 1024 * 1024),
     )(*[pltpu.with_memory_space_constraint(x, pltpu.HBM) for x in (assignment, *arrays)])
 
@@ -475,7 +481,8 @@
     shares = [(0, quarter), (quarter, quarter), (2 * quarter, blocks - 2 * quarter)]
     held, made = teacher_post, ()
     staged = stage(
-        assignment, out_weight, encoder_out[0], predictor_out[0], out_bias.reshape(1, vocab), labels
+        assignment, out_weight, encoder_out[0], predictor_out[0], out_bias.reshape(1, vocab), labels,
+        teacher_post,
     )
     for k, mask in enumerate(masks):
         got = exchange(held, mask, mask)
@@ -485,10 +492,13 @@
             made = tuple(forward(
                 token_lengths, label_row, enc, pred, weight, bias_row, rows, begin, number, made
             ))
+        if k == 0:
+            got, staged = lax.optimization_barrier((got, staged))
+            held = staged[5]
         if k < len(masks) - 1:
             held = jnp.concatenate([held, got], axis=0)
             held, made, staged = lax.optimization_barrier((held, made, staged))
-            weight, enc, pred, bias_row, label_row, pick = staged
+            weight, enc, pred, bias_row, label_row, _, pick = staged
     far = got
     e, st, jt = made
     d_low, loss, send, keep = gradients(

time: 72.1 us -> 70.7 us (0.981)
  no operation moved by 1% of the time
where the time goes in v7:
time: 70.7 us; the launch traced here: 70.5 us
  Pallas kernels  29 us (41%)
  waiting for transfers between devices  21.8 us (31%)
  starting transfers between devices  16.5 us (23%)
  between operations  2.12 us (3%)
  other arithmetic  0.99 us (1%)
    ppermute x15, waiting for transfers between devices, exchange(): return lax.ppermute(value, 'dp', pairs)  21.8 us
    ppermute x15, starting transfers between devices, exchange(): return lax.ppermute(value, 'dp', pairs)  16.5 us
    pallas_call x2, Pallas kernels, input_gradients(): pl.pallas_call(functools.partial(input_kernel, begin, last), grid=(cells...  8.12 us
    pallas_call x3, Pallas kernels, forward(): pl.pallas_call(functools.partial(forward_kernel, begin), grid=(blocks,),...  7.95 us
    pallas_call x1, Pallas kernels, gradients(): pl.pallas_call(functools.partial(grad_kernel, blocks), grid_spec=grid_spe...  7.45 us
    pallas_call x2, Pallas kernels, widen(): pl.pallas_call(final_kernel, grid_spec=pltpu.PrefetchScalarGridSpec(num_s...  3.34 us
    pallas_call x1, Pallas kernels, stage(): pl.pallas_call(stage_kernel, in_specs=[anywhere] * (1 + len(arrays)), out...  1.98 us
  transfers between devices with their start and end apart: 15, of which 11 were waited for; matrix products, arithmetic and copies ran while one was open for 1% of the time, Pallas kernels for 28%

profile of v7, /device:TPU:0, one launch (start us, length us, event | category | flops | bytes accessed | tf_op | source)
XLA Modules:
  0.0 70.5 jit_solution(12469227582022622792)
XLA Ops:
  0.6 0.5 collective-permute-start
  1.2 2.0 %shard_map.128 = (bf16[640,1024]{1,0:T(8,128)(2,1)S(1)}, bf16[64,640]{1,0:T(8,128)(2,1)S(1)}, bf16[32,640]{1,0:T(8,128)(2,1)S(1)}, f32[1,1024]{1,0:T(1,128)S(1)}...) custom-call(s32[16]{0:T(128)} %assignment_ref.1, bf16[640,1024]{1,0:T(8,128)(2,1)} %refs_0_.1, ...), custom_call_target="tpu_custom_call" | custom-call | tf_op jit(solution)/shard_map/pallas_call | solution.py:59
  3.2 2.6 %collective-permute-start.1 = (bf16[2,3,2048]{2,1,0:T(4,128)(2,1)S(1)}, bf16[2,3,2048]{2,1,0:T(4,128)(2,1)S(1)}, u32[]{:S(2)}, u32[]{:S(2)}) collective-permute-start(bf16[2,3,2048]{2,1,0:T(4,128)(2,1)S(1)} %pad_maximum_fusion.6), channel_id=1, source_target_pairs={{0,2},{1,3},{2,0},{3,1},{4,6},{5,7},{6,4},{7,5},{8,10},{9,11},{10,... | collective-permute-start | bytes 73736 | tf_op jit(solution)/shard_map/ppermute | solution.py:477
  6.4 1.9 %shard_map.129 = (f32[2048,1024]{1,0:T(8,128)S(1)}, f32[8,2048]{1,0:T(8,128)S(1)}, bf16[640,2048]{1,0:T(8,128)(2,1)S(1)}) custom-call(s32[1]{0:T(128)S(6)} %copy.33.tlen_ref, s32[1,31]{1,0:T(1,128)S(1)} %get-tuple-element.132.labels_ref, bf16[64,640]{1,0:T(8,128)(2,1)S(1)} %get-tuple-element.134.enc_ref, bf16[32,640]{1,0:T(8,128)(2,1)S(1)} %get-tuple-element.135.pred_ref, ...), custom_call_target="tpu_custom_call" | custom-call | tf_op jit(solution)/shard_map/pallas_call | solution.py:324
  8.4 1.6 %collective-permute-start.2 = (bf16[4,3,2048]{2,1,0:T(4,128)(2,1)S(1)}, bf16[4,3,2048]{2,1,0:T(4,128)(2,1)S(1)}, u32[]{:S(2)}, u32[]{:S(2)}) collective-permute-start(bf16[4,3,2048]{2,1,0:T(4,128)(2,1)S(1)} %pad_maximum_fusion.5), channel_id=1, source_target_pairs={{0,4},{1,5},{2,6},{3,7},{4,0},{5,1},{6,2},{7,3},{8,12},{9,13},{10,... | collective-permute-start | bytes 147464 | tf_op jit(solution)/shard_map/ppermute | solution.py:477
  10.0 1.9 %shard_map.130 = (f32[2048,1024]{1,0:T(8,128)S(1)}, f32[8,2048]{1,0:T(8,128)S(1)}, bf16[640,2048]{1,0:T(8,128)(2,1)S(1)}) custom-call(s32[1]{0:T(128)S(6)} %copy.33.tlen_ref, s32[1,31]{1,0:T(1,128)S(1)} %get-tuple-element.132.labels_ref, bf16[64,640]{1,0:T(8,128)(2,1)S(1)} %get-tuple-element.134.enc_ref, ...), custom_call_target="tpu_custom_call", output_to_operand_aliasing={{0}: (6, {}), {1}: (7, {}), {2}: (8, {})} | custom-call | tf_op jit(solution)/shard_map/pallas_call | solution.py:324
  12.0 0.8 %collective-permute-done.2 = bf16[4,3,2048]{2,1,0:T(4,128)(2,1)S(1)} collective-permute-done((bf16[4,3,2048]{2,1,0:T(4,128)(2,1)S(1)}, bf16[4,3,2048]{2,1,0:T(4,128)(2,1)S(1)}, u32[]{:S(2)}, u32[]{:S(2)}) %collective-permute-start.2) | collective-permute-done | bytes 49184 | tf_op jit(solution)/shard_map/ppermute | solution.py:477
  12.8 2.7 %collective-permute-start.3 = (bf16[8,3,2048]{2,1,0:T(4,128)(2,1)S(1)}, bf16[8,3,2048]{2,1,0:T(4,128)(2,1)S(1)}, u32[]{:S(2)}, u32[]{:S(2)}) collective-permute-start(bf16[8,3,2048]{2,1,0:T(4,128)(2,1)S(1)} %pad_maximum_fusion.2.qa_ref), channel_id=1, source_target_pairs={{0,8},{1,9},{2,10},{3,11},{4,12},{5,13},{6,14},{7,15},{8,0},{9,1},... | collective-permute-start | bytes 294920 | tf_op jit(solution)/shard_map/ppermute | solution.py:477
  16.1 4.1 %shard_map.131 = (f32[2048,1024]{1,0:T(8,128)S(1)}, f32[8,2048]{1,0:T(8,128)S(1)}, bf16[640,2048]{1,0:T(8,128)(2,1)S(1)}) custom-call(s32[1]{0:T(128)S(6)} %copy.33.tlen_ref, s32[1,31]{1,0:T(1,128)S(1)} %get-tuple-element.132.labels_ref, bf16[64,640]{1,0:T(8,128)(2,1)S(1)} %get-tuple-element.134.enc_ref, ...), custom_call_target="tpu_custom_call", output_to_operand_aliasing={{0}: (6, {}), {1}: (7, {}), {2}: (8, {})} | custom-call | tf_op jit(solution)/shard_map/pallas_call | solution.py:324
  20.2 1.0 %collective-permute-done.3.qb_ref = bf16[8,3,2048]{2,1,0:T(4,128)(2,1)S(1)} collective-permute-done((bf16[8,3,2048]{2,1,0:T(4,128)(2,1)S(1)}, bf16[8,3,2048]{2,1,0:T(4,128)(2,1)S(1)}, u32[]{:S(2)}, u32[]{:S(2)}) %collective-permute-start.3) | collective-permute-done | bytes 98336 | tf_op jit(solution)/shard_map/ppermute | solution.py:477
  21.2 7.4 %shard_map.132 = (bf16[2048,1024]{1,0:T(8,128)(2,1)}, f32[1,1]{1,0:T(1,128)}, bf16[656,512]{1,0:T(8,128)(2,1)S(1)}, f32[656,512]{1,0:T(8,128)S(1)}) custom-call(s32[3]{0:T(128)S(1)} %get-tuple-element.131.pick_ref, s32[1]{0:T(128)S(6)} %copy.32.flen_ref, s32[1]{0:T(128)S(6)} %copy.33.tlen_ref, s32[1,31]{1,0:T(1,128)S(1)} %get-tuple-element.132.labels_ref, ...), custom_call_target="tpu_custom_call" | custom-call | tf_op jit(solution)/shard_map/pallas_call | solution.py:383
  28.6 2.1 %collective-permute-done.4.got_ref = bf16[656,512]{1,0:T(8,128)(2,1)S(1)} collective-permute-done((bf16[656,512]{1,0:T(8,128)(2,1)S(1)}, bf16[656,512]{1,0:T(8,128)(2,1)S(1)}, u32[]{:S(2)}, u32[]{:S(2)}) %collective-permute-start.4) | collective-permute-done | bytes 671776 | tf_op jit(solution)/shard_map/ppermute | solution.py:477
  30.9 0.6 collective-permute-start.5
  31.6 4.1 %shard_map.134 = (bf16[64,640]{1,0:T(8,128)(2,1)}, f32[32,640]{1,0:T(8,128)S(1)}) custom-call(bf16[64,640]{1,0:T(8,128)(2,1)S(1)} %get-tuple-element.134.enc_ref, bf16[32,640]{1,0:T(8,128)(2,1)S(1)} %get-tuple-element.135.pred_ref, bf16[2048,1024]{1,0:T(8,128)(2,1)} %get-tuple-element.159.d_ref, bf16[640,1024]{1,0:T(8,128)(2,1)S(1)} %get-tuple-element.136.w_ref), custom_call_target="tpu_custom_call" | custom-call | tf_op jit(solution)/shard_map/pallas_call | solution.py:402
  35.7 2.6 %collective-permute-done.5 = bf16[336,512]{1,0:T(8,128)(2,1)S(1)} collective-permute-done((bf16[336,512]{1,0:T(8,128)(2,1)S(1)}, bf16[336,512]{1,0:T(8,128)(2,1)S(1)}, u32[]{:S(2)}, u32[]{:S(2)}) %collective-permute-start.5) | collective-permute-done | bytes 344096 | tf_op jit(solution)/shard_map/ppermute | solution.py:477
  38.6 0.8 %collective-permute-start.6 = (bf16[176,512]{1,0:T(8,128)(2,1)S(1)}, bf16[176,512]{1,0:T(8,128)(2,1)S(1)}, u32[]{:S(2)}, u32[]{:S(2)}) collective-permute-start(bf16[176,512]{1,0:T(8,128)(2,1)S(1)} %maximum_maximum_fusion), channel_id=1, source_target_pairs={{0,4},{1,3},{2,6},{3,1},{4,0},{5,7},{6,2},{7,5},{8,12},{9,11},{10,... | collective-permute-start | bytes 540680 | tf_op jit(solution)/shard_map/ppermute | solution.py:477
  39.3 4.1 %shard_map.135 = (bf16[64,640]{1,0:T(8,128)(2,1)}, bf16[32,640]{1,0:T(8,128)(2,1)}) custom-call(bf16[64,640]{1,0:T(8,128)(2,1)S(1)} %get-tuple-element.134.enc_ref, bf16[32,640]{1,0:T(8,128)(2,1)S(1)} %get-tuple-element.135.pred_ref, bf16[2048,1024]{1,0:T(8,128)(2,1)} %get-tuple-element.159.d_ref, ...), custom_call_target="tpu_custom_call", output_to_operand_aliasing={{0}: (5, {})} | custom-call | tf_op jit(solution)/shard_map/pallas_call | solution.py:402
  43.4 0.7 %collective-permute-done.6 = bf16[176,512]{1,0:T(8,128)(2,1)S(1)} collective-permute-done((bf16[176,512]{1,0:T(8,128)(2,1)S(1)}, bf16[176,512]{1,0:T(8,128)(2,1)S(1)}, u32[]{:S(2)}, u32[]{:S(2)}) %collective-permute-start.6) | collective-permute-done | bytes 180256 | tf_op jit(solution)/shard_map/ppermute | solution.py:477
  44.3 2.7 %collective-permute-start.8 = (bf16[176,256]{1,0:T(8,128)(2,1)S(1)}, bf16[176,256]{1,0:T(8,128)(2,1)S(1)}, u32[]{:S(2)}, u32[]{:S(2)}) collective-permute-start(bf16[176,256]{1,0:T(8,128)(2,1)S(1)} %get-tuple-element.192), channel_id=1, source_target_pairs={{0,8},{1,9},{2,10},{3,11},{4,12},{5,13},{6,14},{7,15},{8,0},{9,1},... | collective-permute-start | bytes 270344 | tf_op jit(solution)/shard_map/ppermute | solution.py:477
  46.9 0.3 collective-permute-start.7
  47.2 4.8 %collective-permute-done.8 = bf16[176,256]{1,0:T(8,128)(2,1)S(1)} collective-permute-done((bf16[176,256]{1,0:T(8,128)(2,1)S(1)}, bf16[176,256]{1,0:T(8,128)(2,1)S(1)}, u32[]{:S(2)}, u32[]{:S(2)}) %collective-permute-start.8) | collective-permute-done | bytes 90144 | tf_op jit(solution)/shard_map/ppermute | solution.py:477
  52.1 1.9 %collective-permute-done.7 = bf16[176,256]{1,0:T(8,128)(2,1)S(1)} collective-permute-done((bf16[176,256]{1,0:T(8,128)(2,1)S(1)}, bf16[176,256]{1,0:T(8,128)(2,1)S(1)}, u32[]{:S(2)}, u32[]{:S(2)}) %collective-permute-start.7) | collective-permute-done | bytes 90144 | tf_op jit(solution)/shard_map/ppermute | solution.py:477
  54.1 2.0 %collective-permute-start.9 = (bf16[160,256]{1,0:T(8,128)(2,1)S(1)}, bf16[160,256]{1,0:T(8,128)(2,1)S(1)}, u32[]{:S(2)}, u32[]{:S(2)}) collective-permute-start(bf16[160,256]{1,0:T(8,128)(2,1)S(1)} %add_convert_fusion), channel_id=1, source_target_pairs={{0,4},{1,3},{2,6},{3,1},{4,0},{5,7},{6,2},{7,5},{8,12},{9,11},{10,... | collective-permute-start | bytes 245768 | tf_op jit(solution)/shard_map/ppermute | solution.py:477
  56.1 2.3 %collective-permute-done.10 = bf16[160,256]{1,0:T(8,128)(2,1)S(1)} collective-permute-done((bf16[160,256]{1,0:T(8,128)(2,1)S(1)}, bf16[160,256]{1,0:T(8,128)(2,1)S(1)}, u32[]{:S(2)}, u32[]{:S(2)}) %collective-permute-start.10) | collective-permute-done | bytes 81952 | tf_op jit(solution)/shard_map/ppermute | solution.py:477
  58.5 0.8 %collective-permute-done.9 = bf16[160,256]{1,0:T(8,128)(2,1)S(1)} collective-permute-done((bf16[160,256]{1,0:T(8,128)(2,1)S(1)}, bf16[160,256]{1,0:T(8,128)(2,1)S(1)}, u32[]{:S(2)}, u32[]{:S(2)}) %collective-permute-start.9) | collective-permute-done | bytes 81952 | tf_op jit(solution)/shard_map/ppermute | solution.py:477
  59.3 1.2 %collective-permute-start.12 = (bf16[320,256]{1,0:T(8,128)(2,1)S(1)}, bf16[320,256]{1,0:T(8,128)(2,1)S(1)}, u32[]{:S(2)}, u32[]{:S(2)}) collective-permute-start(bf16[320,256]{1,0:T(8,128)(2,1)S(1)} %maximum_select_fusion.2), channel_id=1, source_target_pairs={{0,2},{1,5},{2,0},{3,7},{4,6},{5,1},{6,4},{7,3},{8,10},{9,13},{10,... | collective-permute-start | bytes 491528 | tf_op jit(solution)/shard_map/ppermute | solution.py:477
  60.5 0.9 %collective-permute-start.11 = (bf16[320,256]{1,0:T(8,128)(2,1)S(1)}, bf16[320,256]{1,0:T(8,128)(2,1)S(1)}, u32[]{:S(2)}, u32[]{:S(2)}) collective-permute-start(bf16[320,256]{1,0:T(8,128)(2,1)S(1)} %maximum_select_fusion.3), channel_id=1, source_target_pairs={{0,2},{1,5},{2,0},{3,7},{4,6},{5,1},{6,4},{7,3},{8,10},{9,13},{10,... | collective-permute-start | bytes 491528 | tf_op jit(solution)/shard_map/ppermute | solution.py:477
  61.4 3.2 %collective-permute-done.12 = bf16[320,256]{1,0:T(8,128)(2,1)S(1)} collective-permute-done((bf16[320,256]{1,0:T(8,128)(2,1)S(1)}, bf16[320,256]{1,0:T(8,128)(2,1)S(1)}, u32[]{:S(2)}, u32[]{:S(2)}) %collective-permute-start.12) | collective-permute-done | bytes 163872 | tf_op jit(solution)/shard_map/ppermute | solution.py:477
  64.7 1.6 %collective-permute-done.11 = bf16[320,256]{1,0:T(8,128)(2,1)S(1)} collective-permute-done((bf16[320,256]{1,0:T(8,128)(2,1)S(1)}, bf16[320,256]{1,0:T(8,128)(2,1)S(1)}, u32[]{:S(2)}, u32[]{:S(2)}) %collective-permute-start.11) | collective-permute-done | bytes 163872 | tf_op jit(solution)/shard_map/ppermute | solution.py:477
  66.6 0.5 collective-permute-start.14
  67.1 1.7 %shard_map.136 = (f32[640,1024]{1,0:T(8,128)}, f32[1,1024]{1,0:T(1,128)}) custom-call(s32[3]{0:T(128)S(1)} %get-tuple-element.131.pick_ref, bf16[656,256]{1,0:T(8,128)(2,1)S(1)} %get-tuple-element.190.refs_0_.refs_1_, bf16[656,256]{1,0:T(8,128)(2,1)S(1)} %get-tuple-element.190.refs_0_.refs_1_, bf16[656,256]{1,0:T(8,128)(2,1)S(1)} %get-tuple-element.189.refs_2_.refs_3_, ...), custom_call_target="tpu_custom_call" | custom-call | tf_op jit(solution)/shard_map/pallas_call | solution.py:293
  68.8 1.7 %shard_map.137 = (f32[640,1024]{1,0:T(8,128)}, f32[1,1024]{1,0:T(1,128)}) custom-call(s32[3]{0:T(128)S(1)} %get-tuple-element.131.pick_ref, bf16[656,256]{1,0:T(8,128)(2,1)S(1)} %collective-permute-done.13.refs_0_.refs_1_, bf16[656,256]{1,0:T(8,128)(2,1)S(1)} %collective-permute-done.13.refs_0_.refs_1_, ...), custom_call_target="tpu_custom_call", output_to_operand_aliasing={{0}: (5, {}), {1}: (6, {})} | custom-call | tf_op jit(solution)/shard_map/pallas_call | solution.py:293
  (34 shorter events, 1.4 us)
Async XLA Ops:
  0.6 2.5 %collective-permute-start = (bf16[1,3,2048]{2,1,0:T(4,128)(2,1)}, bf16[1,3,2048]{2,1,0:T(4,128)(2,1)S(1)}, u32[]{:S(2)}, u32[]{:S(2)}) collective-permute-start(bf16[1,3,2048]{2,1,0:T(4,128)(2,1)} %refs_5_.1), channel_id=1, source_target_pairs={{0,1},{1,0},{2,3},{3,2},{4,5},{5,4},{6,7},{7,6},{8,9},{9,8},{10,11... | collective-permute-start | bytes 36872 | tf_op jit(solution)/shard_map/ppermute | solution.py:477
  3.2 5.2 %collective-permute-start.1 = (bf16[2,3,2048]{2,1,0:T(4,128)(2,1)S(1)}, bf16[2,3,2048]{2,1,0:T(4,128)(2,1)S(1)}, u32[]{:S(2)}, u32[]{:S(2)}) collective-permute-start(bf16[2,3,2048]{2,1,0:T(4,128)(2,1)S(1)} %pad_maximum_fusion.6), channel_id=1, source_target_pairs={{0,2},{1,3},{2,0},{3,1},{4,6},{5,7},{6,4},{7,5},{8,10},{9,11},{10,... | collective-permute-start | bytes 73736 | tf_op jit(solution)/shard_map/ppermute | solution.py:477
  8.4 4.3 %collective-permute-start.2 = (bf16[4,3,2048]{2,1,0:T(4,128)(2,1)S(1)}, bf16[4,3,2048]{2,1,0:T(4,128)(2,1)S(1)}, u32[]{:S(2)}, u32[]{:S(2)}) collective-permute-start(bf16[4,3,2048]{2,1,0:T(4,128)(2,1)S(1)} %pad_maximum_fusion.5), channel_id=1, source_target_pairs={{0,4},{1,5},{2,6},{3,7},{4,0},{5,1},{6,2},{7,3},{8,12},{9,13},{10,... | collective-permute-start | bytes 147464 | tf_op jit(solution)/shard_map/ppermute | solution.py:477
  12.8 8.4 %collective-permute-start.3 = (bf16[8,3,2048]{2,1,0:T(4,128)(2,1)S(1)}, bf16[8,3,2048]{2,1,0:T(4,128)(2,1)S(1)}, u32[]{:S(2)}, u32[]{:S(2)}) collective-permute-start(bf16[8,3,2048]{2,1,0:T(4,128)(2,1)S(1)} %pad_maximum_fusion.2.qa_ref), channel_id=1, source_target_pairs={{0,8},{1,9},{2,10},{3,11},{4,12},{5,13},{6,14},{7,15},{8,0},{9,1},... | collective-permute-start | bytes 294920 | tf_op jit(solution)/shard_map/ppermute | solution.py:477
  28.6 2.1 %collective-permute-start.4 = (bf16[656,512]{1,0:T(8,128)(2,1)S(1)}, bf16[656,512]{1,0:T(8,128)(2,1)S(1)}, u32[]{:S(2)}, u32[]{:S(2)}) collective-permute-start(bf16[656,512]{1,0:T(8,128)(2,1)S(1)} %get-tuple-element.146), channel_id=1, source_target_pairs={{0,1},{1,0},{2,3},{3,2},{4,5},{5,4},{6,7},{7,6},{8,9},{9,8},{10,11... | collective-permute-start | bytes 2015240 | tf_op jit(solution)/shard_map/ppermute | solution.py:477
  30.9 7.3 %collective-permute-start.5 = (bf16[336,512]{1,0:T(8,128)(2,1)S(1)}, bf16[336,512]{1,0:T(8,128)(2,1)S(1)}, u32[]{:S(2)}, u32[]{:S(2)}) collective-permute-start(bf16[336,512]{1,0:T(8,128)(2,1)S(1)} %get-tuple-element.151), channel_id=1, source_target_pairs={{0,2},{1,5},{2,0},{3,7},{4,6},{5,1},{6,4},{7,3},{8,10},{9,13},{10,... | collective-permute-start | bytes 1032200 | tf_op jit(solution)/shard_map/ppermute | solution.py:477
  38.6 5.6 %collective-permute-start.6 = (bf16[176,512]{1,0:T(8,128)(2,1)S(1)}, bf16[176,512]{1,0:T(8,128)(2,1)S(1)}, u32[]{:S(2)}, u32[]{:S(2)}) collective-permute-start(bf16[176,512]{1,0:T(8,128)(2,1)S(1)} %maximum_maximum_fusion), channel_id=1, source_target_pairs={{0,4},{1,3},{2,6},{3,1},{4,0},{5,7},{6,2},{7,5},{8,12},{9,11},{10,... | collective-permute-start | bytes 540680 | tf_op jit(solution)/shard_map/ppermute | solution.py:477
  44.3 7.8 %collective-permute-start.8 = (bf16[176,256]{1,0:T(8,128)(2,1)S(1)}, bf16[176,256]{1,0:T(8,128)(2,1)S(1)}, u32[]{:S(2)}, u32[]{:S(2)}) collective-permute-start(bf16[176,256]{1,0:T(8,128)(2,1)S(1)} %get-tuple-element.192), channel_id=1, source_target_pairs={{0,8},{1,9},{2,10},{3,11},{4,12},{5,13},{6,14},{7,15},{8,0},{9,1},... | collective-permute-start | bytes 270344 | tf_op jit(solution)/shard_map/ppermute | solution.py:477
  46.9 7.0 %collective-permute-start.7 = (bf16[176,256]{1,0:T(8,128)(2,1)S(1)}, bf16[176,256]{1,0:T(8,128)(2,1)S(1)}, u32[]{:S(2)}, u32[]{:S(2)}) collective-permute-start(bf16[176,256]{1,0:T(8,128)(2,1)S(1)} %get-tuple-element.191), channel_id=1, source_target_pairs={{0,8},{1,9},{2,10},{3,11},{4,12},{5,13},{6,14},{7,15},{8,0},{9,1},... | collective-permute-start | bytes 270344 | tf_op jit(solution)/shard_map/ppermute | solution.py:477
  54.0 4.4 %collective-permute-start.10 = (bf16[160,256]{1,0:T(8,128)(2,1)S(1)}, bf16[160,256]{1,0:T(8,128)(2,1)S(1)}, u32[]{:S(2)}, u32[]{:S(2)}) collective-permute-start(bf16[160,256]{1,0:T(8,128)(2,1)S(1)} %add_convert_fusion.1), channel_id=1, source_target_pairs={{0,4},{1,3},{2,6},{3,1},{4,0},{5,7},{6,2},{7,5},{8,12},{9,11},{10,... | collective-permute-start | bytes 245768 | tf_op jit(solution)/shard_map/ppermute | solution.py:477
  54.1 5.2 %collective-permute-start.9 = (bf16[160,256]{1,0:T(8,128)(2,1)S(1)}, bf16[160,256]{1,0:T(8,128)(2,1)S(1)}, u32[]{:S(2)}, u32[]{:S(2)}) collective-permute-start(bf16[160,256]{1,0:T(8,128)(2,1)S(1)} %add_convert_fusion), channel_id=1, source_target_pairs={{0,4},{1,3},{2,6},{3,1},{4,0},{5,7},{6,2},{7,5},{8,12},{9,11},{10,... | collective-permute-start | bytes 245768 | tf_op jit(solution)/shard_map/ppermute | solution.py:477
  59.3 5.3 %collective-permute-start.12 = (bf16[320,256]{1,0:T(8,128)(2,1)S(1)}, bf16[320,256]{1,0:T(8,128)(2,1)S(1)}, u32[]{:S(2)}, u32[]{:S(2)}) collective-permute-start(bf16[320,256]{1,0:T(8,128)(2,1)S(1)} %maximum_select_fusion.2), channel_id=1, source_target_pairs={{0,2},{1,5},{2,0},{3,7},{4,6},{5,1},{6,4},{7,3},{8,10},{9,13},{10,... | collective-permute-start | bytes 491528 | tf_op jit(solution)/shard_map/ppermute | solution.py:477
  60.5 5.8 %collective-permute-start.11 = (bf16[320,256]{1,0:T(8,128)(2,1)S(1)}, bf16[320,256]{1,0:T(8,128)(2,1)S(1)}, u32[]{:S(2)}, u32[]{:S(2)}) collective-permute-start(bf16[320,256]{1,0:T(8,128)(2,1)S(1)} %maximum_select_fusion.3), channel_id=1, source_target_pairs={{0,2},{1,5},{2,0},{3,7},{4,6},{5,1},{6,4},{7,3},{8,10},{9,13},{10,... | collective-permute-start | bytes 491528 | tf_op jit(solution)/shard_map/ppermute | solution.py:477
  66.6 2.2 %collective-permute-start.13 = (bf16[656,256]{1,0:T(8,128)(2,1)S(1)}, bf16[656,256]{1,0:T(8,128)(2,1)S(1)}, u32[]{:S(2)}, u32[]{:S(2)}) collective-permute-start(bf16[656,256]{1,0:T(8,128)(2,1)S(1)} %get-tuple-element.190.refs_0_.refs_1_), channel_id=1, source_target_pairs={{0,1},{1,0},{2,3},{3,2},{4,5},{5,4},{6,7},{7,6},{8,9},{9,8},{10,11... | collective-permute-start | bytes 1007624 | tf_op jit(solution)/shard_map/ppermute | solution.py:477
  66.6 2.2 %collective-permute-start.14 = (bf16[656,256]{1,0:T(8,128)(2,1)S(1)}, bf16[656,256]{1,0:T(8,128)(2,1)S(1)}, u32[]{:S(2)}, u32[]{:S(2)}) collective-permute-start(bf16[656,256]{1,0:T(8,128)(2,1)S(1)} %get-tuple-element.189.refs_2_.refs_3_), channel_id=1, source_target_pairs={{0,1},{1,0},{2,3},{3,2},{4,5},{5,4},{6,7},{7,6},{8,9},{9,8},{10,11... | collective-permute-start | bytes 1007624 | tf_op jit(solution)/shard_map/ppermute | solution.py:477

commit v8 on v7

--- a/solution.py
+++ b/solution.py
@@ -269,44 +269,52 @@
         gp_ref[...] = gp_scr[...].astype(gp_ref.dtype)
 
 
-def final_kernel(pick_ref, *refs):
-    out_ref, bias_ref = refs[-2:]
-    for c in range(CHAINS):
-        source_ref, rows_ref = refs[2 * c], refs[2 * c + 1]
-        span = source_ref.shape[1]
-        cols = slice(c * span, (c + 1) * span)
-        out_ref[:, cols] = source_ref[...].astype(F32)
-        bias_ref[:, cols] = rows_ref[0:1, :].astype(F32) + rows_ref[1:2, :].astype(F32)
-
-
-def widen(pick, sources, width, vocab, mine, before):
-    span = sources[0].shape[1]
-    rows = width // 2
-
-    def column(pick):
-        return pick[2] if mine else 1 - pick[2]
-
-    pair = [
-        pl.BlockSpec((rows, span), lambda i, pick: (i, 0)),
-        pl.BlockSpec((EXTRA, span), lambda i, pick: (width // EXTRA, 0)),
-    ]
+PIECES = 4
+
+
+def final_kernel(mine, *refs):
+    sources = refs[:CHAINS]
+    out_ref, bias_ref, wide, bias_wide, sems = refs[-5:]
+    width, part = wide.shape
+    core = lax.axis_index("dp") & 1
+    cols = pl.ds(pl.multiple_of((core if mine else 1 - core) * part, part), part)
+    span = part // CHAINS
+    size = width // PIECES
+    copies = []
+    for c, source in enumerate(sources):
+        extra = source[width:, :].astype(F32)
+        bias_wide[:, c * span : (c + 1) * span] = extra[0:1] + extra[1:2]
+    copies.append(pltpu.make_async_copy(bias_wide, bias_ref.at[:, cols], sems.at[PIECES]))
+    copies[0].start()
+    for p in range(PIECES):
+        rows = slice(p * size, (p + 1) * size)
+        for c, source in enumerate(sources):
+            wide[rows, c * span : (c + 1) * span] = source[rows, :].astype(F32)
+        copies.append(
+            pltpu.make_async_copy(wide.at[rows], out_ref.at[rows, cols], sems.at[p])
+        )
+        copies[-1].start()
+    for copy in copies:
+        copy.wait()
+
+
+def widen(sources, width, vocab, mine, before):
+    part = vocab // 2
+    anywhere = pl.BlockSpec(memory_space=pl.ANY)
     return pl.pallas_call(
-        final_kernel,
-        grid_spec=pltpu.PrefetchScalarGridSpec(
-            num_scalar_prefetch=1,
-            grid=(width // rows,),
-            in_specs=pair * CHAINS + [pl.BlockSpec(memory_space=pl.ANY)] * len(before),
-            out_specs=[
-                pl.BlockSpec((rows, vocab // 2), lambda i, pick: (i, column(pick))),
-                pl.BlockSpec((1, vocab // 2), lambda i, pick: (0, column(pick))),
-            ],
-        ),
+        functools.partial(final_kernel, mine),
+        in_specs=[pl.BlockSpec(memory_space=pltpu.VMEM)] * CHAINS + [anywhere] * len(before),
+        out_specs=[anywhere, anywhere],
         out_shape=[
-            jax.ShapeDtypeStruct((width, vocab), F32), jax.ShapeDtypeStruct((1, vocab), F32)
-        ],
-        input_output_aliases={1 + 2 * CHAINS + k: k for k in range(len(before))},
-        compiler_params=params(8),
-    )(pick, *[s for source in sources for s in (source, source)], *before)
+            pltpu.HBM((width, vocab), F32), pltpu.HBM((1, vocab), F32)
+        ],
+        scratch_shapes=[
+            pltpu.VMEM((width, part), F32), pltpu.VMEM((1, part), F32),
+            pltpu.SemaphoreType.DMA((PIECES + 1,)),
+        ],
+        input_output_aliases={CHAINS + k: k for k in range(len(before))},
+        compiler_params=pltpu.CompilerParams(vmem_limit_bytes=8 * 1024 * 1024),
+    )(*sources, *before)
 
 
 def whole(shape):
@@ -575,9 +583,9 @@
         have = joined
     sent = [jnp.concatenate([have[c], bias_rows(*sums[c])], axis=0) for c in chains]
     others = [exchange(sent[c], 1, 1) for c in chains]
-    result = tuple(widen(pick, sent, width, vocab, True, ()))
+    result = tuple(widen(sent, width, vocab, True, ()))
     others, result = lax.optimization_barrier((others, result))
-    result = tuple(widen(pick, others, width, vocab, False, result))
+    result = tuple(widen(others, width, vocab, False, result))
     grad_weight, grad_bias = result
     return (loss.reshape(1), grad_weight, grad_bias.reshape(vocab), done[0][None], done[1][None])
 

time: 70.7 us -> 70.2 us (level)
  Pallas kernels: 29 us -> 27.9 us
    pallas_call x2, Pallas kernels: 3.34 us -> 2.23 us  [widen(): pl.pallas_call(functools.partial(final_kernel, mine), in_specs=[pl.BlockS...]
  transfers between devices with their start and end apart: 15 -> 15, of which waited for: 11 -> 12; matrix products, arithmetic and copies ran while one was open for 1% -> 1% of each run, Pallas kernels for 28% -> 27%
where the time goes in v8:
time: 70.2 us; the launch traced here: 70 us
  Pallas kernels  27.9 us (40%)
  waiting for transfers between devices  22.3 us (32%)
  starting transfers between devices  16.5 us (24%)
  between operations  2.29 us (3%)
  other arithmetic  1 us (1%)
    ppermute x15, waiting for transfers between devices, exchange(): return lax.ppermute(value, 'dp', pairs)  22.3 us
    ppermute x15, starting transfers between devices, exchange(): return lax.ppermute(value, 'dp', pairs)  16.5 us
    pallas_call x2, Pallas kernels, input_gradients(): pl.pallas_call(functools.partial(input_kernel, begin, last), grid=(cells...  8.12 us
    pallas_call x3, Pallas kernels, forward(): pl.pallas_call(functools.partial(forward_kernel, begin), grid=(blocks,),...  7.95 us
    pallas_call x1, Pallas kernels, gradients(): pl.pallas_call(functools.partial(grad_kernel, blocks), grid_spec=grid_spe...  7.45 us
    pallas_call x2, Pallas kernels, widen(): pl.pallas_call(functools.partial(final_kernel, mine), in_specs=[pl.BlockS...  2.23 us
    pallas_call x1, Pallas kernels, stage(): pl.pallas_call(stage_kernel, in_specs=[anywhere] * (1 + len(arrays)), out...  1.98 us
  transfers between devices with their start and end apart: 15, of which 12 were waited for; matrix products, arithmetic and copies ran while one was open for 1% of the time, Pallas kernels for 27%

profile of v8, /device:TPU:0, one launch (start us, length us, event | category | flops | bytes accessed | tf_op | source)
XLA Modules:
  0.0 70.0 jit_solution(10127878006401010997)
XLA Ops:
  0.6 0.5 collective-permute-start
  1.2 2.0 %shard_map.128 = (bf16[640,1024]{1,0:T(8,128)(2,1)S(1)}, bf16[64,640]{1,0:T(8,128)(2,1)S(1)}, bf16[32,640]{1,0:T(8,128)(2,1)S(1)}, f32[1,1024]{1,0:T(1,128)S(1)}...) custom-call(s32[16]{0:T(128)} %assignment_ref.1, bf16[640,1024]{1,0:T(8,128)(2,1)} %refs_0_.1, ...), custom_call_target="tpu_custom_call" | custom-call | tf_op jit(solution)/shard_map/pallas_call | solution.py:59
  3.2 2.6 %collective-permute-start.1 = (bf16[2,3,2048]{2,1,0:T(4,128)(2,1)S(1)}, bf16[2,3,2048]{2,1,0:T(4,128)(2,1)S(1)}, u32[]{:S(2)}, u32[]{:S(2)}) collective-permute-start(bf16[2,3,2048]{2,1,0:T(4,128)(2,1)S(1)} %pad_maximum_fusion.6), channel_id=1, source_target_pairs={{0,2},{1,3},{2,0},{3,1},{4,6},{5,7},{6,4},{7,5},{8,10},{9,11},{10,... | collective-permute-start | bytes 73736 | tf_op jit(solution)/shard_map/ppermute | solution.py:485
  6.4 1.9 %shard_map.129 = (f32[2048,1024]{1,0:T(8,128)S(1)}, f32[8,2048]{1,0:T(8,128)S(1)}, bf16[640,2048]{1,0:T(8,128)(2,1)S(1)}) custom-call(s32[1]{0:T(128)S(6)} %copy.33.tlen_ref, s32[1,31]{1,0:T(1,128)S(1)} %get-tuple-element.132.labels_ref, bf16[64,640]{1,0:T(8,128)(2,1)S(1)} %get-tuple-element.134.enc_ref, bf16[32,640]{1,0:T(8,128)(2,1)S(1)} %get-tuple-element.135.pred_ref, ...), custom_call_target="tpu_custom_call" | custom-call | tf_op jit(solution)/shard_map/pallas_call | solution.py:332
  8.4 1.6 %collective-permute-start.2 = (bf16[4,3,2048]{2,1,0:T(4,128)(2,1)S(1)}, bf16[4,3,2048]{2,1,0:T(4,128)(2,1)S(1)}, u32[]{:S(2)}, u32[]{:S(2)}) collective-permute-start(bf16[4,3,2048]{2,1,0:T(4,128)(2,1)S(1)} %pad_maximum_fusion.5), channel_id=1, source_target_pairs={{0,4},{1,5},{2,6},{3,7},{4,0},{5,1},{6,2},{7,3},{8,12},{9,13},{10,... | collective-permute-start | bytes 147464 | tf_op jit(solution)/shard_map/ppermute | solution.py:485
  10.0 1.9 %shard_map.130 = (f32[2048,1024]{1,0:T(8,128)S(1)}, f32[8,2048]{1,0:T(8,128)S(1)}, bf16[640,2048]{1,0:T(8,128)(2,1)S(1)}) custom-call(s32[1]{0:T(128)S(6)} %copy.33.tlen_ref, s32[1,31]{1,0:T(1,128)S(1)} %get-tuple-element.132.labels_ref, bf16[64,640]{1,0:T(8,128)(2,1)S(1)} %get-tuple-element.134.enc_ref, ...), custom_call_target="tpu_custom_call", output_to_operand_aliasing={{0}: (6, {}), {1}: (7, {}), {2}: (8, {})} | custom-call | tf_op jit(solution)/shard_map/pallas_call | solution.py:332
  12.0 0.8 %collective-permute-done.2 = bf16[4,3,2048]{2,1,0:T(4,128)(2,1)S(1)} collective-permute-done((bf16[4,3,2048]{2,1,0:T(4,128)(2,1)S(1)}, bf16[4,3,2048]{2,1,0:T(4,128)(2,1)S(1)}, u32[]{:S(2)}, u32[]{:S(2)}) %collective-permute-start.2) | collective-permute-done | bytes 49184 | tf_op jit(solution)/shard_map/ppermute | solution.py:485
  12.8 2.7 %collective-permute-start.3 = (bf16[8,3,2048]{2,1,0:T(4,128)(2,1)S(1)}, bf16[8,3,2048]{2,1,0:T(4,128)(2,1)S(1)}, u32[]{:S(2)}, u32[]{:S(2)}) collective-permute-start(bf16[8,3,2048]{2,1,0:T(4,128)(2,1)S(1)} %pad_maximum_fusion.2.qa_ref), channel_id=1, source_target_pairs={{0,8},{1,9},{2,10},{3,11},{4,12},{5,13},{6,14},{7,15},{8,0},{9,1},... | collective-permute-start | bytes 294920 | tf_op jit(solution)/shard_map/ppermute | solution.py:485
  16.1 4.1 %shard_map.131 = (f32[2048,1024]{1,0:T(8,128)S(1)}, f32[8,2048]{1,0:T(8,128)S(1)}, bf16[640,2048]{1,0:T(8,128)(2,1)S(1)}) custom-call(s32[1]{0:T(128)S(6)} %copy.33.tlen_ref, s32[1,31]{1,0:T(1,128)S(1)} %get-tuple-element.132.labels_ref, bf16[64,640]{1,0:T(8,128)(2,1)S(1)} %get-tuple-element.134.enc_ref, ...), custom_call_target="tpu_custom_call", output_to_operand_aliasing={{0}: (6, {}), {1}: (7, {}), {2}: (8, {})} | custom-call | tf_op jit(solution)/shard_map/pallas_call | solution.py:332
  20.2 1.0 %collective-permute-done.3.qb_ref = bf16[8,3,2048]{2,1,0:T(4,128)(2,1)S(1)} collective-permute-done((bf16[8,3,2048]{2,1,0:T(4,128)(2,1)S(1)}, bf16[8,3,2048]{2,1,0:T(4,128)(2,1)S(1)}, u32[]{:S(2)}, u32[]{:S(2)}) %collective-permute-start.3) | collective-permute-done | bytes 98336 | tf_op jit(solution)/shard_map/ppermute | solution.py:485
  21.2 7.4 %shard_map.132 = (bf16[2048,1024]{1,0:T(8,128)(2,1)}, f32[1,1]{1,0:T(1,128)}, bf16[656,512]{1,0:T(8,128)(2,1)S(1)}, f32[656,512]{1,0:T(8,128)S(1)}) custom-call(s32[3]{0:T(128)S(1)} %get-tuple-element.131.pick_ref, s32[1]{0:T(128)S(6)} %copy.32.flen_ref, s32[1]{0:T(128)S(6)} %copy.33.tlen_ref, s32[1,31]{1,0:T(1,128)S(1)} %get-tuple-element.132.labels_ref, ...), custom_call_target="tpu_custom_call" | custom-call | tf_op jit(solution)/shard_map/pallas_call | solution.py:391
  28.6 2.1 %collective-permute-done.4.got_ref = bf16[656,512]{1,0:T(8,128)(2,1)S(1)} collective-permute-done((bf16[656,512]{1,0:T(8,128)(2,1)S(1)}, bf16[656,512]{1,0:T(8,128)(2,1)S(1)}, u32[]{:S(2)}, u32[]{:S(2)}) %collective-permute-start.4) | collective-permute-done | bytes 671776 | tf_op jit(solution)/shard_map/ppermute | solution.py:485
  30.9 0.6 collective-permute-start.5
  31.6 4.1 %shard_map.134 = (bf16[64,640]{1,0:T(8,128)(2,1)}, f32[32,640]{1,0:T(8,128)S(1)}) custom-call(bf16[64,640]{1,0:T(8,128)(2,1)S(1)} %get-tuple-element.134.enc_ref, bf16[32,640]{1,0:T(8,128)(2,1)S(1)} %get-tuple-element.135.pred_ref, bf16[2048,1024]{1,0:T(8,128)(2,1)} %get-tuple-element.159.d_ref, bf16[640,1024]{1,0:T(8,128)(2,1)S(1)} %get-tuple-element.136.w_ref), custom_call_target="tpu_custom_call" | custom-call | tf_op jit(solution)/shard_map/pallas_call | solution.py:410
  35.7 2.6 %collective-permute-done.5 = bf16[336,512]{1,0:T(8,128)(2,1)S(1)} collective-permute-done((bf16[336,512]{1,0:T(8,128)(2,1)S(1)}, bf16[336,512]{1,0:T(8,128)(2,1)S(1)}, u32[]{:S(2)}, u32[]{:S(2)}) %collective-permute-start.5) | collective-permute-done | bytes 344096 | tf_op jit(solution)/shard_map/ppermute | solution.py:485
  38.6 0.7 %collective-permute-start.6 = (bf16[176,512]{1,0:T(8,128)(2,1)S(1)}, bf16[176,512]{1,0:T(8,128)(2,1)S(1)}, u32[]{:S(2)}, u32[]{:S(2)}) collective-permute-start(bf16[176,512]{1,0:T(8,128)(2,1)S(1)} %maximum_maximum_fusion), channel_id=1, source_target_pairs={{0,4},{1,3},{2,6},{3,1},{4,0},{5,7},{6,2},{7,5},{8,12},{9,11},{10,... | collective-permute-start | bytes 540680 | tf_op jit(solution)/shard_map/ppermute | solution.py:485
  39.3 4.1 %shard_map.135 = (bf16[64,640]{1,0:T(8,128)(2,1)}, bf16[32,640]{1,0:T(8,128)(2,1)}) custom-call(bf16[64,640]{1,0:T(8,128)(2,1)S(1)} %get-tuple-element.134.enc_ref, bf16[32,640]{1,0:T(8,128)(2,1)S(1)} %get-tuple-element.135.pred_ref, bf16[2048,1024]{1,0:T(8,128)(2,1)} %get-tuple-element.159.d_ref, ...), custom_call_target="tpu_custom_call", output_to_operand_aliasing={{0}: (5, {})} | custom-call | tf_op jit(solution)/shard_map/pallas_call | solution.py:410
  43.4 0.8 %collective-permute-done.6 = bf16[176,512]{1,0:T(8,128)(2,1)S(1)} collective-permute-done((bf16[176,512]{1,0:T(8,128)(2,1)S(1)}, bf16[176,512]{1,0:T(8,128)(2,1)S(1)}, u32[]{:S(2)}, u32[]{:S(2)}) %collective-permute-start.6) | collective-permute-done | bytes 180256 | tf_op jit(solution)/shard_map/ppermute | solution.py:485
  44.3 2.7 %collective-permute-start.8 = (bf16[176,256]{1,0:T(8,128)(2,1)S(1)}, bf16[176,256]{1,0:T(8,128)(2,1)S(1)}, u32[]{:S(2)}, u32[]{:S(2)}) collective-permute-start(bf16[176,256]{1,0:T(8,128)(2,1)S(1)} %get-tuple-element.192), channel_id=1, source_target_pairs={{0,8},{1,9},{2,10},{3,11},{4,12},{5,13},{6,14},{7,15},{8,0},{9,1},... | collective-permute-start | bytes 270344 | tf_op jit(solution)/shard_map/ppermute | solution.py:485
  47.3 4.8 %collective-permute-done.8 = bf16[176,256]{1,0:T(8,128)(2,1)S(1)} collective-permute-done((bf16[176,256]{1,0:T(8,128)(2,1)S(1)}, bf16[176,256]{1,0:T(8,128)(2,1)S(1)}, u32[]{:S(2)}, u32[]{:S(2)}) %collective-permute-start.8) | collective-permute-done | bytes 90144 | tf_op jit(solution)/shard_map/ppermute | solution.py:485
  52.1 1.9 %collective-permute-done.7 = bf16[176,256]{1,0:T(8,128)(2,1)S(1)} collective-permute-done((bf16[176,256]{1,0:T(8,128)(2,1)S(1)}, bf16[176,256]{1,0:T(8,128)(2,1)S(1)}, u32[]{:S(2)}, u32[]{:S(2)}) %collective-permute-start.7) | collective-permute-done | bytes 90144 | tf_op jit(solution)/shard_map/ppermute | solution.py:485
  54.1 2.0 %collective-permute-start.9 = (bf16[160,256]{1,0:T(8,128)(2,1)S(1)}, bf16[160,256]{1,0:T(8,128)(2,1)S(1)}, u32[]{:S(2)}, u32[]{:S(2)}) collective-permute-start(bf16[160,256]{1,0:T(8,128)(2,1)S(1)} %add_convert_fusion), channel_id=1, source_target_pairs={{0,4},{1,3},{2,6},{3,1},{4,0},{5,7},{6,2},{7,5},{8,12},{9,11},{10,... | collective-permute-start | bytes 245768 | tf_op jit(solution)/shard_map/ppermute | solution.py:485
  56.1 2.3 %collective-permute-done.10 = bf16[160,256]{1,0:T(8,128)(2,1)S(1)} collective-permute-done((bf16[160,256]{1,0:T(8,128)(2,1)S(1)}, bf16[160,256]{1,0:T(8,128)(2,1)S(1)}, u32[]{:S(2)}, u32[]{:S(2)}) %collective-permute-start.10) | collective-permute-done | bytes 81952 | tf_op jit(solution)/shard_map/ppermute | solution.py:485
  58.5 0.8 %collective-permute-done.9 = bf16[160,256]{1,0:T(8,128)(2,1)S(1)} collective-permute-done((bf16[160,256]{1,0:T(8,128)(2,1)S(1)}, bf16[160,256]{1,0:T(8,128)(2,1)S(1)}, u32[]{:S(2)}, u32[]{:S(2)}) %collective-permute-start.9) | collective-permute-done | bytes 81952 | tf_op jit(solution)/shard_map/ppermute | solution.py:485
  59.3 1.2 %collective-permute-start.12 = (bf16[320,256]{1,0:T(8,128)(2,1)S(1)}, bf16[320,256]{1,0:T(8,128)(2,1)S(1)}, u32[]{:S(2)}, u32[]{:S(2)}) collective-permute-start(bf16[320,256]{1,0:T(8,128)(2,1)S(1)} %maximum_select_fusion.2), channel_id=1, source_target_pairs={{0,2},{1,5},{2,0},{3,7},{4,6},{5,1},{6,4},{7,3},{8,10},{9,13},{10,... | collective-permute-start | bytes 491528 | tf_op jit(solution)/shard_map/ppermute | solution.py:485
  60.5 0.9 %collective-permute-start.11 = (bf16[320,256]{1,0:T(8,128)(2,1)S(1)}, bf16[320,256]{1,0:T(8,128)(2,1)S(1)}, u32[]{:S(2)}, u32[]{:S(2)}) collective-permute-start(bf16[320,256]{1,0:T(8,128)(2,1)S(1)} %maximum_select_fusion.3), channel_id=1, source_target_pairs={{0,2},{1,5},{2,0},{3,7},{4,6},{5,1},{6,4},{7,3},{8,10},{9,13},{10,... | collective-permute-start | bytes 491528 | tf_op jit(solution)/shard_map/ppermute | solution.py:485
  61.4 3.2 %collective-permute-done.12 = bf16[320,256]{1,0:T(8,128)(2,1)S(1)} collective-permute-done((bf16[320,256]{1,0:T(8,128)(2,1)S(1)}, bf16[320,256]{1,0:T(8,128)(2,1)S(1)}, u32[]{:S(2)}, u32[]{:S(2)}) %collective-permute-start.12) | collective-permute-done | bytes 163872 | tf_op jit(solution)/shard_map/ppermute | solution.py:485
  64.7 1.6 %collective-permute-done.11 = bf16[320,256]{1,0:T(8,128)(2,1)S(1)} collective-permute-done((bf16[320,256]{1,0:T(8,128)(2,1)S(1)}, bf16[320,256]{1,0:T(8,128)(2,1)S(1)}, u32[]{:S(2)}, u32[]{:S(2)}) %collective-permute-start.11) | collective-permute-done | bytes 163872 | tf_op jit(solution)/shard_map/ppermute | solution.py:485
  66.6 0.5 collective-permute-start.14
  67.1 1.1 %shard_map.136 = (f32[640,1024]{1,0:T(8,128)}, f32[1,1024]{1,0:T(1,128)}) custom-call(bf16[656,256]{1,0:T(8,128)(2,1)S(1)} %get-tuple-element.190.refs_0_, bf16[656,256]{1,0:T(8,128)(2,1)S(1)} %get-tuple-element.189.refs_1_), custom_call_target="tpu_custom_call" | custom-call | tf_op jit(solution)/shard_map/pallas_call | solution.py:304
  68.3 0.5 collective-permute-done.14.refs_1_
  68.7 1.1 %shard_map.137 = (f32[640,1024]{1,0:T(8,128)}, f32[1,1024]{1,0:T(1,128)}) custom-call(bf16[656,256]{1,0:T(8,128)(2,1)S(1)} %collective-permute-done.13.refs_0_, bf16[656,256]{1,0:T(8,128)(2,1)S(1)} %collective-permute-done.14.refs_1_, f32[640,1024]{1,0:T(8,128)} %get-tuple-element.175.refs_2_, ...), custom_call_target="tpu_custom_call", output_to_operand_aliasing={{0}: (2, {}), {1}: (3, {})} | custom-call | tf_op jit(solution)/shard_map/pallas_call | solution.py:304
  (34 shorter events, 1.7 us)
Async XLA Ops:
  0.6 2.5 %collective-permute-start = (bf16[1,3,2048]{2,1,0:T(4,128)(2,1)}, bf16[1,3,2048]{2,1,0:T(4,128)(2,1)S(1)}, u32[]{:S(2)}, u32[]{:S(2)}) collective-permute-start(bf16[1,3,2048]{2,1,0:T(4,128)(2,1)} %refs_5_.1), channel_id=1, source_target_pairs={{0,1},{1,0},{2,3},{3,2},{4,5},{5,4},{6,7},{7,6},{8,9},{9,8},{10,11... | collective-permute-start | bytes 36872 | tf_op jit(solution)/shard_map/ppermute | solution.py:485
  3.2 5.2 %collective-permute-start.1 = (bf16[2,3,2048]{2,1,0:T(4,128)(2,1)S(1)}, bf16[2,3,2048]{2,1,0:T(4,128)(2,1)S(1)}, u32[]{:S(2)}, u32[]{:S(2)}) collective-permute-start(bf16[2,3,2048]{2,1,0:T(4,128)(2,1)S(1)} %pad_maximum_fusion.6), channel_id=1, source_target_pairs={{0,2},{1,3},{2,0},{3,1},{4,6},{5,7},{6,4},{7,5},{8,10},{9,11},{10,... | collective-permute-start | bytes 73736 | tf_op jit(solution)/shard_map/ppermute | solution.py:485
  8.4 4.3 %collective-permute-start.2 = (bf16[4,3,2048]{2,1,0:T(4,128)(2,1)S(1)}, bf16[4,3,2048]{2,1,0:T(4,128)(2,1)S(1)}, u32[]{:S(2)}, u32[]{:S(2)}) collective-permute-start(bf16[4,3,2048]{2,1,0:T(4,128)(2,1)S(1)} %pad_maximum_fusion.5), channel_id=1, source_target_pairs={{0,4},{1,5},{2,6},{3,7},{4,0},{5,1},{6,2},{7,3},{8,12},{9,13},{10,... | collective-permute-start | bytes 147464 | tf_op jit(solution)/shard_map/ppermute | solution.py:485
  12.8 8.4 %collective-permute-start.3 = (bf16[8,3,2048]{2,1,0:T(4,128)(2,1)S(1)}, bf16[8,3,2048]{2,1,0:T(4,128)(2,1)S(1)}, u32[]{:S(2)}, u32[]{:S(2)}) collective-permute-start(bf16[8,3,2048]{2,1,0:T(4,128)(2,1)S(1)} %pad_maximum_fusion.2.qa_ref), channel_id=1, source_target_pairs={{0,8},{1,9},{2,10},{3,11},{4,12},{5,13},{6,14},{7,15},{8,0},{9,1},... | collective-permute-start | bytes 294920 | tf_op jit(solution)/shard_map/ppermute | solution.py:485
  28.6 2.1 %collective-permute-start.4 = (bf16[656,512]{1,0:T(8,128)(2,1)S(1)}, bf16[656,512]{1,0:T(8,128)(2,1)S(1)}, u32[]{:S(2)}, u32[]{:S(2)}) collective-permute-start(bf16[656,512]{1,0:T(8,128)(2,1)S(1)} %get-tuple-element.146), channel_id=1, source_target_pairs={{0,1},{1,0},{2,3},{3,2},{4,5},{5,4},{6,7},{7,6},{8,9},{9,8},{10,11... | collective-permute-start | bytes 2015240 | tf_op jit(solution)/shard_map/ppermute | solution.py:485
  30.9 7.3 %collective-permute-start.5 = (bf16[336,512]{1,0:T(8,128)(2,1)S(1)}, bf16[336,512]{1,0:T(8,128)(2,1)S(1)}, u32[]{:S(2)}, u32[]{:S(2)}) collective-permute-start(bf16[336,512]{1,0:T(8,128)(2,1)S(1)} %get-tuple-element.151), channel_id=1, source_target_pairs={{0,2},{1,5},{2,0},{3,7},{4,6},{5,1},{6,4},{7,3},{8,10},{9,13},{10,... | collective-permute-start | bytes 1032200 | tf_op jit(solution)/shard_map/ppermute | solution.py:485
  38.6 5.6 %collective-permute-start.6 = (bf16[176,512]{1,0:T(8,128)(2,1)S(1)}, bf16[176,512]{1,0:T(8,128)(2,1)S(1)}, u32[]{:S(2)}, u32[]{:S(2)}) collective-permute-start(bf16[176,512]{1,0:T(8,128)(2,1)S(1)} %maximum_maximum_fusion), channel_id=1, source_target_pairs={{0,4},{1,3},{2,6},{3,1},{4,0},{5,7},{6,2},{7,5},{8,12},{9,11},{10,... | collective-permute-start | bytes 540680 | tf_op jit(solution)/shard_map/ppermute | solution.py:485
  44.3 7.8 %collective-permute-start.8 = (bf16[176,256]{1,0:T(8,128)(2,1)S(1)}, bf16[176,256]{1,0:T(8,128)(2,1)S(1)}, u32[]{:S(2)}, u32[]{:S(2)}) collective-permute-start(bf16[176,256]{1,0:T(8,128)(2,1)S(1)} %get-tuple-element.192), channel_id=1, source_target_pairs={{0,8},{1,9},{2,10},{3,11},{4,12},{5,13},{6,14},{7,15},{8,0},{9,1},... | collective-permute-start | bytes 270344 | tf_op jit(solution)/shard_map/ppermute | solution.py:485
  47.0 7.0 %collective-permute-start.7 = (bf16[176,256]{1,0:T(8,128)(2,1)S(1)}, bf16[176,256]{1,0:T(8,128)(2,1)S(1)}, u32[]{:S(2)}, u32[]{:S(2)}) collective-permute-start(bf16[176,256]{1,0:T(8,128)(2,1)S(1)} %get-tuple-element.191), channel_id=1, source_target_pairs={{0,8},{1,9},{2,10},{3,11},{4,12},{5,13},{6,14},{7,15},{8,0},{9,1},... | collective-permute-start | bytes 270344 | tf_op jit(solution)/shard_map/ppermute | solution.py:485
  54.0 4.4 %collective-permute-start.10 = (bf16[160,256]{1,0:T(8,128)(2,1)S(1)}, bf16[160,256]{1,0:T(8,128)(2,1)S(1)}, u32[]{:S(2)}, u32[]{:S(2)}) collective-permute-start(bf16[160,256]{1,0:T(8,128)(2,1)S(1)} %add_convert_fusion.1), channel_id=1, source_target_pairs={{0,4},{1,3},{2,6},{3,1},{4,0},{5,7},{6,2},{7,5},{8,12},{9,11},{10,... | collective-permute-start | bytes 245768 | tf_op jit(solution)/shard_map/ppermute | solution.py:485
  54.1 5.2 %collective-permute-start.9 = (bf16[160,256]{1,0:T(8,128)(2,1)S(1)}, bf16[160,256]{1,0:T(8,128)(2,1)S(1)}, u32[]{:S(2)}, u32[]{:S(2)}) collective-permute-start(bf16[160,256]{1,0:T(8,128)(2,1)S(1)} %add_convert_fusion), channel_id=1, source_target_pairs={{0,4},{1,3},{2,6},{3,1},{4,0},{5,7},{6,2},{7,5},{8,12},{9,11},{10,... | collective-permute-start | bytes 245768 | tf_op jit(solution)/shard_map/ppermute | solution.py:485
  59.3 5.3 %collective-permute-start.12 = (bf16[320,256]{1,0:T(8,128)(2,1)S(1)}, bf16[320,256]{1,0:T(8,128)(2,1)S(1)}, u32[]{:S(2)}, u32[]{:S(2)}) collective-permute-start(bf16[320,256]{1,0:T(8,128)(2,1)S(1)} %maximum_select_fusion.2), channel_id=1, source_target_pairs={{0,2},{1,5},{2,0},{3,7},{4,6},{5,1},{6,4},{7,3},{8,10},{9,13},{10,... | collective-permute-start | bytes 491528 | tf_op jit(solution)/shard_map/ppermute | solution.py:485
  60.5 5.8 %collective-permute-start.11 = (bf16[320,256]{1,0:T(8,128)(2,1)S(1)}, bf16[320,256]{1,0:T(8,128)(2,1)S(1)}, u32[]{:S(2)}, u32[]{:S(2)}) collective-permute-start(bf16[320,256]{1,0:T(8,128)(2,1)S(1)} %maximum_select_fusion.3), channel_id=1, source_target_pairs={{0,2},{1,5},{2,0},{3,7},{4,6},{5,1},{6,4},{7,3},{8,10},{9,13},{10,... | collective-permute-start | bytes 491528 | tf_op jit(solution)/shard_map/ppermute | solution.py:485
  66.6 1.7 %collective-permute-start.13 = (bf16[656,256]{1,0:T(8,128)(2,1)S(1)}, bf16[656,256]{1,0:T(8,128)(2,1)S(1)}, u32[]{:S(2)}, u32[]{:S(2)}) collective-permute-start(bf16[656,256]{1,0:T(8,128)(2,1)S(1)} %get-tuple-element.190.refs_0_), channel_id=1, source_target_pairs={{0,1},{1,0},{2,3},{3,2},{4,5},{5,4},{6,7},{7,6},{8,9},{9,8},{10,11... | collective-permute-start | bytes 1007624 | tf_op jit(solution)/shard_map/ppermute | solution.py:485
  66.6 2.1 %collective-permute-start.14 = (bf16[656,256]{1,0:T(8,128)(2,1)S(1)}, bf16[656,256]{1,0:T(8,128)(2,1)S(1)}, u32[]{:S(2)}, u32[]{:S(2)}) collective-permute-start(bf16[656,256]{1,0:T(8,128)(2,1)S(1)} %get-tuple-element.189.refs_1_), channel_id=1, source_target_pairs={{0,1},{1,0},{2,3},{3,2},{4,5},{5,4},{6,7},{7,6},{8,9},{9,8},{10,11... | collective-permute-start | bytes 1007624 | tf_op jit(solution)/shard_map/ppermute | solution.py:485

commit v9 on v8

--- a/solution.py
+++ b/solution.py
@@ -152,7 +152,7 @@
         gb_scr[...] = jnp.zeros_like(gb_scr)
         loss_scr[...] = jnp.zeros_like(loss_scr)
         column = target_column(labels_ref, token_len, tok_slots, block_frames)
-        target_scr[...] = jnp.broadcast_to(column, (rows, LANES))
+        target_scr[...] = column - lax.broadcasted_iota(jnp.int32, (rows, LANES), 1)
 
     def collapse(held_ref):
         half_count = pick_ref[1]
@@ -191,7 +191,7 @@
         lane = lax.broadcasted_iota(jnp.int32, (rows, LANES), 1)
         for j in range(vocab // LANES):
             cols = slice(j * LANES, (j + 1) * LANES)
-            d = jnp.where(lane + j * LANES == target_scr[...], d_label, e_ref[:, cols] * scale)
+            d = jnp.where(target_scr[...] == j * LANES, d_label, e_ref[:, cols] * scale)
             if j == 0:
                 d = jnp.where(lane == 0, columns[:, 2:3], d)
             low = d.astype(BF16)

time: 70.2 us -> 70.1 us (level)
  no operation moved by 1% of the time
where the time goes in v9:
time: 70.1 us; the launch traced here: 69.9 us
  Pallas kernels  27.7 us (40%)
  waiting for transfers between devices  22.3 us (32%)
  starting transfers between devices  16.5 us (24%)
  between operations  2.29 us (3%)
  other arithmetic  1 us (1%)
    ppermute x15, waiting for transfers between devices, exchange(): return lax.ppermute(value, 'dp', pairs)  22.3 us
    ppermute x15, starting transfers between devices, exchange(): return lax.ppermute(value, 'dp', pairs)  16.5 us
    pallas_call x2, Pallas kernels, input_gradients(): pl.pallas_call(functools.partial(input_kernel, begin, last), grid=(cells...  8.12 us
    pallas_call x3, Pallas kernels, forward(): pl.pallas_call(functools.partial(forward_kernel, begin), grid=(blocks,),...  7.95 us
    pallas_call x1, Pallas kernels, gradients(): pl.pallas_call(functools.partial(grad_kernel, blocks), grid_spec=grid_spe...  7.3 us
    pallas_call x2, Pallas kernels, widen(): pl.pallas_call(functools.partial(final_kernel, mine), in_specs=[pl.BlockS...  2.23 us
    pallas_call x1, Pallas kernels, stage(): pl.pallas_call(stage_kernel, in_specs=[anywhere] * (1 + len(arrays)), out...  1.98 us
  transfers between devices with their start and end apart: 15, of which 12 were waited for; matrix products, arithmetic and copies ran while one was open for 1% of the time, Pallas kernels for 27%

profile of v9, /device:TPU:0, one launch (start us, length us, event | category | flops | bytes accessed | tf_op | source)
XLA Modules:
  0.0 69.9 jit_solution(11397871857026354042)
XLA Ops:
  0.6 0.5 collective-permute-start
  1.2 2.0 %shard_map.128 = (bf16[640,1024]{1,0:T(8,128)(2,1)S(1)}, bf16[64,640]{1,0:T(8,128)(2,1)S(1)}, bf16[32,640]{1,0:T(8,128)(2,1)S(1)}, f32[1,1024]{1,0:T(1,128)S(1)}...) custom-call(s32[16]{0:T(128)} %assignment_ref.1, bf16[640,1024]{1,0:T(8,128)(2,1)} %refs_0_.1, ...), custom_call_target="tpu_custom_call" | custom-call | tf_op jit(solution)/shard_map/pallas_call | solution.py:59
  3.2 2.6 %collective-permute-start.1 = (bf16[2,3,2048]{2,1,0:T(4,128)(2,1)S(1)}, bf16[2,3,2048]{2,1,0:T(4,128)(2,1)S(1)}, u32[]{:S(2)}, u32[]{:S(2)}) collective-permute-start(bf16[2,3,2048]{2,1,0:T(4,128)(2,1)S(1)} %pad_maximum_fusion.6), channel_id=1, source_target_pairs={{0,2},{1,3},{2,0},{3,1},{4,6},{5,7},{6,4},{7,5},{8,10},{9,11},{10,... | collective-permute-start | bytes 73736 | tf_op jit(solution)/shard_map/ppermute | solution.py:485
  6.4 1.9 %shard_map.129 = (f32[2048,1024]{1,0:T(8,128)S(1)}, f32[8,2048]{1,0:T(8,128)S(1)}, bf16[640,2048]{1,0:T(8,128)(2,1)S(1)}) custom-call(s32[1]{0:T(128)S(6)} %copy.33.tlen_ref, s32[1,31]{1,0:T(1,128)S(1)} %get-tuple-element.132.labels_ref, bf16[64,640]{1,0:T(8,128)(2,1)S(1)} %get-tuple-element.134.enc_ref, bf16[32,640]{1,0:T(8,128)(2,1)S(1)} %get-tuple-element.135.pred_ref, ...), custom_call_target="tpu_custom_call" | custom-call | tf_op jit(solution)/shard_map/pallas_call | solution.py:332
  8.4 1.6 %collective-permute-start.2 = (bf16[4,3,2048]{2,1,0:T(4,128)(2,1)S(1)}, bf16[4,3,2048]{2,1,0:T(4,128)(2,1)S(1)}, u32[]{:S(2)}, u32[]{:S(2)}) collective-permute-start(bf16[4,3,2048]{2,1,0:T(4,128)(2,1)S(1)} %pad_maximum_fusion.5), channel_id=1, source_target_pairs={{0,4},{1,5},{2,6},{3,7},{4,0},{5,1},{6,2},{7,3},{8,12},{9,13},{10,... | collective-permute-start | bytes 147464 | tf_op jit(solution)/shard_map/ppermute | solution.py:485
  10.0 1.9 %shard_map.130 = (f32[2048,1024]{1,0:T(8,128)S(1)}, f32[8,2048]{1,0:T(8,128)S(1)}, bf16[640,2048]{1,0:T(8,128)(2,1)S(1)}) custom-call(s32[1]{0:T(128)S(6)} %copy.33.tlen_ref, s32[1,31]{1,0:T(1,128)S(1)} %get-tuple-element.132.labels_ref, bf16[64,640]{1,0:T(8,128)(2,1)S(1)} %get-tuple-element.134.enc_ref, ...), custom_call_target="tpu_custom_call", output_to_operand_aliasing={{0}: (6, {}), {1}: (7, {}), {2}: (8, {})} | custom-call | tf_op jit(solution)/shard_map/pallas_call | solution.py:332
  12.0 0.8 %collective-permute-done.2 = bf16[4,3,2048]{2,1,0:T(4,128)(2,1)S(1)} collective-permute-done((bf16[4,3,2048]{2,1,0:T(4,128)(2,1)S(1)}, bf16[4,3,2048]{2,1,0:T(4,128)(2,1)S(1)}, u32[]{:S(2)}, u32[]{:S(2)}) %collective-permute-start.2) | collective-permute-done | bytes 49184 | tf_op jit(solution)/shard_map/ppermute | solution.py:485
  12.8 2.7 %collective-permute-start.3 = (bf16[8,3,2048]{2,1,0:T(4,128)(2,1)S(1)}, bf16[8,3,2048]{2,1,0:T(4,128)(2,1)S(1)}, u32[]{:S(2)}, u32[]{:S(2)}) collective-permute-start(bf16[8,3,2048]{2,1,0:T(4,128)(2,1)S(1)} %pad_maximum_fusion.2.qa_ref), channel_id=1, source_target_pairs={{0,8},{1,9},{2,10},{3,11},{4,12},{5,13},{6,14},{7,15},{8,0},{9,1},... | collective-permute-start | bytes 294920 | tf_op jit(solution)/shard_map/ppermute | solution.py:485
  16.1 4.1 %shard_map.131 = (f32[2048,1024]{1,0:T(8,128)S(1)}, f32[8,2048]{1,0:T(8,128)S(1)}, bf16[640,2048]{1,0:T(8,128)(2,1)S(1)}) custom-call(s32[1]{0:T(128)S(6)} %copy.33.tlen_ref, s32[1,31]{1,0:T(1,128)S(1)} %get-tuple-element.132.labels_ref, bf16[64,640]{1,0:T(8,128)(2,1)S(1)} %get-tuple-element.134.enc_ref, ...), custom_call_target="tpu_custom_call", output_to_operand_aliasing={{0}: (6, {}), {1}: (7, {}), {2}: (8, {})} | custom-call | tf_op jit(solution)/shard_map/pallas_call | solution.py:332
  20.2 1.0 %collective-permute-done.3.qb_ref = bf16[8,3,2048]{2,1,0:T(4,128)(2,1)S(1)} collective-permute-done((bf16[8,3,2048]{2,1,0:T(4,128)(2,1)S(1)}, bf16[8,3,2048]{2,1,0:T(4,128)(2,1)S(1)}, u32[]{:S(2)}, u32[]{:S(2)}) %collective-permute-start.3) | collective-permute-done | bytes 98336 | tf_op jit(solution)/shard_map/ppermute | solution.py:485
  21.2 7.3 %shard_map.132 = (bf16[2048,1024]{1,0:T(8,128)(2,1)}, f32[1,1]{1,0:T(1,128)}, bf16[656,512]{1,0:T(8,128)(2,1)S(1)}, f32[656,512]{1,0:T(8,128)S(1)}) custom-call(s32[3]{0:T(128)S(1)} %get-tuple-element.131.pick_ref, s32[1]{0:T(128)S(6)} %copy.32.flen_ref, s32[1]{0:T(128)S(6)} %copy.33.tlen_ref, s32[1,31]{1,0:T(1,128)S(1)} %get-tuple-element.132.labels_ref, ...), custom_call_target="tpu_custom_call" | custom-call | tf_op jit(solution)/shard_map/pallas_call | solution.py:391
  28.5 2.1 %collective-permute-done.4.got_ref = bf16[656,512]{1,0:T(8,128)(2,1)S(1)} collective-permute-done((bf16[656,512]{1,0:T(8,128)(2,1)S(1)}, bf16[656,512]{1,0:T(8,128)(2,1)S(1)}, u32[]{:S(2)}, u32[]{:S(2)}) %collective-permute-start.4) | collective-permute-done | bytes 671776 | tf_op jit(solution)/shard_map/ppermute | solution.py:485
  30.8 0.6 collective-permute-start.5
  31.5 4.1 %shard_map.134 = (bf16[64,640]{1,0:T(8,128)(2,1)}, f32[32,640]{1,0:T(8,128)S(1)}) custom-call(bf16[64,640]{1,0:T(8,128)(2,1)S(1)} %get-tuple-element.134.enc_ref, bf16[32,640]{1,0:T(8,128)(2,1)S(1)} %get-tuple-element.135.pred_ref, bf16[2048,1024]{1,0:T(8,128)(2,1)} %get-tuple-element.159.d_ref, bf16[640,1024]{1,0:T(8,128)(2,1)S(1)} %get-tuple-element.136.w_ref), custom_call_target="tpu_custom_call" | custom-call | tf_op jit(solution)/shard_map/pallas_call | solution.py:410
  35.5 2.6 %collective-permute-done.5 = bf16[336,512]{1,0:T(8,128)(2,1)S(1)} collective-permute-done((bf16[336,512]{1,0:T(8,128)(2,1)S(1)}, bf16[336,512]{1,0:T(8,128)(2,1)S(1)}, u32[]{:S(2)}, u32[]{:S(2)}) %collective-permute-start.5) | collective-permute-done | bytes 344096 | tf_op jit(solution)/shard_map/ppermute | solution.py:485
  38.4 0.7 %collective-permute-start.6 = (bf16[176,512]{1,0:T(8,128)(2,1)S(1)}, bf16[176,512]{1,0:T(8,128)(2,1)S(1)}, u32[]{:S(2)}, u32[]{:S(2)}) collective-permute-start(bf16[176,512]{1,0:T(8,128)(2,1)S(1)} %maximum_maximum_fusion), channel_id=1, source_target_pairs={{0,4},{1,3},{2,6},{3,1},{4,0},{5,7},{6,2},{7,5},{8,12},{9,11},{10,... | collective-permute-start | bytes 540680 | tf_op jit(solution)/shard_map/ppermute | solution.py:485
  39.1 4.1 %shard_map.135 = (bf16[64,640]{1,0:T(8,128)(2,1)}, bf16[32,640]{1,0:T(8,128)(2,1)}) custom-call(bf16[64,640]{1,0:T(8,128)(2,1)S(1)} %get-tuple-element.134.enc_ref, bf16[32,640]{1,0:T(8,128)(2,1)S(1)} %get-tuple-element.135.pred_ref, bf16[2048,1024]{1,0:T(8,128)(2,1)} %get-tuple-element.159.d_ref, ...), custom_call_target="tpu_custom_call", output_to_operand_aliasing={{0}: (5, {})} | custom-call | tf_op jit(solution)/shard_map/pallas_call | solution.py:410
  43.2 0.7 %collective-permute-done.6 = bf16[176,512]{1,0:T(8,128)(2,1)S(1)} collective-permute-done((bf16[176,512]{1,0:T(8,128)(2,1)S(1)}, bf16[176,512]{1,0:T(8,128)(2,1)S(1)}, u32[]{:S(2)}, u32[]{:S(2)}) %collective-permute-start.6) | collective-permute-done | bytes 180256 | tf_op jit(solution)/shard_map/ppermute | solution.py:485
  44.1 2.7 %collective-permute-start.8 = (bf16[176,256]{1,0:T(8,128)(2,1)S(1)}, bf16[176,256]{1,0:T(8,128)(2,1)S(1)}, u32[]{:S(2)}, u32[]{:S(2)}) collective-permute-start(bf16[176,256]{1,0:T(8,128)(2,1)S(1)} %get-tuple-element.192), channel_id=1, source_target_pairs={{0,8},{1,9},{2,10},{3,11},{4,12},{5,13},{6,14},{7,15},{8,0},{9,1},... | collective-permute-start | bytes 270344 | tf_op jit(solution)/shard_map/ppermute | solution.py:485
  47.1 4.8 %collective-permute-done.8 = bf16[176,256]{1,0:T(8,128)(2,1)S(1)} collective-permute-done((bf16[176,256]{1,0:T(8,128)(2,1)S(1)}, bf16[176,256]{1,0:T(8,128)(2,1)S(1)}, u32[]{:S(2)}, u32[]{:S(2)}) %collective-permute-start.8) | collective-permute-done | bytes 90144 | tf_op jit(solution)/shard_map/ppermute | solution.py:485
  51.9 1.9 %collective-permute-done.7 = bf16[176,256]{1,0:T(8,128)(2,1)S(1)} collective-permute-done((bf16[176,256]{1,0:T(8,128)(2,1)S(1)}, bf16[176,256]{1,0:T(8,128)(2,1)S(1)}, u32[]{:S(2)}, u32[]{:S(2)}) %collective-permute-start.7) | collective-permute-done | bytes 90144 | tf_op jit(solution)/shard_map/ppermute | solution.py:485
  53.9 2.0 %collective-permute-start.9 = (bf16[160,256]{1,0:T(8,128)(2,1)S(1)}, bf16[160,256]{1,0:T(8,128)(2,1)S(1)}, u32[]{:S(2)}, u32[]{:S(2)}) collective-permute-start(bf16[160,256]{1,0:T(8,128)(2,1)S(1)} %add_convert_fusion), channel_id=1, source_target_pairs={{0,4},{1,3},{2,6},{3,1},{4,0},{5,7},{6,2},{7,5},{8,12},{9,11},{10,... | collective-permute-start | bytes 245768 | tf_op jit(solution)/shard_map/ppermute | solution.py:485
  56.0 2.3 %collective-permute-done.10 = bf16[160,256]{1,0:T(8,128)(2,1)S(1)} collective-permute-done((bf16[160,256]{1,0:T(8,128)(2,1)S(1)}, bf16[160,256]{1,0:T(8,128)(2,1)S(1)}, u32[]{:S(2)}, u32[]{:S(2)}) %collective-permute-start.10) | collective-permute-done | bytes 81952 | tf_op jit(solution)/shard_map/ppermute | solution.py:485
  58.3 0.8 %collective-permute-done.9 = bf16[160,256]{1,0:T(8,128)(2,1)S(1)} collective-permute-done((bf16[160,256]{1,0:T(8,128)(2,1)S(1)}, bf16[160,256]{1,0:T(8,128)(2,1)S(1)}, u32[]{:S(2)}, u32[]{:S(2)}) %collective-permute-start.9) | collective-permute-done | bytes 81952 | tf_op jit(solution)/shard_map/ppermute | solution.py:485
  59.1 1.2 %collective-permute-start.12 = (bf16[320,256]{1,0:T(8,128)(2,1)S(1)}, bf16[320,256]{1,0:T(8,128)(2,1)S(1)}, u32[]{:S(2)}, u32[]{:S(2)}) collective-permute-start(bf16[320,256]{1,0:T(8,128)(2,1)S(1)} %maximum_select_fusion.2), channel_id=1, source_target_pairs={{0,2},{1,5},{2,0},{3,7},{4,6},{5,1},{6,4},{7,3},{8,10},{9,13},{10,... | collective-permute-start | bytes 491528 | tf_op jit(solution)/shard_map/ppermute | solution.py:485
  60.4 0.9 %collective-permute-start.11 = (bf16[320,256]{1,0:T(8,128)(2,1)S(1)}, bf16[320,256]{1,0:T(8,128)(2,1)S(1)}, u32[]{:S(2)}, u32[]{:S(2)}) collective-permute-start(bf16[320,256]{1,0:T(8,128)(2,1)S(1)} %maximum_select_fusion.3), channel_id=1, source_target_pairs={{0,2},{1,5},{2,0},{3,7},{4,6},{5,1},{6,4},{7,3},{8,10},{9,13},{10,... | collective-permute-start | bytes 491528 | tf_op jit(solution)/shard_map/ppermute | solution.py:485
  61.3 3.2 %collective-permute-done.12 = bf16[320,256]{1,0:T(8,128)(2,1)S(1)} collective-permute-done((bf16[320,256]{1,0:T(8,128)(2,1)S(1)}, bf16[320,256]{1,0:T(8,128)(2,1)S(1)}, u32[]{:S(2)}, u32[]{:S(2)}) %collective-permute-start.12) | collective-permute-done | bytes 163872 | tf_op jit(solution)/shard_map/ppermute | solution.py:485
  64.6 1.6 %collective-permute-done.11 = bf16[320,256]{1,0:T(8,128)(2,1)S(1)} collective-permute-done((bf16[320,256]{1,0:T(8,128)(2,1)S(1)}, bf16[320,256]{1,0:T(8,128)(2,1)S(1)}, u32[]{:S(2)}, u32[]{:S(2)}) %collective-permute-start.11) | collective-permute-done | bytes 163872 | tf_op jit(solution)/shard_map/ppermute | solution.py:485
  66.5 0.5 collective-permute-start.14
  67.0 1.1 %shard_map.136 = (f32[640,1024]{1,0:T(8,128)}, f32[1,1024]{1,0:T(1,128)}) custom-call(bf16[656,256]{1,0:T(8,128)(2,1)S(1)} %get-tuple-element.190.refs_0_, bf16[656,256]{1,0:T(8,128)(2,1)S(1)} %get-tuple-element.189.refs_1_), custom_call_target="tpu_custom_call" | custom-call | tf_op jit(solution)/shard_map/pallas_call | solution.py:304
  68.1 0.5 collective-permute-done.14.refs_1_
  68.6 1.1 %shard_map.137 = (f32[640,1024]{1,0:T(8,128)}, f32[1,1024]{1,0:T(1,128)}) custom-call(bf16[656,256]{1,0:T(8,128)(2,1)S(1)} %collective-permute-done.13.refs_0_, bf16[656,256]{1,0:T(8,128)(2,1)S(1)} %collective-permute-done.14.refs_1_, f32[640,1024]{1,0:T(8,128)} %get-tuple-element.175.refs_2_, ...), custom_call_target="tpu_custom_call", output_to_operand_aliasing={{0}: (2, {}), {1}: (3, {})} | custom-call | tf_op jit(solution)/shard_map/pallas_call | solution.py:304
  (34 shorter events, 1.7 us)
Async XLA Ops:
  0.6 2.5 %collective-permute-start = (bf16[1,3,2048]{2,1,0:T(4,128)(2,1)}, bf16[1,3,2048]{2,1,0:T(4,128)(2,1)S(1)}, u32[]{:S(2)}, u32[]{:S(2)}) collective-permute-start(bf16[1,3,2048]{2,1,0:T(4,128)(2,1)} %refs_5_.1), channel_id=1, source_target_pairs={{0,1},{1,0},{2,3},{3,2},{4,5},{5,4},{6,7},{7,6},{8,9},{9,8},{10,11... | collective-permute-start | bytes 36872 | tf_op jit(solution)/shard_map/ppermute | solution.py:485
  3.2 5.2 %collective-permute-start.1 = (bf16[2,3,2048]{2,1,0:T(4,128)(2,1)S(1)}, bf16[2,3,2048]{2,1,0:T(4,128)(2,1)S(1)}, u32[]{:S(2)}, u32[]{:S(2)}) collective-permute-start(bf16[2,3,2048]{2,1,0:T(4,128)(2,1)S(1)} %pad_maximum_fusion.6), channel_id=1, source_target_pairs={{0,2},{1,3},{2,0},{3,1},{4,6},{5,7},{6,4},{7,5},{8,10},{9,11},{10,... | collective-permute-start | bytes 73736 | tf_op jit(solution)/shard_map/ppermute | solution.py:485
  8.4 4.3 %collective-permute-start.2 = (bf16[4,3,2048]{2,1,0:T(4,128)(2,1)S(1)}, bf16[4,3,2048]{2,1,0:T(4,128)(2,1)S(1)}, u32[]{:S(2)}, u32[]{:S(2)}) collective-permute-start(bf16[4,3,2048]{2,1,0:T(4,128)(2,1)S(1)} %pad_maximum_fusion.5), channel_id=1, source_target_pairs={{0,4},{1,5},{2,6},{3,7},{4,0},{5,1},{6,2},{7,3},{8,12},{9,13},{10,... | collective-permute-start | bytes 147464 | tf_op jit(solution)/shard_map/ppermute | solution.py:485
  12.8 8.4 %collective-permute-start.3 = (bf16[8,3,2048]{2,1,0:T(4,128)(2,1)S(1)}, bf16[8,3,2048]{2,1,0:T(4,128)(2,1)S(1)}, u32[]{:S(2)}, u32[]{:S(2)}) collective-permute-start(bf16[8,3,2048]{2,1,0:T(4,128)(2,1)S(1)} %pad_maximum_fusion.2.qa_ref), channel_id=1, source_target_pairs={{0,8},{1,9},{2,10},{3,11},{4,12},{5,13},{6,14},{7,15},{8,0},{9,1},... | collective-permute-start | bytes 294920 | tf_op jit(solution)/shard_map/ppermute | solution.py:485
  28.5 2.1 %collective-permute-start.4 = (bf16[656,512]{1,0:T(8,128)(2,1)S(1)}, bf16[656,512]{1,0:T(8,128)(2,1)S(1)}, u32[]{:S(2)}, u32[]{:S(2)}) collective-permute-start(bf16[656,512]{1,0:T(8,128)(2,1)S(1)} %get-tuple-element.146), channel_id=1, source_target_pairs={{0,1},{1,0},{2,3},{3,2},{4,5},{5,4},{6,7},{7,6},{8,9},{9,8},{10,11... | collective-permute-start | bytes 2015240 | tf_op jit(solution)/shard_map/ppermute | solution.py:485
  30.8 7.3 %collective-permute-start.5 = (bf16[336,512]{1,0:T(8,128)(2,1)S(1)}, bf16[336,512]{1,0:T(8,128)(2,1)S(1)}, u32[]{:S(2)}, u32[]{:S(2)}) collective-permute-start(bf16[336,512]{1,0:T(8,128)(2,1)S(1)} %get-tuple-element.151), channel_id=1, source_target_pairs={{0,2},{1,5},{2,0},{3,7},{4,6},{5,1},{6,4},{7,3},{8,10},{9,13},{10,... | collective-permute-start | bytes 1032200 | tf_op jit(solution)/shard_map/ppermute | solution.py:485
  38.4 5.6 %collective-permute-start.6 = (bf16[176,512]{1,0:T(8,128)(2,1)S(1)}, bf16[176,512]{1,0:T(8,128)(2,1)S(1)}, u32[]{:S(2)}, u32[]{:S(2)}) collective-permute-start(bf16[176,512]{1,0:T(8,128)(2,1)S(1)} %maximum_maximum_fusion), channel_id=1, source_target_pairs={{0,4},{1,3},{2,6},{3,1},{4,0},{5,7},{6,2},{7,5},{8,12},{9,11},{10,... | collective-permute-start | bytes 540680 | tf_op jit(solution)/shard_map/ppermute | solution.py:485
  44.1 7.8 %collective-permute-start.8 = (bf16[176,256]{1,0:T(8,128)(2,1)S(1)}, bf16[176,256]{1,0:T(8,128)(2,1)S(1)}, u32[]{:S(2)}, u32[]{:S(2)}) collective-permute-start(bf16[176,256]{1,0:T(8,128)(2,1)S(1)} %get-tuple-element.192), channel_id=1, source_target_pairs={{0,8},{1,9},{2,10},{3,11},{4,12},{5,13},{6,14},{7,15},{8,0},{9,1},... | collective-permute-start | bytes 270344 | tf_op jit(solution)/shard_map/ppermute | solution.py:485
  46.8 7.0 %collective-permute-start.7 = (bf16[176,256]{1,0:T(8,128)(2,1)S(1)}, bf16[176,256]{1,0:T(8,128)(2,1)S(1)}, u32[]{:S(2)}, u32[]{:S(2)}) collective-permute-start(bf16[176,256]{1,0:T(8,128)(2,1)S(1)} %get-tuple-element.191), channel_id=1, source_target_pairs={{0,8},{1,9},{2,10},{3,11},{4,12},{5,13},{6,14},{7,15},{8,0},{9,1},... | collective-permute-start | bytes 270344 | tf_op jit(solution)/shard_map/ppermute | solution.py:485
  53.8 4.4 %collective-permute-start.10 = (bf16[160,256]{1,0:T(8,128)(2,1)S(1)}, bf16[160,256]{1,0:T(8,128)(2,1)S(1)}, u32[]{:S(2)}, u32[]{:S(2)}) collective-permute-start(bf16[160,256]{1,0:T(8,128)(2,1)S(1)} %add_convert_fusion.1), channel_id=1, source_target_pairs={{0,4},{1,3},{2,6},{3,1},{4,0},{5,7},{6,2},{7,5},{8,12},{9,11},{10,... | collective-permute-start | bytes 245768 | tf_op jit(solution)/shard_map/ppermute | solution.py:485
  53.9 5.2 %collective-permute-start.9 = (bf16[160,256]{1,0:T(8,128)(2,1)S(1)}, bf16[160,256]{1,0:T(8,128)(2,1)S(1)}, u32[]{:S(2)}, u32[]{:S(2)}) collective-permute-start(bf16[160,256]{1,0:T(8,128)(2,1)S(1)} %add_convert_fusion), channel_id=1, source_target_pairs={{0,4},{1,3},{2,6},{3,1},{4,0},{5,7},{6,2},{7,5},{8,12},{9,11},{10,... | collective-permute-start | bytes 245768 | tf_op jit(solution)/shard_map/ppermute | solution.py:485
  59.1 5.3 %collective-permute-start.12 = (bf16[320,256]{1,0:T(8,128)(2,1)S(1)}, bf16[320,256]{1,0:T(8,128)(2,1)S(1)}, u32[]{:S(2)}, u32[]{:S(2)}) collective-permute-start(bf16[320,256]{1,0:T(8,128)(2,1)S(1)} %maximum_select_fusion.2), channel_id=1, source_target_pairs={{0,2},{1,5},{2,0},{3,7},{4,6},{5,1},{6,4},{7,3},{8,10},{9,13},{10,... | collective-permute-start | bytes 491528 | tf_op jit(solution)/shard_map/ppermute | solution.py:485
  60.4 5.8 %collective-permute-start.11 = (bf16[320,256]{1,0:T(8,128)(2,1)S(1)}, bf16[320,256]{1,0:T(8,128)(2,1)S(1)}, u32[]{:S(2)}, u32[]{:S(2)}) collective-permute-start(bf16[320,256]{1,0:T(8,128)(2,1)S(1)} %maximum_select_fusion.3), channel_id=1, source_target_pairs={{0,2},{1,5},{2,0},{3,7},{4,6},{5,1},{6,4},{7,3},{8,10},{9,13},{10,... | collective-permute-start | bytes 491528 | tf_op jit(solution)/shard_map/ppermute | solution.py:485
  66.4 1.7 %collective-permute-start.13 = (bf16[656,256]{1,0:T(8,128)(2,1)S(1)}, bf16[656,256]{1,0:T(8,128)(2,1)S(1)}, u32[]{:S(2)}, u32[]{:S(2)}) collective-permute-start(bf16[656,256]{1,0:T(8,128)(2,1)S(1)} %get-tuple-element.190.refs_0_), channel_id=1, source_target_pairs={{0,1},{1,0},{2,3},{3,2},{4,5},{5,4},{6,7},{7,6},{8,9},{9,8},{10,11... | collective-permute-start | bytes 1007624 | tf_op jit(solution)/shard_map/ppermute | solution.py:485
  66.5 2.1 %collective-permute-start.14 = (bf16[656,256]{1,0:T(8,128)(2,1)S(1)}, bf16[656,256]{1,0:T(8,128)(2,1)S(1)}, u32[]{:S(2)}, u32[]{:S(2)}) collective-permute-start(bf16[656,256]{1,0:T(8,128)(2,1)S(1)} %get-tuple-element.189.refs_1_), channel_id=1, source_target_pairs={{0,1},{1,0},{2,3},{3,2},{4,5},{5,4},{6,7},{7,6},{8,9},{9,8},{10,11... | collective-permute-start | bytes 1007624 | tf_op jit(solution)/shard_map/ppermute | solution.py:485

commit v10 on v9

--- a/solution.py
+++ b/solution.py
@@ -93,6 +93,7 @@
     sub_frames = SUB // tok_slots
     target = target_column(labels_ref, tlen_ref[0], tok_slots, sub_frames)
     lane = lax.broadcasted_iota(jnp.int32, (SUB, LANES), 1)
+    offset = target - lane
     parts = rows // SUB
 
     def multiply(k):
@@ -116,13 +117,13 @@
             shifted = logit_scr[k % 2, :, cols] + b_ref[:, cols] - row_max
             e = jnp.exp(shifted)
             e_ref[place, cols] = e
-            hot = lane == target - j * LANES
+            hot = offset == j * LANES
             rest = jnp.where(hot, 0.0, e)
             if j == 0:
                 z_blank = shifted[:, 0:1]
                 rest = jnp.where(lane == 0, 0.0, rest)
             rest_acc = rest_acc + rest
-            label_acc = label_acc + jnp.where(hot, shifted, 0.0)
+            label_acc = jnp.where(hot, shifted, label_acc)
         rest_sum = jnp.sum(rest_acc, axis=1, keepdims=True)
         z_label = jnp.sum(label_acc, axis=1, keepdims=True)
         packed = jnp.where(lane == 0, rest_sum, jnp.where(lane == 1, z_blank, z_label))

time: 70.1 us -> 70.2 us (level)
  transfers between devices with their start and end apart: 15 -> 15, of which waited for: 12 -> 12; matrix products, arithmetic and copies ran while one was open for 1% -> 1% of each run, Pallas kernels for 27% -> 28%
where the time goes in v10:
time: 70.2 us; the launch traced here: 70 us
  Pallas kernels  28 us (40%)
  waiting for transfers between devices  22.1 us (31%)
  starting transfers between devices  16.5 us (24%)
  between operations  2.29 us (3%)
  other arithmetic  1.01 us (1%)
    ppermute x15, waiting for transfers between devices, exchange(): return lax.ppermute(value, 'dp', pairs)  22.1 us
    ppermute x15, starting transfers between devices, exchange(): return lax.ppermute(value, 'dp', pairs)  16.5 us
    pallas_call x3, Pallas kernels, forward(): pl.pallas_call(functools.partial(forward_kernel, begin), grid=(blocks,),...  8.21 us
    pallas_call x2, Pallas kernels, input_gradients(): pl.pallas_call(functools.partial(input_kernel, begin, last), grid=(cells...  8.13 us
    pallas_call x1, Pallas kernels, gradients(): pl.pallas_call(functools.partial(grad_kernel, blocks), grid_spec=grid_spe...  7.29 us
    pallas_call x2, Pallas kernels, widen(): pl.pallas_call(functools.partial(final_kernel, mine), in_specs=[pl.BlockS...  2.23 us
    pallas_call x1, Pallas kernels, stage(): pl.pallas_call(stage_kernel, in_specs=[anywhere] * (1 + len(arrays)), out...  1.98 us
  transfers between devices with their start and end apart: 15, of which 12 were waited for; matrix products, arithmetic and copies ran while one was open for 1% of the time, Pallas kernels for 28%

profile of v10, /device:TPU:0, one launch (start us, length us, event | category | flops | bytes accessed | tf_op | source)
XLA Modules:
  0.0 70.0 jit_solution(14533920693974277450)
XLA Ops:
  0.6 0.5 collective-permute-start
  1.2 2.0 %shard_map.128 = (bf16[640,1024]{1,0:T(8,128)(2,1)S(1)}, bf16[64,640]{1,0:T(8,128)(2,1)S(1)}, bf16[32,640]{1,0:T(8,128)(2,1)S(1)}, f32[1,1024]{1,0:T(1,128)S(1)}...) custom-call(s32[16]{0:T(128)} %assignment_ref.1, bf16[640,1024]{1,0:T(8,128)(2,1)} %refs_0_.1, ...), custom_call_target="tpu_custom_call" | custom-call | tf_op jit(solution)/shard_map/pallas_call | solution.py:59
  3.2 2.6 %collective-permute-start.1 = (bf16[2,3,2048]{2,1,0:T(4,128)(2,1)S(1)}, bf16[2,3,2048]{2,1,0:T(4,128)(2,1)S(1)}, u32[]{:S(2)}, u32[]{:S(2)}) collective-permute-start(bf16[2,3,2048]{2,1,0:T(4,128)(2,1)S(1)} %pad_maximum_fusion.6), channel_id=1, source_target_pairs={{0,2},{1,3},{2,0},{3,1},{4,6},{5,7},{6,4},{7,5},{8,10},{9,11},{10,... | collective-permute-start | bytes 73736 | tf_op jit(solution)/shard_map/ppermute | solution.py:486
  6.4 2.0 %shard_map.129 = (f32[2048,1024]{1,0:T(8,128)S(1)}, f32[8,2048]{1,0:T(8,128)S(1)}, bf16[640,2048]{1,0:T(8,128)(2,1)S(1)}) custom-call(s32[1]{0:T(128)S(6)} %copy.33.tlen_ref, s32[1,31]{1,0:T(1,128)S(1)} %get-tuple-element.132.labels_ref, bf16[64,640]{1,0:T(8,128)(2,1)S(1)} %get-tuple-element.134.enc_ref, bf16[32,640]{1,0:T(8,128)(2,1)S(1)} %get-tuple-element.135.pred_ref, ...), custom_call_target="tpu_custom_call" | custom-call | tf_op jit(solution)/shard_map/pallas_call | solution.py:333
  8.5 1.6 %collective-permute-start.2 = (bf16[4,3,2048]{2,1,0:T(4,128)(2,1)S(1)}, bf16[4,3,2048]{2,1,0:T(4,128)(2,1)S(1)}, u32[]{:S(2)}, u32[]{:S(2)}) collective-permute-start(bf16[4,3,2048]{2,1,0:T(4,128)(2,1)S(1)} %pad_maximum_fusion.5), channel_id=1, source_target_pairs={{0,4},{1,5},{2,6},{3,7},{4,0},{5,1},{6,2},{7,3},{8,12},{9,13},{10,... | collective-permute-start | bytes 147464 | tf_op jit(solution)/shard_map/ppermute | solution.py:486
  10.1 2.0 %shard_map.130 = (f32[2048,1024]{1,0:T(8,128)S(1)}, f32[8,2048]{1,0:T(8,128)S(1)}, bf16[640,2048]{1,0:T(8,128)(2,1)S(1)}) custom-call(s32[1]{0:T(128)S(6)} %copy.33.tlen_ref, s32[1,31]{1,0:T(1,128)S(1)} %get-tuple-element.132.labels_ref, bf16[64,640]{1,0:T(8,128)(2,1)S(1)} %get-tuple-element.134.enc_ref, ...), custom_call_target="tpu_custom_call", output_to_operand_aliasing={{0}: (6, {}), {1}: (7, {}), {2}: (8, {})} | custom-call | tf_op jit(solution)/shard_map/pallas_call | solution.py:333
  12.1 0.7 collective-permute-done.2
  12.9 2.7 %collective-permute-start.3 = (bf16[8,3,2048]{2,1,0:T(4,128)(2,1)S(1)}, bf16[8,3,2048]{2,1,0:T(4,128)(2,1)S(1)}, u32[]{:S(2)}, u32[]{:S(2)}) collective-permute-start(bf16[8,3,2048]{2,1,0:T(4,128)(2,1)S(1)} %pad_maximum_fusion.2.qa_ref), channel_id=1, source_target_pairs={{0,8},{1,9},{2,10},{3,11},{4,12},{5,13},{6,14},{7,15},{8,0},{9,1},... | collective-permute-start | bytes 294920 | tf_op jit(solution)/shard_map/ppermute | solution.py:486
  16.2 4.2 %shard_map.131 = (f32[2048,1024]{1,0:T(8,128)S(1)}, f32[8,2048]{1,0:T(8,128)S(1)}, bf16[640,2048]{1,0:T(8,128)(2,1)S(1)}) custom-call(s32[1]{0:T(128)S(6)} %copy.33.tlen_ref, s32[1,31]{1,0:T(1,128)S(1)} %get-tuple-element.132.labels_ref, bf16[64,640]{1,0:T(8,128)(2,1)S(1)} %get-tuple-element.134.enc_ref, ...), custom_call_target="tpu_custom_call", output_to_operand_aliasing={{0}: (6, {}), {1}: (7, {}), {2}: (8, {})} | custom-call | tf_op jit(solution)/shard_map/pallas_call | solution.py:333
  20.4 0.9 %collective-permute-done.3.qb_ref = bf16[8,3,2048]{2,1,0:T(4,128)(2,1)S(1)} collective-permute-done((bf16[8,3,2048]{2,1,0:T(4,128)(2,1)S(1)}, bf16[8,3,2048]{2,1,0:T(4,128)(2,1)S(1)}, u32[]{:S(2)}, u32[]{:S(2)}) %collective-permute-start.3) | collective-permute-done | bytes 98336 | tf_op jit(solution)/shard_map/ppermute | solution.py:486
  21.3 7.3 %shard_map.132 = (bf16[2048,1024]{1,0:T(8,128)(2,1)}, f32[1,1]{1,0:T(1,128)}, bf16[656,512]{1,0:T(8,128)(2,1)S(1)}, f32[656,512]{1,0:T(8,128)S(1)}) custom-call(s32[3]{0:T(128)S(1)} %get-tuple-element.131.pick_ref, s32[1]{0:T(128)S(6)} %copy.32.flen_ref, s32[1]{0:T(128)S(6)} %copy.33.tlen_ref, s32[1,31]{1,0:T(1,128)S(1)} %get-tuple-element.132.labels_ref, ...), custom_call_target="tpu_custom_call" | custom-call | tf_op jit(solution)/shard_map/pallas_call | solution.py:392
  28.6 2.1 %collective-permute-done.4.got_ref = bf16[656,512]{1,0:T(8,128)(2,1)S(1)} collective-permute-done((bf16[656,512]{1,0:T(8,128)(2,1)S(1)}, bf16[656,512]{1,0:T(8,128)(2,1)S(1)}, u32[]{:S(2)}, u32[]{:S(2)}) %collective-permute-start.4) | collective-permute-done | bytes 671776 | tf_op jit(solution)/shard_map/ppermute | solution.py:486
  30.9 0.6 collective-permute-start.5
  31.6 4.1 %shard_map.134 = (bf16[64,640]{1,0:T(8,128)(2,1)}, f32[32,640]{1,0:T(8,128)S(1)}) custom-call(bf16[64,640]{1,0:T(8,128)(2,1)S(1)} %get-tuple-element.134.enc_ref, bf16[32,640]{1,0:T(8,128)(2,1)S(1)} %get-tuple-element.135.pred_ref, bf16[2048,1024]{1,0:T(8,128)(2,1)} %get-tuple-element.159.d_ref, bf16[640,1024]{1,0:T(8,128)(2,1)S(1)} %get-tuple-element.136.w_ref), custom_call_target="tpu_custom_call" | custom-call | tf_op jit(solution)/shard_map/pallas_call | solution.py:411
  35.7 2.6 %collective-permute-done.5 = bf16[336,512]{1,0:T(8,128)(2,1)S(1)} collective-permute-done((bf16[336,512]{1,0:T(8,128)(2,1)S(1)}, bf16[336,512]{1,0:T(8,128)(2,1)S(1)}, u32[]{:S(2)}, u32[]{:S(2)}) %collective-permute-start.5) | collective-permute-done | bytes 344096 | tf_op jit(solution)/shard_map/ppermute | solution.py:486
  38.5 0.8 %collective-permute-start.6 = (bf16[176,512]{1,0:T(8,128)(2,1)S(1)}, bf16[176,512]{1,0:T(8,128)(2,1)S(1)}, u32[]{:S(2)}, u32[]{:S(2)}) collective-permute-start(bf16[176,512]{1,0:T(8,128)(2,1)S(1)} %maximum_maximum_fusion), channel_id=1, source_target_pairs={{0,4},{1,3},{2,6},{3,1},{4,0},{5,7},{6,2},{7,5},{8,12},{9,11},{10,... | collective-permute-start | bytes 540680 | tf_op jit(solution)/shard_map/ppermute | solution.py:486
  39.3 4.1 %shard_map.135 = (bf16[64,640]{1,0:T(8,128)(2,1)}, bf16[32,640]{1,0:T(8,128)(2,1)}) custom-call(bf16[64,640]{1,0:T(8,128)(2,1)S(1)} %get-tuple-element.134.enc_ref, bf16[32,640]{1,0:T(8,128)(2,1)S(1)} %get-tuple-element.135.pred_ref, bf16[2048,1024]{1,0:T(8,128)(2,1)} %get-tuple-element.159.d_ref, ...), custom_call_target="tpu_custom_call", output_to_operand_aliasing={{0}: (5, {})} | custom-call | tf_op jit(solution)/shard_map/pallas_call | solution.py:411
  43.4 0.7 %collective-permute-done.6 = bf16[176,512]{1,0:T(8,128)(2,1)S(1)} collective-permute-done((bf16[176,512]{1,0:T(8,128)(2,1)S(1)}, bf16[176,512]{1,0:T(8,128)(2,1)S(1)}, u32[]{:S(2)}, u32[]{:S(2)}) %collective-permute-start.6) | collective-permute-done | bytes 180256 | tf_op jit(solution)/shard_map/ppermute | solution.py:486
  44.2 2.6 %collective-permute-start.8 = (bf16[176,256]{1,0:T(8,128)(2,1)S(1)}, bf16[176,256]{1,0:T(8,128)(2,1)S(1)}, u32[]{:S(2)}, u32[]{:S(2)}) collective-permute-start(bf16[176,256]{1,0:T(8,128)(2,1)S(1)} %get-tuple-element.192), channel_id=1, source_target_pairs={{0,8},{1,9},{2,10},{3,11},{4,12},{5,13},{6,14},{7,15},{8,0},{9,1},... | collective-permute-start | bytes 270344 | tf_op jit(solution)/shard_map/ppermute | solution.py:486
  47.2 4.8 %collective-permute-done.8 = bf16[176,256]{1,0:T(8,128)(2,1)S(1)} collective-permute-done((bf16[176,256]{1,0:T(8,128)(2,1)S(1)}, bf16[176,256]{1,0:T(8,128)(2,1)S(1)}, u32[]{:S(2)}, u32[]{:S(2)}) %collective-permute-start.8) | collective-permute-done | bytes 90144 | tf_op jit(solution)/shard_map/ppermute | solution.py:486
  52.1 1.9 %collective-permute-done.7 = bf16[176,256]{1,0:T(8,128)(2,1)S(1)} collective-permute-done((bf16[176,256]{1,0:T(8,128)(2,1)S(1)}, bf16[176,256]{1,0:T(8,128)(2,1)S(1)}, u32[]{:S(2)}, u32[]{:S(2)}) %collective-permute-start.7) | collective-permute-done | bytes 90144 | tf_op jit(solution)/shard_map/ppermute | solution.py:486
  54.0 2.1 %collective-permute-start.9 = (bf16[160,256]{1,0:T(8,128)(2,1)S(1)}, bf16[160,256]{1,0:T(8,128)(2,1)S(1)}, u32[]{:S(2)}, u32[]{:S(2)}) collective-permute-start(bf16[160,256]{1,0:T(8,128)(2,1)S(1)} %add_convert_fusion), channel_id=1, source_target_pairs={{0,4},{1,3},{2,6},{3,1},{4,0},{5,7},{6,2},{7,5},{8,12},{9,11},{10,... | collective-permute-start | bytes 245768 | tf_op jit(solution)/shard_map/ppermute | solution.py:486
  56.1 2.3 %collective-permute-done.10 = bf16[160,256]{1,0:T(8,128)(2,1)S(1)} collective-permute-done((bf16[160,256]{1,0:T(8,128)(2,1)S(1)}, bf16[160,256]{1,0:T(8,128)(2,1)S(1)}, u32[]{:S(2)}, u32[]{:S(2)}) %collective-permute-start.10) | collective-permute-done | bytes 81952 | tf_op jit(solution)/shard_map/ppermute | solution.py:486
  58.5 0.8 %collective-permute-done.9 = bf16[160,256]{1,0:T(8,128)(2,1)S(1)} collective-permute-done((bf16[160,256]{1,0:T(8,128)(2,1)S(1)}, bf16[160,256]{1,0:T(8,128)(2,1)S(1)}, u32[]{:S(2)}, u32[]{:S(2)}) %collective-permute-start.9) | collective-permute-done | bytes 81952 | tf_op jit(solution)/shard_map/ppermute | solution.py:486
  59.3 1.2 %collective-permute-start.12 = (bf16[320,256]{1,0:T(8,128)(2,1)S(1)}, bf16[320,256]{1,0:T(8,128)(2,1)S(1)}, u32[]{:S(2)}, u32[]{:S(2)}) collective-permute-start(bf16[320,256]{1,0:T(8,128)(2,1)S(1)} %maximum_select_fusion.2), channel_id=1, source_target_pairs={{0,2},{1,5},{2,0},{3,7},{4,6},{5,1},{6,4},{7,3},{8,10},{9,13},{10,... | collective-permute-start | bytes 491528 | tf_op jit(solution)/shard_map/ppermute | solution.py:486
  60.5 0.9 %collective-permute-start.11 = (bf16[320,256]{1,0:T(8,128)(2,1)S(1)}, bf16[320,256]{1,0:T(8,128)(2,1)S(1)}, u32[]{:S(2)}, u32[]{:S(2)}) collective-permute-start(bf16[320,256]{1,0:T(8,128)(2,1)S(1)} %maximum_select_fusion.3), channel_id=1, source_target_pairs={{0,2},{1,5},{2,0},{3,7},{4,6},{5,1},{6,4},{7,3},{8,10},{9,13},{10,... | collective-permute-start | bytes 491528 | tf_op jit(solution)/shard_map/ppermute | solution.py:486
  61.4 3.2 %collective-permute-done.12 = bf16[320,256]{1,0:T(8,128)(2,1)S(1)} collective-permute-done((bf16[320,256]{1,0:T(8,128)(2,1)S(1)}, bf16[320,256]{1,0:T(8,128)(2,1)S(1)}, u32[]{:S(2)}, u32[]{:S(2)}) %collective-permute-start.12) | collective-permute-done | bytes 163872 | tf_op jit(solution)/shard_map/ppermute | solution.py:486
  64.7 1.6 %collective-permute-done.11 = bf16[320,256]{1,0:T(8,128)(2,1)S(1)} collective-permute-done((bf16[320,256]{1,0:T(8,128)(2,1)S(1)}, bf16[320,256]{1,0:T(8,128)(2,1)S(1)}, u32[]{:S(2)}, u32[]{:S(2)}) %collective-permute-start.11) | collective-permute-done | bytes 163872 | tf_op jit(solution)/shard_map/ppermute | solution.py:486
  66.6 0.5 collective-permute-start.14
  67.1 1.1 %shard_map.136 = (f32[640,1024]{1,0:T(8,128)}, f32[1,1024]{1,0:T(1,128)}) custom-call(bf16[656,256]{1,0:T(8,128)(2,1)S(1)} %get-tuple-element.190.refs_0_, bf16[656,256]{1,0:T(8,128)(2,1)S(1)} %get-tuple-element.189.refs_1_), custom_call_target="tpu_custom_call" | custom-call | tf_op jit(solution)/shard_map/pallas_call | solution.py:305
  68.3 0.5 collective-permute-done.14.refs_1_
  68.7 1.1 %shard_map.137 = (f32[640,1024]{1,0:T(8,128)}, f32[1,1024]{1,0:T(1,128)}) custom-call(bf16[656,256]{1,0:T(8,128)(2,1)S(1)} %collective-permute-done.13.refs_0_, bf16[656,256]{1,0:T(8,128)(2,1)S(1)} %collective-permute-done.14.refs_1_, f32[640,1024]{1,0:T(8,128)} %get-tuple-element.175.refs_2_, ...), custom_call_target="tpu_custom_call", output_to_operand_aliasing={{0}: (2, {}), {1}: (3, {})} | custom-call | tf_op jit(solution)/shard_map/pallas_call | solution.py:305
  (34 shorter events, 1.8 us)
Async XLA Ops:
  0.6 2.5 %collective-permute-start = (bf16[1,3,2048]{2,1,0:T(4,128)(2,1)}, bf16[1,3,2048]{2,1,0:T(4,128)(2,1)S(1)}, u32[]{:S(2)}, u32[]{:S(2)}) collective-permute-start(bf16[1,3,2048]{2,1,0:T(4,128)(2,1)} %refs_5_.1), channel_id=1, source_target_pairs={{0,1},{1,0},{2,3},{3,2},{4,5},{5,4},{6,7},{7,6},{8,9},{9,8},{10,11... | collective-permute-start | bytes 36872 | tf_op jit(solution)/shard_map/ppermute | solution.py:486
  3.2 5.2 %collective-permute-start.1 = (bf16[2,3,2048]{2,1,0:T(4,128)(2,1)S(1)}, bf16[2,3,2048]{2,1,0:T(4,128)(2,1)S(1)}, u32[]{:S(2)}, u32[]{:S(2)}) collective-permute-start(bf16[2,3,2048]{2,1,0:T(4,128)(2,1)S(1)} %pad_maximum_fusion.6), channel_id=1, source_target_pairs={{0,2},{1,3},{2,0},{3,1},{4,6},{5,7},{6,4},{7,5},{8,10},{9,11},{10,... | collective-permute-start | bytes 73736 | tf_op jit(solution)/shard_map/ppermute | solution.py:486
  8.5 4.3 %collective-permute-start.2 = (bf16[4,3,2048]{2,1,0:T(4,128)(2,1)S(1)}, bf16[4,3,2048]{2,1,0:T(4,128)(2,1)S(1)}, u32[]{:S(2)}, u32[]{:S(2)}) collective-permute-start(bf16[4,3,2048]{2,1,0:T(4,128)(2,1)S(1)} %pad_maximum_fusion.5), channel_id=1, source_target_pairs={{0,4},{1,5},{2,6},{3,7},{4,0},{5,1},{6,2},{7,3},{8,12},{9,13},{10,... | collective-permute-start | bytes 147464 | tf_op jit(solution)/shard_map/ppermute | solution.py:486
  12.9 8.4 %collective-permute-start.3 = (bf16[8,3,2048]{2,1,0:T(4,128)(2,1)S(1)}, bf16[8,3,2048]{2,1,0:T(4,128)(2,1)S(1)}, u32[]{:S(2)}, u32[]{:S(2)}) collective-permute-start(bf16[8,3,2048]{2,1,0:T(4,128)(2,1)S(1)} %pad_maximum_fusion.2.qa_ref), channel_id=1, source_target_pairs={{0,8},{1,9},{2,10},{3,11},{4,12},{5,13},{6,14},{7,15},{8,0},{9,1},... | collective-permute-start | bytes 294920 | tf_op jit(solution)/shard_map/ppermute | solution.py:486
  28.6 2.1 %collective-permute-start.4 = (bf16[656,512]{1,0:T(8,128)(2,1)S(1)}, bf16[656,512]{1,0:T(8,128)(2,1)S(1)}, u32[]{:S(2)}, u32[]{:S(2)}) collective-permute-start(bf16[656,512]{1,0:T(8,128)(2,1)S(1)} %get-tuple-element.146), channel_id=1, source_target_pairs={{0,1},{1,0},{2,3},{3,2},{4,5},{5,4},{6,7},{7,6},{8,9},{9,8},{10,11... | collective-permute-start | bytes 2015240 | tf_op jit(solution)/shard_map/ppermute | solution.py:486
  30.9 7.3 %collective-permute-start.5 = (bf16[336,512]{1,0:T(8,128)(2,1)S(1)}, bf16[336,512]{1,0:T(8,128)(2,1)S(1)}, u32[]{:S(2)}, u32[]{:S(2)}) collective-permute-start(bf16[336,512]{1,0:T(8,128)(2,1)S(1)} %get-tuple-element.151), channel_id=1, source_target_pairs={{0,2},{1,5},{2,0},{3,7},{4,6},{5,1},{6,4},{7,3},{8,10},{9,13},{10,... | collective-permute-start | bytes 1032200 | tf_op jit(solution)/shard_map/ppermute | solution.py:486
  38.5 5.6 %collective-permute-start.6 = (bf16[176,512]{1,0:T(8,128)(2,1)S(1)}, bf16[176,512]{1,0:T(8,128)(2,1)S(1)}, u32[]{:S(2)}, u32[]{:S(2)}) collective-permute-start(bf16[176,512]{1,0:T(8,128)(2,1)S(1)} %maximum_maximum_fusion), channel_id=1, source_target_pairs={{0,4},{1,3},{2,6},{3,1},{4,0},{5,7},{6,2},{7,5},{8,12},{9,11},{10,... | collective-permute-start | bytes 540680 | tf_op jit(solution)/shard_map/ppermute | solution.py:486
  44.2 7.8 %collective-permute-start.8 = (bf16[176,256]{1,0:T(8,128)(2,1)S(1)}, bf16[176,256]{1,0:T(8,128)(2,1)S(1)}, u32[]{:S(2)}, u32[]{:S(2)}) collective-permute-start(bf16[176,256]{1,0:T(8,128)(2,1)S(1)} %get-tuple-element.192), channel_id=1, source_target_pairs={{0,8},{1,9},{2,10},{3,11},{4,12},{5,13},{6,14},{7,15},{8,0},{9,1},... | collective-permute-start | bytes 270344 | tf_op jit(solution)/shard_map/ppermute | solution.py:486
  46.9 7.1 %collective-permute-start.7 = (bf16[176,256]{1,0:T(8,128)(2,1)S(1)}, bf16[176,256]{1,0:T(8,128)(2,1)S(1)}, u32[]{:S(2)}, u32[]{:S(2)}) collective-permute-start(bf16[176,256]{1,0:T(8,128)(2,1)S(1)} %get-tuple-element.191), channel_id=1, source_target_pairs={{0,8},{1,9},{2,10},{3,11},{4,12},{5,13},{6,14},{7,15},{8,0},{9,1},... | collective-permute-start | bytes 270344 | tf_op jit(solution)/shard_map/ppermute | solution.py:486
  54.0 4.4 %collective-permute-start.10 = (bf16[160,256]{1,0:T(8,128)(2,1)S(1)}, bf16[160,256]{1,0:T(8,128)(2,1)S(1)}, u32[]{:S(2)}, u32[]{:S(2)}) collective-permute-start(bf16[160,256]{1,0:T(8,128)(2,1)S(1)} %add_convert_fusion.1), channel_id=1, source_target_pairs={{0,4},{1,3},{2,6},{3,1},{4,0},{5,7},{6,2},{7,5},{8,12},{9,11},{10,... | collective-permute-start | bytes 245768 | tf_op jit(solution)/shard_map/ppermute | solution.py:486
  54.0 5.3 %collective-permute-start.9 = (bf16[160,256]{1,0:T(8,128)(2,1)S(1)}, bf16[160,256]{1,0:T(8,128)(2,1)S(1)}, u32[]{:S(2)}, u32[]{:S(2)}) collective-permute-start(bf16[160,256]{1,0:T(8,128)(2,1)S(1)} %add_convert_fusion), channel_id=1, source_target_pairs={{0,4},{1,3},{2,6},{3,1},{4,0},{5,7},{6,2},{7,5},{8,12},{9,11},{10,... | collective-permute-start | bytes 245768 | tf_op jit(solution)/shard_map/ppermute | solution.py:486
  59.3 5.3 %collective-permute-start.12 = (bf16[320,256]{1,0:T(8,128)(2,1)S(1)}, bf16[320,256]{1,0:T(8,128)(2,1)S(1)}, u32[]{:S(2)}, u32[]{:S(2)}) collective-permute-start(bf16[320,256]{1,0:T(8,128)(2,1)S(1)} %maximum_select_fusion.2), channel_id=1, source_target_pairs={{0,2},{1,5},{2,0},{3,7},{4,6},{5,1},{6,4},{7,3},{8,10},{9,13},{10,... | collective-permute-start | bytes 491528 | tf_op jit(solution)/shard_map/ppermute | solution.py:486
  60.5 5.8 %collective-permute-start.11 = (bf16[320,256]{1,0:T(8,128)(2,1)S(1)}, bf16[320,256]{1,0:T(8,128)(2,1)S(1)}, u32[]{:S(2)}, u32[]{:S(2)}) collective-permute-start(bf16[320,256]{1,0:T(8,128)(2,1)S(1)} %maximum_select_fusion.3), channel_id=1, source_target_pairs={{0,2},{1,5},{2,0},{3,7},{4,6},{5,1},{6,4},{7,3},{8,10},{9,13},{10,... | collective-permute-start | bytes 491528 | tf_op jit(solution)/shard_map/ppermute | solution.py:486
  66.5 1.7 %collective-permute-start.13 = (bf16[656,256]{1,0:T(8,128)(2,1)S(1)}, bf16[656,256]{1,0:T(8,128)(2,1)S(1)}, u32[]{:S(2)}, u32[]{:S(2)}) collective-permute-start(bf16[656,256]{1,0:T(8,128)(2,1)S(1)} %get-tuple-element.190.refs_0_), channel_id=1, source_target_pairs={{0,1},{1,0},{2,3},{3,2},{4,5},{5,4},{6,7},{7,6},{8,9},{9,8},{10,11... | collective-permute-start | bytes 1007624 | tf_op jit(solution)/shard_map/ppermute | solution.py:486
  66.6 2.1 %collective-permute-start.14 = (bf16[656,256]{1,0:T(8,128)(2,1)S(1)}, bf16[656,256]{1,0:T(8,128)(2,1)S(1)}, u32[]{:S(2)}, u32[]{:S(2)}) collective-permute-start(bf16[656,256]{1,0:T(8,128)(2,1)S(1)} %get-tuple-element.189.refs_1_), channel_id=1, source_target_pairs={{0,1},{1,0},{2,3},{3,2},{4,5},{5,4},{6,7},{7,6},{8,9},{9,8},{10,11... | collective-permute-start | bytes 1007624 | tf_op jit(solution)/shard_map/ppermute | solution.py:486
